TPU v7x, 128 devices: a whole 4x4x4 slice. The times are simulated.
128 devices in a mesh: cells: 128 (over x, y, z, core).
Axes of the slice: x: 4, y: 4, z: 4, core: 2. Of those that a mesh axis runs over, the one named last changes fastest.
Arguments:
- position: float32 [3, 2097152], P(None, 'cells'), may hold values from -1 to 1
- velocity: float32 [3, 2097152], P(None, 'cells'), may hold values from -6 to 6
- particle_mass: float32 [2097152], P('cells'), may hold values from 0.5 to 2
- entropy: float32 [2097152], P('cells'), may hold values from 0.5 to 2
- density_old: float32 [2097152], P('cells'), may hold values from 0.25 to 2
- active: int32 [2097152], P('cells'), may hold values 0 or 1
- neighbours: int32 [8192, 6], P('cells'), may hold values from 0 to 8191, as said below
- destination: int32 [2097152], P('cells'), may hold values from 0 to 127, as said below
- recv_slot: int32 [2097152], P('cells'), may hold values from 0 to 24575, as said below
Outputs:
- moved_state: float32 [9, 3145728], P(None, 'cells')
Inputs may be any that keep to these rules, and one draw needn't show every extreme that they name: `neighbours`: row c begins with c itself; its other entries are distinct cells (c + o) mod 8192 with 0 < |o| <= 4; every even cell lists c + 4 and every odd cell c - 4. `destination`: A particle of device d goes to (d + o) mod 128 with |o| <= 4; some device sends exactly 1024 particles to another one, and none sends more. `recv_slot`: A particle that stays keeps its own row among its device's first 16384; one arriving from offset o (numbered g = 0 to 7 for o = -4 .. -1, 1 .. 4) takes a row 16384 + g * 1024 + r with r < 1024; no two particles of one destination share a row.
All inputs are finite; a program needn't handle non-finite values. No bound on the sum of `active` on one device may be relied on, other than what follows from the above.
Results may differ from a plain program's by a relative error of at most 0.00002.
Values sent between devices are 32-bit elements; how exact they have to be, the bound alone decides.
No kernel may reach another device: no remote copies, remote signals or barrier semaphores. Data moves between devices by JAX's collectives and lax.ppermute only.
A program may use at most 64 MiB of HBM per device.

v0:
```python
import jax
import jax.numpy as jnp
from jax import lax
from jax.sharding import PartitionSpec as P

CELL_PARTICLES = 256
HALO = 4
REACH = 4
PART_DEV = 16384
MOST = 1024


cell_block = 8
time_step = 0.25
gamma_rate = 5.0 / 3.0


def extended(block, sides, width):
    for axis, dim in sides:
        count = lax.axis_size(axis)
        forward = [(i, i + 1) for i in range(count - 1)]
        forward.append((count - 1, 0))
        backward = [(target, source) for source, target in forward]
        low = lax.ppermute(
            lax.slice_in_dim(block, block.shape[dim] - width, None, axis=dim), axis, forward
        )
        high = lax.ppermute(lax.slice_in_dim(block, 0, width, axis=dim), axis, backward)
        block = jnp.concatenate([low, block, high], axis=dim)
    return block


def passed_along(block, axis, distance):
    devices = range(lax.axis_size(axis))
    route = [((i - distance) % len(devices), i) for i in devices]
    return lax.ppermute(block, axis, route)


def squared_distance(target_particles, source_particles):
    separation = target_particles[0][:, None, :, None] - source_particles[0][:, :, None, :]
    squared = separation * separation
    for component in (1, 2):
        separation = (
            target_particles[component][:, None, :, None]
            - source_particles[component][:, :, None, :]
        )
        squared = squared + separation * separation
    return squared


def summed_density(target_particles, source_particles, kernel_scale):
    kernel_baseline = jnp.maximum(
        1.0 - 0.25 * squared_distance(target_particles, source_particles), 0.0
    )
    kernel_weight = kernel_scale * kernel_baseline * kernel_baseline * kernel_baseline
    return jnp.sum(kernel_weight * source_particles[3][:, :, None, :], axis=(1, 3))


def summed_force(target_particles, target_term_rows, source_particles, kernel_scale):
    kernel_baseline = jnp.maximum(
        1.0 - 0.25 * squared_distance(target_particles, source_particles), 0.0
    )
    kernel_weight = (
        1.5 * kernel_scale * kernel_baseline * kernel_baseline * source_particles[3][:, :, None, :]
    )
    kernel_weight = kernel_weight * (
        target_term_rows[:, None, :, None] + source_particles[4][:, :, None, :]
    )
    return jnp.stack(
        [
            jnp.sum(
                kernel_weight
                * (
                    target_particles[component][:, None, :, None]
                    - source_particles[component][:, :, None, :]
                ),
                axis=(1, 3),
            )
            for component in range(3)
        ]
    )


def cell_density_rows(target_particles, source_particle, cell_index_list, kernel_scale):
    cell_count = cell_index_list.shape[0]
    target_view = target_particles.reshape(3, cell_count, CELL_PARTICLES)
    cell_particle_view = source_particle.reshape(source_particle.shape[0], -1, CELL_PARTICLES)

    def one_block(block_start):
        block_index_list = lax.dynamic_slice_in_dim(cell_index_list, block_start, cell_block, 0)
        block_target_rows = lax.dynamic_slice_in_dim(target_view, block_start, cell_block, 1)
        return summed_density(
            block_target_rows, cell_particle_view[:, block_index_list], kernel_scale
        )

    starts = jnp.arange(cell_count // cell_block, dtype=jnp.int32) * cell_block
    return lax.map(one_block, starts).reshape(-1)


def cell_force_rows(
    target_particles, target_term_rows, source_particle, cell_index_list, kernel_scale
):
    cell_count = cell_index_list.shape[0]
    target_view = target_particles.reshape(3, cell_count, CELL_PARTICLES)
    term_view = target_term_rows.reshape(cell_count, CELL_PARTICLES)
    cell_particle_view = source_particle.reshape(source_particle.shape[0], -1, CELL_PARTICLES)

    def one_block(block_start):
        block_index_list = lax.dynamic_slice_in_dim(cell_index_list, block_start, cell_block, 0)
        block_target_rows = lax.dynamic_slice_in_dim(target_view, block_start, cell_block, 1)
        block_term_rows = lax.dynamic_slice_in_dim(term_view, block_start, cell_block, 0)
        return summed_force(
            block_target_rows,
            block_term_rows,
            cell_particle_view[:, block_index_list],
            kernel_scale,
        )

    starts = jnp.arange(cell_count // cell_block, dtype=jnp.int32) * cell_block
    blocks = lax.map(one_block, starts)
    return jnp.moveaxis(blocks, 1, 0).reshape(3, -1)


def pack_movers(payload, lane_key, lane_total):
    target_lane = jnp.where(lane_key < 0, lane_total, lane_key)
    return jnp.zeros((9, lane_total), jnp.float32).at[:, target_lane].set(payload, mode="drop")


def per_device(
    position,
    velocity,
    particle_mass,
    entropy,
    density_old,
    active,
    neighbours,
    destination,
    recv_slot,
):
    dev_count = lax.axis_size("cells")
    own_index = lax.axis_index("cells")
    cells_dev = neighbours.shape[0]
    all_cells = cells_dev * dev_count
    kernel_scale = 8.0 / (neighbours.shape[1] * CELL_PARTICLES)
    is_active = active == 1
    source_particle = jnp.concatenate([position, particle_mass[None]], axis=0)
    local_index_list = (neighbours - (own_index * cells_dev - HALO)) % all_cells
    padded_rows = extended(source_particle, (("cells", 1),), HALO * CELL_PARTICLES)
    summed_total = cell_density_rows(position, padded_rows, local_index_list, kernel_scale)
    density = jnp.where(is_active, summed_total, density_old)
    pressure_term = entropy * density ** (gamma_rate - 2.0)
    ghost_terms = extended(pressure_term, (("cells", 0),), HALO * CELL_PARTICLES)
    source_of_force = jnp.concatenate([padded_rows, ghost_terms[None]], axis=0)
    acceleration = cell_force_rows(
        position, pressure_term, source_of_force, local_index_list, kernel_scale
    )
    acceleration = jnp.where(is_active[None], acceleration, 0.0)
    new_velocity = velocity + time_step * acceleration
    new_position = position + time_step * new_velocity
    payload = jnp.concatenate(
        [new_position, new_velocity, density[None], entropy[None], particle_mass[None]], axis=0
    )
    staying = destination == own_index
    stay_part = jnp.where(staying[None], payload, 0.0)
    groups = 2 * REACH
    lane_total = groups * MOST
    step_away = (destination - own_index) % dev_count
    signed_step = jnp.where(step_away > dev_count // 2, step_away - dev_count, step_away)
    group_index = jnp.where(signed_step < 0, signed_step + REACH, signed_step + REACH - 1)
    lane_row = (recv_slot - PART_DEV) % MOST
    lane_key = jnp.where(staying, -1, group_index * MOST + lane_row)
    packed = pack_movers(payload, lane_key, lane_total)
    offsets = list(range(-REACH, 0)) + list(range(1, REACH + 1))
    arrived_blocks = []
    for group_number in range(groups):
        outgoing = packed[:, group_number * MOST : (group_number + 1) * MOST]
        arrived_blocks.append(passed_along(outgoing, "cells", offsets[group_number]))
    received = jnp.concatenate([stay_part] + arrived_blocks, axis=1)
    return received


def solution(mesh):
    placed = (
        P(None, "cells"),
        P(None, "cells"),
        P("cells"),
        P("cells"),
        P("cells"),
        P("cells"),
        P("cells", None),
        P("cells"),
        P("cells"),
    )
    return jax.shard_map(
        per_device, mesh=mesh, in_specs=placed, out_specs=P(None, "cells"), check_vma=False
    )
```

profile of v0, /device:TPU:1, one launch (start us, length us, event | category | flops | bytes accessed | tf_op | source)
XLA Modules:
  0.0 339.1 jit_solution(6764033145994616549)
XLA Ops:
  0.0 0.8 pad_maximum_fusion.4
  0.9 3.1 collective-permute-start
  4.0 0.8 copy.62
  4.8 1.0 compare_select_fusion.2
  5.7 1.0 copy.89
  7.1 1.1 pad_maximum_fusion.1
  8.2 83.8 %while.20 = (s32[]{:T(128)}, f32[8,8,256]{2,1,0:T(8,128)S(1)}, s32[8]{0:T(128)S(1)}, f32[3,64,256]{2,1,0:T(8,128)S(1)}, s32[64,6]{1,0:T(8,128)S(1)}, /*index=5*/...) while((s32[]{:T(128)}, f32[8,8,256]{2,1,0:T(8,128)S(1)}, ...), condition=%wide.region_2.3_spmd, body=%wide.region_0.2_spmd.sunk | while | flops 50330776 | bytes 1480007 | solution.py:96
  11.5 7.1 %fusion.29 = f32[8,256]{1,0:T(8,128)S(1)} fusion(f32[8,6,256]{2,1,0:T(8,128)S(1)} %get-tuple-element.238, f32[8,6,256]{2,1,0:T(8,128)S(1)} %get-tuple-element.239, f32[8,256]{1,0:T(8,128)S(1)} %get-tuple-element.240, f32[8,6,256]{2,1,0:T(8,128)S(1)} %get-tuple-element.243, f32[8,256]{1,0:T(8,128)S(1)} %get-tuple-element.244, ...), kind=kLoop, calls=%fused_computation.5.clone.1 | loop fusion | flops 50329600 | bytes 229376 | tf_op jit(solution)/shard_map/while/body/eval_jaxpr/reduce_sum | solution.py:55
  22.0 7.1 %fusion.29 = f32[8,256]{1,0:T(8,128)S(1)} fusion(f32[8,6,256]{2,1,0:T(8,128)S(1)} %get-tuple-element.238, f32[8,6,256]{2,1,0:T(8,128)S(1)} %get-tuple-element.239, f32[8,256]{1,0:T(8,128)S(1)} %get-tuple-element.240, f32[8,6,256]{2,1,0:T(8,128)S(1)} %get-tuple-element.243, f32[8,256]{1,0:T(8,128)S(1)} %get-tuple-element.244, ...), kind=kLoop, calls=%fused_computation.5.clone.1 | loop fusion | flops 50329600 | bytes 229376 | tf_op jit(solution)/shard_map/while/body/eval_jaxpr/reduce_sum | solution.py:55
  32.5 7.1 %fusion.29 = f32[8,256]{1,0:T(8,128)S(1)} fusion(f32[8,6,256]{2,1,0:T(8,128)S(1)} %get-tuple-element.238, f32[8,6,256]{2,1,0:T(8,128)S(1)} %get-tuple-element.239, f32[8,256]{1,0:T(8,128)S(1)} %get-tuple-element.240, f32[8,6,256]{2,1,0:T(8,128)S(1)} %get-tuple-element.243, f32[8,256]{1,0:T(8,128)S(1)} %get-tuple-element.244, ...), kind=kLoop, calls=%fused_computation.5.clone.1 | loop fusion | flops 50329600 | bytes 229376 | tf_op jit(solution)/shard_map/while/body/eval_jaxpr/reduce_sum | solution.py:55
  42.9 7.1 %fusion.29 = f32[8,256]{1,0:T(8,128)S(1)} fusion(f32[8,6,256]{2,1,0:T(8,128)S(1)} %get-tuple-element.238, f32[8,6,256]{2,1,0:T(8,128)S(1)} %get-tuple-element.239, f32[8,256]{1,0:T(8,128)S(1)} %get-tuple-element.240, f32[8,6,256]{2,1,0:T(8,128)S(1)} %get-tuple-element.243, f32[8,256]{1,0:T(8,128)S(1)} %get-tuple-element.244, ...), kind=kLoop, calls=%fused_computation.5.clone.1 | loop fusion | flops 50329600 | bytes 229376 | tf_op jit(solution)/shard_map/while/body/eval_jaxpr/reduce_sum | solution.py:55
  52.5 0.7 gather_fusion
  53.4 7.1 %fusion.29 = f32[8,256]{1,0:T(8,128)S(1)} fusion(f32[8,6,256]{2,1,0:T(8,128)S(1)} %get-tuple-element.238, f32[8,6,256]{2,1,0:T(8,128)S(1)} %get-tuple-element.239, f32[8,256]{1,0:T(8,128)S(1)} %get-tuple-element.240, f32[8,6,256]{2,1,0:T(8,128)S(1)} %get-tuple-element.243, f32[8,256]{1,0:T(8,128)S(1)} %get-tuple-element.244, ...), kind=kLoop, calls=%fused_computation.5.clone.1 | loop fusion | flops 50329600 | bytes 229376 | tf_op jit(solution)/shard_map/while/body/eval_jaxpr/reduce_sum | solution.py:55
  63.9 7.1 %fusion.29 = f32[8,256]{1,0:T(8,128)S(1)} fusion(f32[8,6,256]{2,1,0:T(8,128)S(1)} %get-tuple-element.238, f32[8,6,256]{2,1,0:T(8,128)S(1)} %get-tuple-element.239, f32[8,256]{1,0:T(8,128)S(1)} %get-tuple-element.240, f32[8,6,256]{2,1,0:T(8,128)S(1)} %get-tuple-element.243, f32[8,256]{1,0:T(8,128)S(1)} %get-tuple-element.244, ...), kind=kLoop, calls=%fused_computation.5.clone.1 | loop fusion | flops 50329600 | bytes 229376 | tf_op jit(solution)/shard_map/while/body/eval_jaxpr/reduce_sum | solution.py:55
  73.4 0.7 gather_fusion
  74.4 7.1 %fusion.29 = f32[8,256]{1,0:T(8,128)S(1)} fusion(f32[8,6,256]{2,1,0:T(8,128)S(1)} %get-tuple-element.238, f32[8,6,256]{2,1,0:T(8,128)S(1)} %get-tuple-element.239, f32[8,256]{1,0:T(8,128)S(1)} %get-tuple-element.240, f32[8,6,256]{2,1,0:T(8,128)S(1)} %get-tuple-element.243, f32[8,256]{1,0:T(8,128)S(1)} %get-tuple-element.244, ...), kind=kLoop, calls=%fused_computation.5.clone.1 | loop fusion | flops 50329600 | bytes 229376 | tf_op jit(solution)/shard_map/while/body/eval_jaxpr/reduce_sum | solution.py:55
  83.9 0.7 gather_fusion
  84.8 7.1 %fusion.29 = f32[8,256]{1,0:T(8,128)S(1)} fusion(f32[8,6,256]{2,1,0:T(8,128)S(1)} %get-tuple-element.238, f32[8,6,256]{2,1,0:T(8,128)S(1)} %get-tuple-element.239, f32[8,256]{1,0:T(8,128)S(1)} %get-tuple-element.240, f32[8,6,256]{2,1,0:T(8,128)S(1)} %get-tuple-element.243, f32[8,256]{1,0:T(8,128)S(1)} %get-tuple-element.244, ...), kind=kLoop, calls=%fused_computation.5.clone.1 | loop fusion | flops 50329600 | bytes 229376 | tf_op jit(solution)/shard_map/while/body/eval_jaxpr/reduce_sum | solution.py:55
  92.2 1.5 collective-permute-start.2
  93.7 5.0 %collective-permute-start.3 = (f32[1024]{0:T(1024)S(1)}, f32[1024]{0:T(1024)S(1)}, u32[]{:S(2)}, u32[]{:S(2)}) collective-permute-start(f32[1024]{0:T(1024)S(1)} %get-tuple-element.140), channel_id=1, source_target_pairs={{1,0},{2,1},{3,2},{4,3},{5,4},{6,5},{7,6},{8,7},{9,8},{10,9},{11,1... | collective-permute-start | bytes 12296 | tf_op jit(solution)/shard_map/ppermute | solution.py:27
  99.7 118.5 %while.21 = (s32[]{:T(128)}, f32[8,3,8,256]{3,2,1,0:T(8,128)S(1)}, s32[8]{0:T(128)S(1)}, f32[3,64,256]{2,1,0:T(8,128)S(1)}, s32[64,6]{1,0:T(8,128)S(1)}, /*index...) while((s32[]{:T(128)}, f32[8,3,8,256]{3,2,1,0:T(8,128)S(1)}, ...), condition=%wide.region_7.8_spmd, body=%wide.region_3.7_spmd.sunk | while | flops 69213336 | bytes 1897811 | solution.py:119
  102.8 11.6 %fusion.30 = (f32[8,256]{1,0:T(8,128)S(1)}, f32[8,256]{1,0:T(8,128)S(1)}, f32[8,256]{1,0:T(8,128)S(1)}) fusion(f32[8,6,256]{2,1,0:T(8,128)S(1)} %get-tuple-element.254, f32[8,256]{1,0:T(8,128)S(1)} %get-tuple-element.255, f32[8,6,256]{2,1,0:T(8,128)S(1)} %get-tuple-element.256, f32[8,256]{1,0:T(8,128)S(1)} %constant_dynamic-slice_fusion.2, ...), kind=kLoop, calls=%fused_computation.28.clone.1 | loop fusion | flops 69199872 | bytes 303104 | tf_op jit(solution)/shard_map/while/body/eval_jaxpr/reduce_sum | solution.py:70
  117.6 11.6 %fusion.30 = (f32[8,256]{1,0:T(8,128)S(1)}, f32[8,256]{1,0:T(8,128)S(1)}, f32[8,256]{1,0:T(8,128)S(1)}) fusion(f32[8,6,256]{2,1,0:T(8,128)S(1)} %get-tuple-element.254, f32[8,256]{1,0:T(8,128)S(1)} %get-tuple-element.255, f32[8,6,256]{2,1,0:T(8,128)S(1)} %get-tuple-element.256, f32[8,256]{1,0:T(8,128)S(1)} %constant_dynamic-slice_fusion.2, ...), kind=kLoop, calls=%fused_computation.28.clone.1 | loop fusion | flops 69199872 | bytes 303104 | tf_op jit(solution)/shard_map/while/body/eval_jaxpr/reduce_sum | solution.py:70
  132.5 11.6 %fusion.30 = (f32[8,256]{1,0:T(8,128)S(1)}, f32[8,256]{1,0:T(8,128)S(1)}, f32[8,256]{1,0:T(8,128)S(1)}) fusion(f32[8,6,256]{2,1,0:T(8,128)S(1)} %get-tuple-element.254, f32[8,256]{1,0:T(8,128)S(1)} %get-tuple-element.255, f32[8,6,256]{2,1,0:T(8,128)S(1)} %get-tuple-element.256, f32[8,256]{1,0:T(8,128)S(1)} %constant_dynamic-slice_fusion.2, ...), kind=kLoop, calls=%fused_computation.28.clone.1 | loop fusion | flops 69199872 | bytes 303104 | tf_op jit(solution)/shard_map/while/body/eval_jaxpr/reduce_sum | solution.py:70
  147.3 11.6 %fusion.30 = (f32[8,256]{1,0:T(8,128)S(1)}, f32[8,256]{1,0:T(8,128)S(1)}, f32[8,256]{1,0:T(8,128)S(1)}) fusion(f32[8,6,256]{2,1,0:T(8,128)S(1)} %get-tuple-element.254, f32[8,256]{1,0:T(8,128)S(1)} %get-tuple-element.255, f32[8,6,256]{2,1,0:T(8,128)S(1)} %get-tuple-element.256, f32[8,256]{1,0:T(8,128)S(1)} %constant_dynamic-slice_fusion.2, ...), kind=kLoop, calls=%fused_computation.28.clone.1 | loop fusion | flops 69199872 | bytes 303104 | tf_op jit(solution)/shard_map/while/body/eval_jaxpr/reduce_sum | solution.py:70
  162.1 11.6 %fusion.30 = (f32[8,256]{1,0:T(8,128)S(1)}, f32[8,256]{1,0:T(8,128)S(1)}, f32[8,256]{1,0:T(8,128)S(1)}) fusion(f32[8,6,256]{2,1,0:T(8,128)S(1)} %get-tuple-element.254, f32[8,256]{1,0:T(8,128)S(1)} %get-tuple-element.255, f32[8,6,256]{2,1,0:T(8,128)S(1)} %get-tuple-element.256, f32[8,256]{1,0:T(8,128)S(1)} %constant_dynamic-slice_fusion.2, ...), kind=kLoop, calls=%fused_computation.28.clone.1 | loop fusion | flops 69199872 | bytes 303104 | tf_op jit(solution)/shard_map/while/body/eval_jaxpr/reduce_sum | solution.py:70
  176.9 11.6 %fusion.30 = (f32[8,256]{1,0:T(8,128)S(1)}, f32[8,256]{1,0:T(8,128)S(1)}, f32[8,256]{1,0:T(8,128)S(1)}) fusion(f32[8,6,256]{2,1,0:T(8,128)S(1)} %get-tuple-element.254, f32[8,256]{1,0:T(8,128)S(1)} %get-tuple-element.255, f32[8,6,256]{2,1,0:T(8,128)S(1)} %get-tuple-element.256, f32[8,256]{1,0:T(8,128)S(1)} %constant_dynamic-slice_fusion.2, ...), kind=kLoop, calls=%fused_computation.28.clone.1 | loop fusion | flops 69199872 | bytes 303104 | tf_op jit(solution)/shard_map/while/body/eval_jaxpr/reduce_sum | solution.py:70
  191.7 11.6 %fusion.30 = (f32[8,256]{1,0:T(8,128)S(1)}, f32[8,256]{1,0:T(8,128)S(1)}, f32[8,256]{1,0:T(8,128)S(1)}) fusion(f32[8,6,256]{2,1,0:T(8,128)S(1)} %get-tuple-element.254, f32[8,256]{1,0:T(8,128)S(1)} %get-tuple-element.255, f32[8,6,256]{2,1,0:T(8,128)S(1)} %get-tuple-element.256, f32[8,256]{1,0:T(8,128)S(1)} %constant_dynamic-slice_fusion.2, ...), kind=kLoop, calls=%fused_computation.28.clone.1 | loop fusion | flops 69199872 | bytes 303104 | tf_op jit(solution)/shard_map/while/body/eval_jaxpr/reduce_sum | solution.py:70
  206.5 11.6 %fusion.30 = (f32[8,256]{1,0:T(8,128)S(1)}, f32[8,256]{1,0:T(8,128)S(1)}, f32[8,256]{1,0:T(8,128)S(1)}) fusion(f32[8,6,256]{2,1,0:T(8,128)S(1)} %get-tuple-element.254, f32[8,256]{1,0:T(8,128)S(1)} %get-tuple-element.255, f32[8,6,256]{2,1,0:T(8,128)S(1)} %get-tuple-element.256, f32[8,256]{1,0:T(8,128)S(1)} %constant_dynamic-slice_fusion.2, ...), kind=kLoop, calls=%fused_computation.28.clone.1 | loop fusion | flops 69199872 | bytes 303104 | tf_op jit(solution)/shard_map/while/body/eval_jaxpr/reduce_sum | solution.py:70
  219.2 4.7 %copy.64 = f32[16384,9]{1,0:T(8,128)} copy(f32[16384,9]{0,1:T(8,128)S(1)} %bitcast.105) | data formatting | bytes 1179648 | tf_op jit(solution)/shard_map/concatenate | solution.py:159
  223.8 42.8 %scatter_custom_fusion = f32[9,8192]{0,1:T(8,128)} fusion(s32[16384]{0:T(1024)S(1)} %compare_select_fusion.2, f32[16384,9]{1,0:T(8,128)} %copy.64, f32[]{:T(128)} %constant.80.clone.1), kind=kCustom, calls=%fused_computation.47 | custom fusion | bytes 295424 | tf_op jit(solution)/shard_map/scatter | solution.py:125
  266.7 3.8 %fusion.21 = (f32[9,1024]{0,1:T(8,128)S(1)}, f32[9,1024]{0,1:T(8,128)}, f32[9,1024]{0,1:T(8,128)}, f32[9,1024]{0,1:T(8,128)}, f32[9,1024]{0,1:T(8,128)}, /*index...) fusion(f32[9,8192]{0,1:T(8,128)} %scatter_custom_fusion), kind=kLoop, calls=%fused_computation.89 | loop fusion | bytes 589824 | tf_op jit(solution)/shard_map/slice | solution.py:175
  270.5 7.4 %collective-permute-start.4 = (f32[9,1024]{0,1:T(8,128)S(1)}, f32[9,1024]{0,1:T(8,128)}, u32[]{:S(2)}, u32[]{:S(2)}) collective-permute-start(f32[9,1024]{0,1:T(8,128)S(1)} %get-tuple-element.136), channel_id=1, source_target_pairs={{4,0},{5,1},{6,2},{7,3},{8,4},{9,5},{10,6},{11,7},{12,8},{13,9},{1... | collective-permute-start | bytes 110600 | tf_op jit(solution)/shard_map/ppermute | solution.py:35
  278.1 7.1 %collective-permute-start.6 = (f32[9,1024]{0,1:T(8,128)}, f32[9,1024]{0,1:T(8,128)}, u32[]{:S(2)}, u32[]{:S(2)}) collective-permute-start(f32[9,1024]{0,1:T(8,128)} %get-tuple-element.134), channel_id=1, source_target_pairs={{2,0},{3,1},{4,2},{5,3},{6,4},{7,5},{8,6},{9,7},{10,8},{11,9},{12,... | collective-permute-start | bytes 110600 | tf_op jit(solution)/shard_map/ppermute | solution.py:35
  285.1 1.7 collective-permute-start.8
  286.9 2.4 collective-permute-done.4
  289.3 7.6 %collective-permute-start.9 = (f32[9,1024]{0,1:T(8,128)}, f32[9,1024]{0,1:T(8,128)S(1)}, u32[]{:S(2)}, u32[]{:S(2)}) collective-permute-start(f32[9,1024]{0,1:T(8,128)} %get-tuple-element.131), channel_id=1, source_target_pairs={{126,0},{127,1},{0,2},{1,3},{2,4},{3,5},{4,6},{5,7},{6,8},{7,9},{8... | collective-permute-start | bytes 110600 | tf_op jit(solution)/shard_map/ppermute | solution.py:35
  296.9 1.2 copy.65
  298.1 2.5 collective-permute-done.5
  300.6 1.2 copy.66
  301.8 11.6 %collective-permute-done.6 = f32[9,1024]{0,1:T(8,128)} collective-permute-done((f32[9,1024]{0,1:T(8,128)}, f32[9,1024]{0,1:T(8,128)}, u32[]{:S(2)}, u32[]{:S(2)}) %collective-permute-start.6) | collective-permute-done | bytes 36896 | tf_op jit(solution)/shard_map/ppermute | solution.py:35
  313.5 1.2 copy.67
  314.7 1.2 copy.68
  316.2 6.1 %collective-permute-done.9 = f32[9,1024]{0,1:T(8,128)S(1)} collective-permute-done((f32[9,1024]{0,1:T(8,128)}, f32[9,1024]{0,1:T(8,128)S(1)}, u32[]{:S(2)}, u32[]{:S(2)}) %collective-permute-start.9) | collective-permute-done | bytes 36896 | tf_op jit(solution)/shard_map/ppermute | solution.py:35
  322.5 5.8 %collective-permute-done.10 = f32[9,1024]{0,1:T(8,128)} collective-permute-done((f32[9,1024]{0,1:T(8,128)}, f32[9,1024]{0,1:T(8,128)}, u32[]{:S(2)}, u32[]{:S(2)}) %collective-permute-start.10) | collective-permute-done | bytes 36896 | tf_op jit(solution)/shard_map/ppermute | solution.py:35
  328.3 1.2 copy.71
  329.6 7.6 %collective-permute-done.11 = f32[9,1024]{0,1:T(8,128)} collective-permute-done((f32[9,1024]{0,1:T(8,128)S(1)}, f32[9,1024]{0,1:T(8,128)}, u32[]{:S(2)}, u32[]{:S(2)}) %collective-permute-start.11) | collective-permute-done | bytes 36896 | tf_op jit(solution)/shard_map/ppermute | solution.py:35
  337.2 1.2 copy.72
  (210 shorter events, 25.8 us)
Async XLA Ops:
  0.0 98.7 %copy-start.4 = (s32[16384]{0:T(1024)S(1)}, s32[16384]{0:T(1024)}, u32[]{:S(2)}) copy-start(s32[16384]{0:T(1024)} %param.20) | copy-start | bytes 196612
  0.0 92.1 %copy-start.3 = (f32[16384]{0:T(1024)S(1)}, f32[16384]{0:T(1024)}, u32[]{:S(2)}) copy-start(f32[16384]{0:T(1024)} %param.16) | copy-start | bytes 196612
  0.0 92.1 %copy-start.6 = (f32[16384]{0:T(1024)S(1)}, f32[16384]{0:T(1024)}, u32[]{:S(2)}) copy-start(f32[16384]{0:T(1024)} %param.17) | copy-start | bytes 196612
  0.0 92.1 %copy-start.7 = (s32[16384]{0:T(1024)S(1)}, s32[16384]{0:T(1024)}, u32[]{:S(2)}) copy-start(s32[16384]{0:T(1024)} %param.18) | copy-start | bytes 196612
  0.9 5.9 %collective-permute-start = (f32[4,1024]{1,0:T(4,128)S(1)}, f32[4,1024]{1,0:T(4,128)S(1)}, u32[]{:S(2)}, u32[]{:S(2)}) collective-permute-start(f32[4,1024]{1,0:T(4,128)S(1)} %get-tuple-element.137), channel_id=1, source_target_pairs={{0,1},{1,2},{2,3},{3,4},{4,5},{5,6},{6,7},{7,8},{8,9},{9,10},{10,1... | collective-permute-start | bytes 49160 | tf_op jit(solution)/shard_map/ppermute | solution.py:24
  3.9 3.2 collective-permute-start.1
  92.0 126.3 %copy-start = (f32[3,16384]{1,0:T(4,128)S(1)}, f32[3,16384]{1,0:T(4,128)}, u32[]{:S(2)}) copy-start(f32[3,16384]{1,0:T(4,128)} %param.13) | copy-start | bytes 589828
  92.0 126.3 %copy-start.5 = (f32[3,16384]{1,0:T(4,128)S(1)}, f32[3,16384]{1,0:T(4,128)}, u32[]{:S(2)}) copy-start(f32[3,16384]{1,0:T(4,128)} %param.14) | copy-start | bytes 589828
  92.2 126.3 %copy-start.2 = (f32[16384]{0:T(1024)S(1)}, f32[16384]{0:T(1024)}, u32[]{:S(2)}) copy-start(f32[16384]{0:T(1024)} %param.15) | copy-start | bytes 196612
  92.2 7.1 %collective-permute-start.2 = (f32[1024]{0:T(1024)S(1)}, f32[1024]{0:T(1024)S(1)}, u32[]{:S(2)}, u32[]{:S(2)}) collective-permute-start(f32[1024]{0:T(1024)S(1)} %get-tuple-element.139), channel_id=1, source_target_pairs={{0,1},{1,2},{2,3},{3,4},{4,5},{5,6},{6,7},{7,8},{8,9},{9,10},{10,1... | collective-permute-start | bytes 12296 | tf_op jit(solution)/shard_map/ppermute | solution.py:24
  93.7 5.8 %collective-permute-start.3 = (f32[1024]{0:T(1024)S(1)}, f32[1024]{0:T(1024)S(1)}, u32[]{:S(2)}, u32[]{:S(2)}) collective-permute-start(f32[1024]{0:T(1024)S(1)} %get-tuple-element.140), channel_id=1, source_target_pairs={{1,0},{2,1},{3,2},{4,3},{5,4},{6,5},{7,6},{8,7},{9,8},{10,9},{11,1... | collective-permute-start | bytes 12296 | tf_op jit(solution)/shard_map/ppermute | solution.py:27
  270.5 18.8 %collective-permute-start.4 = (f32[9,1024]{0,1:T(8,128)S(1)}, f32[9,1024]{0,1:T(8,128)}, u32[]{:S(2)}, u32[]{:S(2)}) collective-permute-start(f32[9,1024]{0,1:T(8,128)S(1)} %get-tuple-element.136), channel_id=1, source_target_pairs={{4,0},{5,1},{6,2},{7,3},{8,4},{9,5},{10,6},{11,7},{12,8},{13,9},{1... | collective-permute-start | bytes 110600 | tf_op jit(solution)/shard_map/ppermute | solution.py:35
  278.0 22.6 %collective-permute-start.5 = (f32[9,1024]{0,1:T(8,128)}, f32[9,1024]{0,1:T(8,128)}, u32[]{:S(2)}, u32[]{:S(2)}) collective-permute-start(f32[9,1024]{0,1:T(8,128)} %get-tuple-element.135), channel_id=1, source_target_pairs={{3,0},{4,1},{5,2},{6,3},{7,4},{8,5},{9,6},{10,7},{11,8},{12,9},{13... | collective-permute-start | bytes 110600 | tf_op jit(solution)/shard_map/ppermute | solution.py:35
  278.1 35.4 %collective-permute-start.6 = (f32[9,1024]{0,1:T(8,128)}, f32[9,1024]{0,1:T(8,128)}, u32[]{:S(2)}, u32[]{:S(2)}) collective-permute-start(f32[9,1024]{0,1:T(8,128)} %get-tuple-element.134), channel_id=1, source_target_pairs={{2,0},{3,1},{4,2},{5,3},{6,4},{7,5},{8,6},{9,7},{10,8},{11,9},{12,... | collective-permute-start | bytes 110600 | tf_op jit(solution)/shard_map/ppermute | solution.py:35
  285.1 29.6 %collective-permute-start.7 = (f32[9,1024]{0,1:T(8,128)}, f32[9,1024]{0,1:T(8,128)}, u32[]{:S(2)}, u32[]{:S(2)}) collective-permute-start(f32[9,1024]{0,1:T(8,128)} %get-tuple-element.133), channel_id=1, source_target_pairs={{1,0},{2,1},{3,2},{4,3},{5,4},{6,5},{7,6},{8,7},{9,8},{10,9},{11,1... | collective-permute-start | bytes 110600 | tf_op jit(solution)/shard_map/ppermute | solution.py:35
  285.1 30.9 %collective-permute-start.8 = (f32[9,1024]{0,1:T(8,128)}, f32[9,1024]{0,1:T(8,128)S(1)}, u32[]{:S(2)}, u32[]{:S(2)}) collective-permute-start(f32[9,1024]{0,1:T(8,128)} %get-tuple-element.132), channel_id=1, source_target_pairs={{127,0},{0,1},{1,2},{2,3},{3,4},{4,5},{5,6},{6,7},{7,8},{8,9},{9,1... | collective-permute-start | bytes 110600 | tf_op jit(solution)/shard_map/ppermute | solution.py:35
  289.3 33.0 %collective-permute-start.9 = (f32[9,1024]{0,1:T(8,128)}, f32[9,1024]{0,1:T(8,128)S(1)}, u32[]{:S(2)}, u32[]{:S(2)}) collective-permute-start(f32[9,1024]{0,1:T(8,128)} %get-tuple-element.131), channel_id=1, source_target_pairs={{126,0},{127,1},{0,2},{1,3},{2,4},{3,5},{4,6},{5,7},{6,8},{7,9},{8... | collective-permute-start | bytes 110600 | tf_op jit(solution)/shard_map/ppermute | solution.py:35
  300.6 27.7 %collective-permute-start.10 = (f32[9,1024]{0,1:T(8,128)}, f32[9,1024]{0,1:T(8,128)}, u32[]{:S(2)}, u32[]{:S(2)}) collective-permute-start(f32[9,1024]{0,1:T(8,128)} %get-tuple-element.130), channel_id=1, source_target_pairs={{125,0},{126,1},{127,2},{0,3},{1,4},{2,5},{3,6},{4,7},{5,8},{6,9},... | collective-permute-start | bytes 110600 | tf_op jit(solution)/shard_map/ppermute | solution.py:35
  313.5 23.7 %collective-permute-start.11 = (f32[9,1024]{0,1:T(8,128)S(1)}, f32[9,1024]{0,1:T(8,128)}, u32[]{:S(2)}, u32[]{:S(2)}) collective-permute-start(f32[9,1024]{0,1:T(8,128)S(1)} %get-tuple-element.129), channel_id=1, source_target_pairs={{124,0},{125,1},{126,2},{127,3},{0,4},{1,5},{2,6},{3,7},{4,8},{5,9... | collective-permute-start | bytes 110600 | tf_op jit(solution)/shard_map/ppermute | solution.py:35
  329.6 8.9 %copy-start.1 = (f32[9,24576]{1,0:T(8,128)}, f32[9,24576]{1,0:T(8,128)S(1)}, u32[]{:S(2)}) copy-start(f32[9,24576]{1,0:T(8,128)S(1)} %constant_dynamic-update-slice_fusion.1) | copy-start | bytes 2654212
where the time goes:
time: 345 us; the launch traced here: 339 us
  other arithmetic  154 us (45%)
  local copies, waits for them, and re-layouts  86.1 us (25%)
  waiting for transfers between devices  37.3 us (11%)
  starting transfers between devices  33.4 us (10%)
  loops' own time  28.1 us (8%)
    reduce_sum x8, other arithmetic, summed_force(): jnp.sum(kernel_weight * (target_particles[component][:, None, :, None] -...  92.9 us
    reduce_sum x8, other arithmetic, summed_density(): jnp.sum(kernel_weight * source_particles[3][:, :, None, :], axis=(1, 3))  57.2 us
    scatter x1, local copies, waits for them, and re-layouts, pack_movers(): jnp.zeros((9, lane_total), jnp.float32).at[:, target_lane]  42.8 us
    ppermute x8, waiting for transfers between devices, passed_along(): return lax.ppermute(block, axis, route)  36.1 us
    ppermute x8, starting transfers between devices, passed_along(): return lax.ppermute(block, axis, route)  23.9 us
    another operation x1, loops' own time, cell_force_rows(): blocks = lax.map(one_block, starts)  14.1 us
    another operation x1, loops' own time, cell_density_rows(): return lax.map(one_block, starts).reshape(-1)  14.1 us
    gather x24, local copies, waits for them, and re-layouts, one_block(): cell_particle_view[:, block_index_list]  10.9 us
  transfers between devices with their start and end apart: 12, of which 9 were waited for; matrix products, arithmetic and copies ran while one was open for 3% of the time, Pallas kernels for 0%

commit v1 on v0

v1 whole, which is shorter than its diff:
```python
import functools

import jax
import jax.numpy as jnp
from jax import lax
from jax.experimental import pallas as pl
from jax.experimental.pallas import tpu as pltpu
from jax.sharding import PartitionSpec as P

CELL_PARTICLES = 256
HALO = 4
REACH = 4
PART_DEV = 16384
MOST = 1024
RECV_DEV = 24576
CELLS_DEV = 64
NEIGHBOURS = 6
LANES = 128
ROWS = PART_DEV // LANES
EDGE = 2 * HALO
EXT = CELLS_DEV + 2 * EDGE
EXT_ROWS = 2 * EXT
EDGE_ROWS = 2 * EDGE
HALO_ROWS = 96
GHOST = HALO
LISTED = CELLS_DEV + 2 * GHOST
UNROLL = 8
LIST_SIZE = LISTED * 32 + 4 * UNROLL + 64
GROUPS = 2 * REACH
time_step = 0.25
FIELDS = 9


def bcast(ref, row):
    return ref[pl.ds(row, 8, stride=0), :]


def state_kernel(
    own_ref,
    nbr_ref,
    pos_ref,
    vel_ref,
    mass_ref,
    ent_ref,
    rho_ref,
    act_ref,
    dest_ref,
    slot_ref,
    left_ref,
    right_ref,
    out_ref,
    send_ref,
    xs,
    ys,
    zs,
    ms,
    ps,
    rank,
    count_v,
    dens,
    ax,
    ay,
    az,
    fields,
    parts,
    hi_row,
    lo_row,
    a_block,
    b_block,
    packed,
    stay_rows,
    count_s,
    chunk_list,
    sem,
):
    own = own_ref[0]
    scale = 8.0 / (NEIGHBOURS * CELL_PARTICLES)

    for ref, base in ((xs, 0), (ys, 1), (zs, 2)):
        ref[0:EDGE_ROWS, :] = left_ref[base * 16 : base * 16 + 16, :] * 0.5
        ref[EDGE_ROWS + ROWS :, :] = right_ref[base * 16 : base * 16 + 16, :] * 0.5
    ms[0:EDGE_ROWS, :] = left_ref[48:64, :]
    ms[EDGE_ROWS : EDGE_ROWS + ROWS, :] = mass_ref[...]
    ms[EDGE_ROWS + ROWS :, :] = right_ref[48:64, :]

    def split_rows(i, carry):
        col = pl.multiple_of(i * LANES, LANES)
        p = pos_ref[:, pl.ds(col, LANES)]
        v = vel_ref[:, pl.ds(col, LANES)]
        for c, ref in enumerate((xs, ys, zs)):
            ref[pl.ds(EDGE_ROWS + i, 1), :] = p[c : c + 1, :] * 0.5
            fields[3 + c, pl.ds(i, 1), :] = v[c : c + 1, :]
        return carry

    lax.fori_loop(0, ROWS, split_rows, 0, unroll=4)

    zeros8 = jnp.zeros((8, LANES), jnp.float32)
    act = jnp.concatenate(
        [
            zeros8,
            left_ref[80:88, :],
            (act_ref[...] == 1).astype(jnp.float32),
            right_ref[80:88, :],
            zeros8,
        ],
        axis=0,
    )
    before = (
        lax.broadcasted_iota(jnp.int32, (LANES, LANES), 0)
        < lax.broadcasted_iota(jnp.int32, (LANES, LANES), 1)
    ).astype(jnp.bfloat16)
    act16 = act.astype(jnp.bfloat16)
    inside = jnp.dot(act16, before, preferred_element_type=jnp.float32)
    total = jnp.dot(
        act16, jnp.ones((LANES, LANES), jnp.bfloat16), preferred_element_type=jnp.float32
    )
    shifted = pltpu.roll(total, 1, 0)
    row_id = lax.broadcasted_iota(jnp.int32, (EXT_ROWS, LANES), 0)
    rank[...] = jnp.where(
        act > 0.5, inside + jnp.where(row_id % 2 == 1, shifted, 0.0), -1.0
    )
    count_v[...] = (total + shifted).astype(jnp.int32)
    count_copy = pltpu.make_async_copy(count_v, count_s, sem.at[0])
    count_copy.start()
    dens[...] = jnp.zeros_like(dens)
    for ref in (ax, ay, az):
        ref[...] = jnp.zeros_like(ref)
    count_copy.wait()

    def list_cell(cell, at):
        n = count_s[2 * cell + 1, 0]
        chunks = (n + 7) >> 3
        chunk_list[at] = cell * 64
        chunk_list[at + 1] = cell * 64 + 1

        def more(k, carry):
            chunk_list[at + k] = cell * 64 + k
            return carry

        lax.fori_loop(2, chunks, more, 0)
        return at + chunks

    def pad(at):
        for k in range(UNROLL):
            chunk_list[at + k] = EDGE * 64 + 32

    own_total = lax.fori_loop(EDGE, EDGE + CELLS_DEV, list_cell, 0)
    all_total = lax.fori_loop(EDGE - GHOST, EDGE, list_cell, own_total)
    all_total = lax.fori_loop(
        EDGE + CELLS_DEV, EDGE + CELLS_DEV + GHOST, list_cell, all_total
    )
    pad(all_total)

    sub = lax.broadcasted_iota(jnp.int32, (8, LANES), 0).astype(jnp.float32)

    def chunk_of(position):
        code = chunk_list[position]
        cell = code >> 6
        want = sub + ((code & 63) * 8).astype(jnp.float32)
        picks = [bcast(rank, 2 * cell + h) == want for h in range(2)]
        return cell, picks

    def column(ref, cell, picks):
        both = jnp.where(picks[0], bcast(ref, 2 * cell), 0.0) + jnp.where(
            picks[1], bcast(ref, 2 * cell + 1), 0.0
        )
        return jnp.sum(both, axis=1, keepdims=True)

    def spread(ref, cell, picks, value):
        for h in range(2):
            row = jnp.sum(jnp.where(picks[h], value, 0.0), axis=0, keepdims=True)
            ref[pl.ds(2 * cell + h, 1), :] += row

    def density_step(step, carry):
        done = []
        for u in range(UNROLL):
            cell, picks = chunk_of(step * UNROLL + u)
            cx, cy, cz = (column(ref, cell, picks) for ref in (xs, ys, zs))
            total_rows = jnp.zeros((8, LANES), jnp.float32)
            for q in range(NEIGHBOURS):
                source = nbr_ref[(cell - (EDGE - GHOST)) * NEIGHBOURS + q]
                for h in range(2):
                    row = 2 * source + h
                    dx = cx - bcast(xs, row)
                    dy = cy - bcast(ys, row)
                    dz = cz - bcast(zs, row)
                    u1 = jnp.maximum(1.0 - (dx * dx + dy * dy + dz * dz), 0.0)
                    total_rows += u1 * u1 * u1 * bcast(ms, row)
            value = jnp.sum(total_rows, axis=1, keepdims=True) * scale
            done.append((cell, picks, value))
        for cell, picks, value in done:
            spread(dens, cell, picks, value)
        return carry

    lax.fori_loop(0, (all_total + UNROLL - 1) // UNROLL, density_step, 0)

    ones8 = jnp.ones((8, LANES), jnp.float32)
    rho_old = jnp.concatenate(
        [ones8, left_ref[72:80, :], rho_ref[...], right_ref[72:80, :], ones8], axis=0
    )
    entropy = jnp.concatenate(
        [zeros8, left_ref[64:72, :], ent_ref[...], right_ref[64:72, :], zeros8], axis=0
    )
    rho = jnp.where(rank[...] >= 0.0, dens[...], rho_old)
    dens[...] = rho
    ps[...] = entropy * jnp.exp(jnp.log(rho) * (-1.0 / 3.0))

    def force_step(step, carry):
        done = []
        for u in range(UNROLL):
            cell, picks = chunk_of(step * UNROLL + u)
            cx, cy, cz, cp = (column(ref, cell, picks) for ref in (xs, ys, zs, ps))
            sx = jnp.zeros((8, LANES), jnp.float32)
            sy = jnp.zeros((8, LANES), jnp.float32)
            sz = jnp.zeros((8, LANES), jnp.float32)
            for q in range(NEIGHBOURS):
                source = nbr_ref[(cell - (EDGE - GHOST)) * NEIGHBOURS + q]
                for h in range(2):
                    row = 2 * source + h
                    dx = cx - bcast(xs, row)
                    dy = cy - bcast(ys, row)
                    dz = cz - bcast(zs, row)
                    u1 = jnp.maximum(1.0 - (dx * dx + dy * dy + dz * dz), 0.0)
                    w = u1 * u1 * (bcast(ms, row) * (cp + bcast(ps, row)))
                    sx += w * dx
                    sy += w * dy
                    sz += w * dz
            values = [
                jnp.sum(s, axis=1, keepdims=True) * (3.0 * scale) for s in (sx, sy, sz)
            ]
            done.append((cell, picks, values))
        for cell, picks, values in done:
            for ref, value in zip((ax, ay, az), values):
                spread(ref, cell, picks, value)
        return carry

    lax.fori_loop(0, (own_total + UNROLL - 1) // UNROLL, force_step, 0)

    own_rows = slice(EDGE_ROWS, EDGE_ROWS + ROWS)
    for c, (ref, acc) in enumerate(((xs, ax), (ys, ay), (zs, az))):
        kicked = fields[3 + c] + time_step * acc[own_rows, :]
        fields[3 + c] = kicked
        fields[c] = ref[own_rows, :] * 2.0 + time_step * kicked
    fields[6] = dens[own_rows, :]
    fields[7] = ent_ref[...]
    fields[8] = mass_ref[...]

    dest = dest_ref[...]
    staying = dest == own
    away = (dest - own) & 127
    signed = jnp.where(away > 64, away - 128, away)
    group = jnp.where(signed < 0, signed + REACH, signed + REACH - 1)
    place = (slot_ref[...] - PART_DEV) & (MOST - 1)
    hi = (group >> 1) * 8 + (place >> 7)
    lo = (group & 1) * LANES + (place & (LANES - 1))
    hi_row[...] = jnp.where(staying, -1, hi).astype(jnp.float32)
    lo_row[...] = jnp.where(staying, -1, lo).astype(jnp.float32)
    keep = staying
    for v in range(FIELDS):
        whole = fields[v]
        head = whole.astype(jnp.bfloat16).astype(jnp.float32)
        parts[v] = head
        parts[FIELDS + v] = whole - head
        fields[v] = jnp.where(keep, whole, 0.0)

    def stay_step(i, carry):
        col = pl.multiple_of(i * LANES, LANES)
        for v in range(FIELDS):
            stay_rows[v : v + 1, pl.ds(col, LANES)] = fields[v, pl.ds(i, 1), :]
        return carry

    lax.fori_loop(0, ROWS, stay_step, 0, unroll=4)
    stay_copy = pltpu.make_async_copy(
        stay_rows, out_ref.at[:, pl.ds(0, PART_DEV)], sem.at[1]
    )
    stay_copy.start()

    packed[...] = jnp.zeros_like(packed)
    hi_iota = lax.broadcasted_iota(jnp.int32, (32, LANES), 0).astype(jnp.float32)
    lo_iota = lax.broadcasted_iota(jnp.int32, (256, LANES), 0).astype(jnp.float32)
    per = 4

    def pack_step(step, carry):
        for j in range(per):
            row = step * per + j
            cols = slice(j * LANES, (j + 1) * LANES)
            hi_b = jnp.concatenate([bcast(hi_row, row)] * 4, axis=0)
            pick = (hi_b == hi_iota).astype(jnp.bfloat16)
            lo_b = jnp.concatenate([bcast(lo_row, row)] * 32, axis=0)
            b_block[:, cols] = (lo_b == lo_iota).astype(jnp.bfloat16)
            for v in range(2 * FIELDS):
                value = parts[v, pl.ds(row, 8, stride=0), :]
                value = jnp.concatenate([value] * 4, axis=0).astype(jnp.bfloat16)
                a_block[32 * v : 32 * v + 32, cols] = pick * value
        packed[...] += lax.dot_general(
            a_block[...],
            b_block[...],
            (((1,), (1,)), ((), ())),
            preferred_element_type=jnp.float32,
        )
        return carry

    lax.fori_loop(0, ROWS // per, pack_step, 0)
    for g in range(GROUPS):
        cols = slice((g & 1) * LANES, (g & 1) * LANES + LANES)
        for v in range(FIELDS):
            r = 32 * v + (g >> 1) * 8
            send_ref[g, v] = (
                packed[r : r + 8, cols] + packed[32 * FIELDS + r : 32 * FIELDS + r + 8, cols]
            )
    stay_copy.wait()


def assemble_kernel(*refs):
    arrived = refs[:GROUPS]
    out_ref, rows, sem = refs[GROUPS + 1 :]
    for g in range(GROUPS):
        for r in range(8):
            col = g * MOST + r * LANES
            for v in range(FIELDS):
                rows[v : v + 1, col : col + LANES] = arrived[g][v, r : r + 1, :]
    copy = pltpu.make_async_copy(
        rows, out_ref.at[:, pl.ds(PART_DEV, GROUPS * MOST)], sem.at[0]
    )
    copy.start()
    copy.wait()


def swapped(block, pairs):
    route = [(a, b) for a, b in pairs] + [(b, a) for a, b in pairs]
    return lax.ppermute(block, "cells", route)


def edge_rows(position, mass, entropy, rho, act, nbr, start, ghost_start):
    wide = slice(start, start + EDGE * CELL_PARTICLES)
    near = slice(ghost_start * CELL_PARTICLES, (ghost_start + GHOST) * CELL_PARTICLES)
    listed = nbr[ghost_start : ghost_start + GHOST].astype(jnp.float32).reshape(-1)
    tail = jnp.pad(listed, (0, 8 * LANES - listed.shape[0]))
    return jnp.concatenate(
        [
            position[:, wide].reshape(-1),
            mass[wide],
            entropy[near],
            rho[near],
            act[near],
            tail,
        ]
    ).reshape(HALO_ROWS, LANES)


def per_device(
    position,
    velocity,
    particle_mass,
    entropy,
    density_old,
    active,
    neighbours,
    destination,
    recv_slot,
):
    count = lax.axis_size("cells")
    own = lax.axis_index("cells")
    all_cells = CELLS_DEV * count
    act_f = (active == 1).astype(jnp.float32)
    low_edge = edge_rows(
        position, particle_mass, entropy, density_old, act_f, neighbours, 0, 0
    )
    high_edge = edge_rows(
        position,
        particle_mass,
        entropy,
        density_old,
        act_f,
        neighbours,
        PART_DEV - EDGE * CELL_PARTICLES,
        CELLS_DEV - GHOST,
    )
    even = own % 2 == 0
    near_pairs = [(2 * k, 2 * k + 1) for k in range(count // 2)]
    far_pairs = [(2 * k + 1, (2 * k + 2) % count) for k in range(count // 2)]
    far = swapped(jnp.where(even, low_edge, high_edge), far_pairs)
    near = swapped(jnp.where(even, high_edge, low_edge), near_pairs)
    left = jnp.where(even, far, near)
    right = jnp.where(even, near, far)
    listed = GHOST * NEIGHBOURS
    lists = jnp.concatenate(
        [
            left[88, :listed].astype(jnp.int32),
            neighbours.reshape(-1),
            right[88, :listed].astype(jnp.int32),
        ]
    )
    lists = (lists - (own * CELLS_DEV - EDGE)) % all_cells

    vm = pl.BlockSpec(memory_space=pltpu.VMEM)
    sm = pl.BlockSpec(memory_space=pltpu.SMEM)
    hbm = pl.BlockSpec(memory_space=pl.ANY)
    square = (ROWS, LANES)
    ext = pltpu.VMEM((EXT_ROWS, LANES), jnp.float32)
    out, send = pl.pallas_call(
        state_kernel,
        out_shape=(
            jax.ShapeDtypeStruct((FIELDS, RECV_DEV), jnp.float32),
            jax.ShapeDtypeStruct((GROUPS, FIELDS, 8, LANES), jnp.float32),
        ),
        in_specs=[sm, sm] + [vm] * 10,
        out_specs=(hbm, vm),
        scratch_shapes=[
            ext,
            ext,
            ext,
            ext,
            ext,
            ext,
            pltpu.VMEM((EXT_ROWS, LANES), jnp.int32),
            ext,
            ext,
            ext,
            ext,
            pltpu.VMEM((FIELDS, ROWS, LANES), jnp.float32),
            pltpu.VMEM((2 * FIELDS, ROWS, LANES), jnp.float32),
            pltpu.VMEM(square, jnp.float32),
            pltpu.VMEM(square, jnp.float32),
            pltpu.VMEM((64 * FIELDS, 4 * LANES), jnp.bfloat16),
            pltpu.VMEM((256, 4 * LANES), jnp.bfloat16),
            pltpu.VMEM((64 * FIELDS, 256), jnp.float32),
            pltpu.VMEM((FIELDS, PART_DEV), jnp.float32),
            pltpu.SMEM((EXT_ROWS, LANES), jnp.int32),
            pltpu.SMEM((LIST_SIZE,), jnp.int32),
            pltpu.SemaphoreType.DMA((2,)),
        ],
        compiler_params=pltpu.CompilerParams(vmem_limit_bytes=40 * 2**20),
    )(
        own.reshape(1),
        lists,
        position,
        velocity,
        particle_mass.reshape(square),
        entropy.reshape(square),
        density_old.reshape(square),
        active.reshape(square),
        destination.reshape(square),
        recv_slot.reshape(square),
        left,
        right,
    )
    offsets = list(range(-REACH, 0)) + list(range(1, REACH + 1))
    arrived = []
    for g, offset in enumerate(offsets):
        route = [((i - offset) % count, i) for i in range(count)]
        arrived.append(lax.ppermute(send[g], "cells", route))
    return pl.pallas_call(
        assemble_kernel,
        out_shape=jax.ShapeDtypeStruct((FIELDS, RECV_DEV), jnp.float32),
        in_specs=[vm] * GROUPS + [hbm],
        out_specs=hbm,
        scratch_shapes=[
            pltpu.VMEM((FIELDS, GROUPS * MOST), jnp.float32),
            pltpu.SemaphoreType.DMA((1,)),
        ],
        input_output_aliases={GROUPS: 0},
        compiler_params=pltpu.CompilerParams(vmem_limit_bytes=16 * 2**20),
    )(*arrived, out)


def solution(mesh):
    placed = (
        P(None, "cells"),
        P(None, "cells"),
        P("cells"),
        P("cells"),
        P("cells"),
        P("cells"),
        P("cells", None),
        P("cells"),
        P("cells"),
    )
    return jax.shard_map(
        per_device, mesh=mesh, in_specs=placed, out_specs=P(None, "cells"), check_vma=False
    )
```

time: 345 us -> 68.9 us (0.20); the launches traced: 339 us -> 68.4 us
  other arithmetic: 154 us -> 1.8 us
  local copies, waits for them, and re-layouts: 86.1 us -> 11.2 us
  waiting for transfers between devices: 37.3 us -> 8.78 us
  Pallas kernels: 0 us -> 28.1 us
  loops' own time: 28.1 us -> 0 us
  starting transfers between devices: 33.4 us -> 18.4 us
    reduce_sum x16 -> x0, other arithmetic: 150 us -> none  [the longest x8 92.9 us: summed_force(): jnp.sum(kernel_weight * (target_particles[component][:, None, :, None] -...]
    scatter x1 -> x0, local copies, waits for them, and re-layouts: 42.8 us -> none  [pack_movers(): jnp.zeros((9, lane_total), jnp.float32).at[:, target_lane]]
    ppermute x12 -> x10, waiting for transfers between devices: 37.3 us -> 8.78 us  [the longest x8 8.77 us: per_device(): arrived.append(lax.ppermute(send[g], 'cells', route))]
    another operation x2 -> x0, loops' own time: 28.1 us -> none  [the longest x1 14.1 us: cell_force_rows(): blocks = lax.map(one_block, starts)]
    pallas_call x0 -> x2, Pallas kernels: none -> 28.1 us  [the longest x1 27.1 us: per_device(): pl.pallas_call(state_kernel, out_shape=(jax.ShapeDtypeStruct((FIELDS, REC...]
    ppermute x12 -> x10, starting transfers between devices: 33.4 us -> 18.4 us  [the longest x2 9.71 us: swapped(): return lax.ppermute(block, 'cells', route)]
    gather x24 -> x0, local copies, waits for them, and re-layouts: 10.9 us -> none  [one_block(): cell_particle_view[:, block_index_list]]
    dynamic_slice x24 -> x0, local copies, waits for them, and re-layouts: 9.48 us -> none  [the longest x16 9.38 us: cell_density_rows(): return lax.map(one_block, starts).reshape(-1)]
  transfers between devices with their start and end apart: 12 -> 10, of which waited for: 9 -> 3; matrix products, arithmetic and copies ran while one was open for 3% -> 1% of each run, Pallas kernels for 0% -> 0%
where the time goes in v1:
time: 68.9 us; the launch traced here: 68.4 us
  Pallas kernels  28.1 us (41%)
  starting transfers between devices  18.4 us (27%)
  local copies, waits for them, and re-layouts  11.2 us (16%)
  waiting for transfers between devices  8.78 us (13%)
  other arithmetic  1.8 us (3%)
    pallas_call x1, Pallas kernels, per_device(): pl.pallas_call(state_kernel, out_shape=(jax.ShapeDtypeStruct((FIELDS, REC...  27.1 us
    unnamed x22, local copies, waits for them, and re-layouts  9.85 us
    ppermute x2, starting transfers between devices, swapped(): return lax.ppermute(block, 'cells', route)  9.71 us
    ppermute x8, waiting for transfers between devices, per_device(): arrived.append(lax.ppermute(send[g], 'cells', route))  8.77 us
    ppermute x8, starting transfers between devices, per_device(): arrived.append(lax.ppermute(send[g], 'cells', route))  8.66 us
  transfers between devices with their start and end apart: 10, of which 3 were waited for; matrix products, arithmetic and copies ran while one was open for 1% of the time, Pallas kernels for 0%

profile of v1, /device:TPU:1, one launch (start us, length us, event | category | flops | bytes accessed | tf_op | source)
XLA Modules:
  0.0 68.4 jit_solution(15877002744626718373)
XLA Ops:
  0.0 0.8 %slice_convert_fusion.1 = (f32[4,6]{0,1:T(8,128)S(1)}, f32[4,6]{0,1:T(8,128)S(1)}) fusion(s32[64,6]{0,1:T(8,128)} %param.15), kind=kLoop, calls=%fused_computation.26 | loop fusion | flops 48 | bytes 384 | tf_op jit(solution)/shard_map/convert_element_type | solution.py:337
  0.8 0.1 copy.13
  0.9 0.1 reshape.46
  1.0 0.1 copy.14
  1.1 0.1 reshape.48
  1.2 0.8 %compare_convert_fusion = f32[16384]{0:T(1024)S(1)} fusion(s32[16384]{0:T(1024)} %param.14), kind=kLoop, calls=%fused_computation | loop fusion | flops 32768 | bytes 131072 | tf_op jit(solution)/shard_map/convert_element_type | solution.py:365
  2.0 0.8 %fusion.3 = (f32[3,2048]{1,0:T(4,128)S(1)}, f32[3,2048]{1,0:T(4,128)S(1)}) fusion(f32[3,16384]{1,0:T(4,128)} %pos_ref.1), kind=kLoop, calls=%fused_computation.36 | loop fusion | bytes 98304 | tf_op jit(solution)/shard_map/slice | solution.py:341
  2.9 0.7 %slice_dynamic-update-slice_fusion.1 = (f32[12288]{0:T(1024)S(1)}, f32[12288]{0:T(1024)S(1)}) fusion(f32[12288]{0:T(1024)S(1)} %get-tuple-element.33, f32[16384]{0:T(1024)} %param.11, f32[12288]{0:T(1024)S(1)} %get-tuple-element.34), kind=kLoop, calls=%fused_computation.14 | loop fusion | bytes 32768
  3.6 0.7 %constant_dynamic-update-slice_fusion.6 = (f32[12288]{0:T(1024)S(1)}, f32[12288]{0:T(1024)S(1)}) fusion(f32[12288]{0:T(1024)S(1)} %get-tuple-element.29, f32[16384]{0:T(1024)} %param.12, f32[12288]{0:T(1024)S(1)} %get-tuple-element.30), kind=kLoop, calls=%fused_computation.21 | loop fusion | bytes 16384
  4.3 0.7 %constant_dynamic-update-slice_fusion.4 = (f32[12288]{0:T(1024)S(1)}, f32[12288]{0:T(1024)S(1)}) fusion(f32[12288]{0:T(1024)S(1)} %get-tuple-element.27, f32[16384]{0:T(1024)} %param.13, f32[12288]{0:T(1024)S(1)} %get-tuple-element.28), kind=kLoop, calls=%fused_computation.19 | loop fusion | bytes 16384
  5.1 3.1 %collective-permute-start = (f32[96,128]{1,0:T(8,128)S(1)}, f32[96,128]{1,0:T(8,128)S(1)}, u32[]{:S(2)}, u32[]{:S(2)}) collective-permute-start(f32[96,128]{1,0:T(8,128)S(1)} %get-tuple-element.21), channel_id=1, source_target_pairs={{1,2},{3,4},{5,6},{7,8},{9,10},{11,12},{13,14},{15,16},{17,18},{19... | collective-permute-start | bytes 147464 | tf_op jit(solution)/shard_map/ppermute | solution.py:331
  8.2 6.6 %collective-permute-start.1 = (f32[96,128]{1,0:T(8,128)S(1)}, f32[96,128]{1,0:T(8,128)S(1)}, u32[]{:S(2)}, u32[]{:S(2)}) collective-permute-start(f32[96,128]{1,0:T(8,128)S(1)} %get-tuple-element.22), channel_id=1, source_target_pairs={{0,1},{2,3},{4,5},{6,7},{8,9},{10,11},{12,13},{14,15},{16,17},{18,... | collective-permute-start | bytes 147464 | tf_op jit(solution)/shard_map/ppermute | solution.py:331
  14.8 0.8 %copy.15 = s32[64,6]{1,0:T(8,128)S(1)} copy(s32[64,6]{0,1:T(8,128)} %param.15) | data formatting | bytes 3072 | tf_op args[6]
  15.5 0.1 reshape.49
  15.7 0.0 collective-permute-done
  15.7 0.0 collective-permute-done.1
  15.8 0.1 add_select_fusion.nbr_ref
  15.8 0.0 copy-start
  15.8 0.9 %copy-done = f32[3,16384]{1,0:T(4,128)S(1)} copy-done((f32[3,16384]{1,0:T(4,128)S(1)}, f32[3,16384]{1,0:T(4,128)}, u32[]{:S(2)}) %copy-start) | copy-done | bytes 196632
  16.8 0.0 copy-start.1
  16.8 0.9 %copy-done.1 = f32[3,16384]{1,0:T(4,128)S(1)} copy-done((f32[3,16384]{1,0:T(4,128)S(1)}, f32[3,16384]{1,0:T(4,128)}, u32[]{:S(2)}) %copy-start.1) | copy-done | bytes 196632
  17.7 0.0 copy-start.2
  17.7 0.8 %copy-done.2 = s32[16384]{0:T(1024)S(1)} copy-done((s32[16384]{0:T(1024)S(1)}, s32[16384]{0:T(1024)}, u32[]{:S(2)}) %copy-start.2) | copy-done | bytes 65560
  18.6 0.0 copy-start.3
  18.6 0.8 %copy-done.3 = f32[16384]{0:T(1024)S(1)} copy-done((f32[16384]{0:T(1024)S(1)}, f32[16384]{0:T(1024)}, u32[]{:S(2)}) %copy-start.3) | copy-done | bytes 65560
  19.4 0.0 copy-start.4
  19.4 0.8 %copy-done.4 = f32[16384]{0:T(1024)S(1)} copy-done((f32[16384]{0:T(1024)S(1)}, f32[16384]{0:T(1024)}, u32[]{:S(2)}) %copy-start.4) | copy-done | bytes 65560
  20.3 0.8 %copy-done.5 = f32[16384]{0:T(1024)S(1)} copy-done((f32[16384]{0:T(1024)S(1)}, f32[16384]{0:T(1024)}, u32[]{:S(2)}) %copy-start.5) | copy-done | bytes 65560
  21.1 0.8 %copy-done.6 = s32[16384]{0:T(1024)S(1)} copy-done((s32[16384]{0:T(1024)S(1)}, s32[16384]{0:T(1024)}, u32[]{:S(2)}) %copy-start.6) | copy-done | bytes 65560
  21.9 0.8 %copy-done.7 = s32[16384]{0:T(1024)S(1)} copy-done((s32[16384]{0:T(1024)S(1)}, s32[16384]{0:T(1024)}, u32[]{:S(2)}) %copy-start.7) | copy-done | bytes 65560
  22.8 27.1 %shard_map.91 = (f32[9,24576]{1,0:T(8,128)}, f32[8,9,8,128]{3,2,1,0:T(8,128)S(1)}) custom-call(s32[1]{0:T(128)} %bitcast.own_ref, s32[432]{0:T(512)S(1)} %add_select_fusion.nbr_ref, f32[3,16384]{1,0:T(4,128)S(1)} %copy-done, f32[3,16384]{1,0:T(4,128)S(1)} %copy-done.1, f32[128,128]{1,0:T(8,128)S(1)} %bitcast.32, f32[128,128]{1,0:T(8,128)S(1)} %bitcast.33, ...), custom_call_target="tpu_custom_call" | custom-call | tf_op jit(solution)/shard_map/pallas_call | solution.py:401
  49.9 0.1 collective-permute-start.9
  50.0 1.0 %collective-permute-start.8 = (f32[9,8,128]{2,1,0:T(8,128)S(1)}, f32[9,8,128]{2,1,0:T(8,128)S(1)}, u32[]{:S(2)}, u32[]{:S(2)}) collective-permute-start(f32[9,8,128]{2,1,0:T(8,128)S(1)} %get-tuple-element.10), channel_id=1, source_target_pairs={{125,0},{126,1},{127,2},{0,3},{1,4},{2,5},{3,6},{4,7},{5,8},{6,9},... | collective-permute-start | bytes 110600 | tf_op jit(solution)/shard_map/ppermute | solution.py:452
  51.0 0.0 collective-permute-start.7
  51.0 0.0 collective-permute-start.6
  51.0 0.5 collective-permute-start.5
  51.6 7.0 %collective-permute-done.9.refs_7_ = f32[9,8,128]{2,1,0:T(8,128)S(1)} collective-permute-done((f32[9,8,128]{2,1,0:T(8,128)S(1)}, f32[9,8,128]{2,1,0:T(8,128)S(1)}, u32[]{:S(2)}, u32[]{:S(2)}) %collective-permute-start.9) | collective-permute-done | bytes 36896 | tf_op jit(solution)/shard_map/ppermute | solution.py:452
  58.5 2.9 %collective-permute-start.4 = (f32[9,8,128]{2,1,0:T(8,128)S(1)}, f32[9,8,128]{2,1,0:T(8,128)S(1)}, u32[]{:S(2)}, u32[]{:S(2)}) collective-permute-start(f32[9,8,128]{2,1,0:T(8,128)S(1)} %get-tuple-element.14), channel_id=1, source_target_pairs={{2,0},{3,1},{4,2},{5,3},{6,4},{7,5},{8,6},{9,7},{10,8},{11,9},{12,... | collective-permute-start | bytes 110600 | tf_op jit(solution)/shard_map/ppermute | solution.py:452
  61.5 0.0 collective-permute-done.8.refs_6_
  61.5 1.0 %collective-permute-start.3 = (f32[9,8,128]{2,1,0:T(8,128)S(1)}, f32[9,8,128]{2,1,0:T(8,128)S(1)}, u32[]{:S(2)}, u32[]{:S(2)}) collective-permute-start(f32[9,8,128]{2,1,0:T(8,128)S(1)} %get-tuple-element.15), channel_id=1, source_target_pairs={{3,0},{4,1},{5,2},{6,3},{7,4},{8,5},{9,6},{10,7},{11,8},{12,9},{13... | collective-permute-start | bytes 110600 | tf_op jit(solution)/shard_map/ppermute | solution.py:452
  62.4 0.0 collective-permute-done.7.refs_5_
  62.4 3.1 %collective-permute-start.2 = (f32[9,8,128]{2,1,0:T(8,128)S(1)}, f32[9,8,128]{2,1,0:T(8,128)S(1)}, u32[]{:S(2)}, u32[]{:S(2)}) collective-permute-start(f32[9,8,128]{2,1,0:T(8,128)S(1)} %get-tuple-element.16), channel_id=1, source_target_pairs={{4,0},{5,1},{6,2},{7,3},{8,4},{9,5},{10,6},{11,7},{12,8},{13,9},{1... | collective-permute-start | bytes 110600 | tf_op jit(solution)/shard_map/ppermute | solution.py:452
  65.6 0.0 collective-permute-done.6.refs_4_
  65.6 0.0 collective-permute-done.5.refs_3_
  65.6 0.0 collective-permute-done.4.refs_2_
  65.6 0.8 %collective-permute-done.3.refs_1_ = f32[9,8,128]{2,1,0:T(8,128)S(1)} collective-permute-done((f32[9,8,128]{2,1,0:T(8,128)S(1)}, f32[9,8,128]{2,1,0:T(8,128)S(1)}, u32[]{:S(2)}, u32[]{:S(2)}) %collective-permute-start.3) | collective-permute-done | bytes 36896 | tf_op jit(solution)/shard_map/ppermute | solution.py:452
  66.4 1.0 %collective-permute-done.2.refs_0_ = f32[9,8,128]{2,1,0:T(8,128)S(1)} collective-permute-done((f32[9,8,128]{2,1,0:T(8,128)S(1)}, f32[9,8,128]{2,1,0:T(8,128)S(1)}, u32[]{:S(2)}, u32[]{:S(2)}) %collective-permute-start.2) | collective-permute-done | bytes 36896 | tf_op jit(solution)/shard_map/ppermute | solution.py:452
  67.4 1.0 %shard_map.92 = f32[9,24576]{1,0:T(8,128)} custom-call(f32[9,8,128]{2,1,0:T(8,128)S(1)} %collective-permute-done.2.refs_0_, f32[9,8,128]{2,1,0:T(8,128)S(1)} %collective-permute-done.3.refs_1_, f32[9,8,128]{2,1,0:T(8,128)S(1)} %collective-permute-done.4.refs_2_, f32[9,8,128]{2,1,0:T(8,128)S(1)} %collective-permute-done.5.refs_3_, ...), custom_call_target="tpu_custom_call", output_to_operand_aliasing={{}: (8, {})} | custom-call | tf_op jit(solution)/shard_map/pallas_call | solution.py:453
  (14 shorter events, 0.1 us)
Async XLA Ops:
  5.1 10.6 %collective-permute-start = (f32[96,128]{1,0:T(8,128)S(1)}, f32[96,128]{1,0:T(8,128)S(1)}, u32[]{:S(2)}, u32[]{:S(2)}) collective-permute-start(f32[96,128]{1,0:T(8,128)S(1)} %get-tuple-element.21), channel_id=1, source_target_pairs={{1,2},{3,4},{5,6},{7,8},{9,10},{11,12},{13,14},{15,16},{17,18},{19... | collective-permute-start | bytes 147464 | tf_op jit(solution)/shard_map/ppermute | solution.py:331
  8.2 7.5 %collective-permute-start.1 = (f32[96,128]{1,0:T(8,128)S(1)}, f32[96,128]{1,0:T(8,128)S(1)}, u32[]{:S(2)}, u32[]{:S(2)}) collective-permute-start(f32[96,128]{1,0:T(8,128)S(1)} %get-tuple-element.22), channel_id=1, source_target_pairs={{0,1},{2,3},{4,5},{6,7},{8,9},{10,11},{12,13},{14,15},{16,17},{18,... | collective-permute-start | bytes 147464 | tf_op jit(solution)/shard_map/ppermute | solution.py:331
  15.8 1.0 %copy-start = (f32[3,16384]{1,0:T(4,128)S(1)}, f32[3,16384]{1,0:T(4,128)}, u32[]{:S(2)}) copy-start(f32[3,16384]{1,0:T(4,128)} %pos_ref.1) | copy-start | bytes 589828
  16.8 0.9 %copy-start.1 = (f32[3,16384]{1,0:T(4,128)S(1)}, f32[3,16384]{1,0:T(4,128)}, u32[]{:S(2)}) copy-start(f32[3,16384]{1,0:T(4,128)} %vel_ref.1) | copy-start | bytes 589828
  17.7 0.8 %copy-start.2 = (s32[16384]{0:T(1024)S(1)}, s32[16384]{0:T(1024)}, u32[]{:S(2)}) copy-start(s32[16384]{0:T(1024)} %param.14) | copy-start | bytes 196612
  18.6 0.8 %copy-start.3 = (f32[16384]{0:T(1024)S(1)}, f32[16384]{0:T(1024)}, u32[]{:S(2)}) copy-start(f32[16384]{0:T(1024)} %param.11) | copy-start | bytes 196612
  19.4 0.8 %copy-start.4 = (f32[16384]{0:T(1024)S(1)}, f32[16384]{0:T(1024)}, u32[]{:S(2)}) copy-start(f32[16384]{0:T(1024)} %param.12) | copy-start | bytes 196612
  20.3 0.8 %copy-start.5 = (f32[16384]{0:T(1024)S(1)}, f32[16384]{0:T(1024)}, u32[]{:S(2)}) copy-start(f32[16384]{0:T(1024)} %param.13) | copy-start | bytes 196612
  21.1 0.8 %copy-start.6 = (s32[16384]{0:T(1024)S(1)}, s32[16384]{0:T(1024)}, u32[]{:S(2)}) copy-start(s32[16384]{0:T(1024)} %param.16) | copy-start | bytes 196612
  21.9 0.8 %copy-start.7 = (s32[16384]{0:T(1024)S(1)}, s32[16384]{0:T(1024)}, u32[]{:S(2)}) copy-start(s32[16384]{0:T(1024)} %param.17) | copy-start | bytes 196612
  49.9 8.6 %collective-permute-start.9 = (f32[9,8,128]{2,1,0:T(8,128)S(1)}, f32[9,8,128]{2,1,0:T(8,128)S(1)}, u32[]{:S(2)}, u32[]{:S(2)}) collective-permute-start(f32[9,8,128]{2,1,0:T(8,128)S(1)} %get-tuple-element.9), channel_id=1, source_target_pairs={{124,0},{125,1},{126,2},{127,3},{0,4},{1,5},{2,6},{3,7},{4,8},{5,9... | collective-permute-start | bytes 110600 | tf_op jit(solution)/shard_map/ppermute | solution.py:452
  50.0 11.5 %collective-permute-start.8 = (f32[9,8,128]{2,1,0:T(8,128)S(1)}, f32[9,8,128]{2,1,0:T(8,128)S(1)}, u32[]{:S(2)}, u32[]{:S(2)}) collective-permute-start(f32[9,8,128]{2,1,0:T(8,128)S(1)} %get-tuple-element.10), channel_id=1, source_target_pairs={{125,0},{126,1},{127,2},{0,3},{1,4},{2,5},{3,6},{4,7},{5,8},{6,9},... | collective-permute-start | bytes 110600 | tf_op jit(solution)/shard_map/ppermute | solution.py:452
  51.0 11.4 %collective-permute-start.7 = (f32[9,8,128]{2,1,0:T(8,128)S(1)}, f32[9,8,128]{2,1,0:T(8,128)S(1)}, u32[]{:S(2)}, u32[]{:S(2)}) collective-permute-start(f32[9,8,128]{2,1,0:T(8,128)S(1)} %get-tuple-element.11), channel_id=1, source_target_pairs={{126,0},{127,1},{0,2},{1,3},{2,4},{3,5},{4,6},{5,7},{6,8},{7,9},{8... | collective-permute-start | bytes 110600 | tf_op jit(solution)/shard_map/ppermute | solution.py:452
  51.0 14.5 %collective-permute-start.6 = (f32[9,8,128]{2,1,0:T(8,128)S(1)}, f32[9,8,128]{2,1,0:T(8,128)S(1)}, u32[]{:S(2)}, u32[]{:S(2)}) collective-permute-start(f32[9,8,128]{2,1,0:T(8,128)S(1)} %get-tuple-element.12), channel_id=1, source_target_pairs={{127,0},{0,1},{1,2},{2,3},{3,4},{4,5},{5,6},{6,7},{7,8},{8,9},{9,1... | collective-permute-start | bytes 110600 | tf_op jit(solution)/shard_map/ppermute | solution.py:452
  51.0 14.5 %collective-permute-start.5 = (f32[9,8,128]{2,1,0:T(8,128)S(1)}, f32[9,8,128]{2,1,0:T(8,128)S(1)}, u32[]{:S(2)}, u32[]{:S(2)}) collective-permute-start(f32[9,8,128]{2,1,0:T(8,128)S(1)} %get-tuple-element.13), channel_id=1, source_target_pairs={{1,0},{2,1},{3,2},{4,3},{5,4},{6,5},{7,6},{8,7},{9,8},{10,9},{11,1... | collective-permute-start | bytes 110600 | tf_op jit(solution)/shard_map/ppermute | solution.py:452
  58.5 7.0 %collective-permute-start.4 = (f32[9,8,128]{2,1,0:T(8,128)S(1)}, f32[9,8,128]{2,1,0:T(8,128)S(1)}, u32[]{:S(2)}, u32[]{:S(2)}) collective-permute-start(f32[9,8,128]{2,1,0:T(8,128)S(1)} %get-tuple-element.14), channel_id=1, source_target_pairs={{2,0},{3,1},{4,2},{5,3},{6,4},{7,5},{8,6},{9,7},{10,8},{11,9},{12,... | collective-permute-start | bytes 110600 | tf_op jit(solution)/shard_map/ppermute | solution.py:452
  61.5 4.9 %collective-permute-start.3 = (f32[9,8,128]{2,1,0:T(8,128)S(1)}, f32[9,8,128]{2,1,0:T(8,128)S(1)}, u32[]{:S(2)}, u32[]{:S(2)}) collective-permute-start(f32[9,8,128]{2,1,0:T(8,128)S(1)} %get-tuple-element.15), channel_id=1, source_target_pairs={{3,0},{4,1},{5,2},{6,3},{7,4},{8,5},{9,6},{10,7},{11,8},{12,9},{13... | collective-permute-start | bytes 110600 | tf_op jit(solution)/shard_map/ppermute | solution.py:452
  62.4 4.9 %collective-permute-start.2 = (f32[9,8,128]{2,1,0:T(8,128)S(1)}, f32[9,8,128]{2,1,0:T(8,128)S(1)}, u32[]{:S(2)}, u32[]{:S(2)}) collective-permute-start(f32[9,8,128]{2,1,0:T(8,128)S(1)} %get-tuple-element.16), channel_id=1, source_target_pairs={{4,0},{5,1},{6,2},{7,3},{8,4},{9,5},{10,6},{11,7},{12,8},{13,9},{1... | collective-permute-start | bytes 110600 | tf_op jit(solution)/shard_map/ppermute | solution.py:452

commit v2 on v0

v2 whole, which is shorter than its diff:
```python
import functools

import jax
import jax.numpy as jnp
from jax import lax
from jax.experimental import pallas as pl
from jax.experimental.pallas import tpu as pltpu
from jax.sharding import PartitionSpec as P

CELL_PARTICLES = 256
HALO = 4
REACH = 4
PART_DEV = 16384
MOST = 1024
RECV_DEV = 24576
CELLS_DEV = 64
NEIGHBOURS = 6
LANES = 128
ROWS = PART_DEV // LANES
EDGE = 2 * HALO
EXT = CELLS_DEV + 2 * EDGE
EXT_ROWS = 2 * EXT
EDGE_ROWS = 2 * EDGE
HALO_ROWS = 96
GHOST = HALO
LISTED = CELLS_DEV + 2 * GHOST
OWN = slice(EDGE_ROWS, EDGE_ROWS + ROWS)
PACK_ROWS = 8
DUMMY = EDGE * 64 + 32 + (8 << 20)
UNROLL = 8
LIST_SIZE = LISTED * 32 + 64
GROUPS = 2 * REACH
time_step = 0.25
FIELDS = 9


def bcast(ref, row):
    return ref[pl.ds(row, 8, stride=0), :]


def edge_kernel(
    own_ref, pos_ref, mass_ref, ent_ref, rho_ref, act_ref, nbr_ref, far_ref, near_ref,
    pos_v, act_v, nbr_v, sem
):
    even = own_ref[0] % 2 == 0
    copies = []
    nbr_copy = pltpu.make_async_copy(nbr_ref, nbr_v, sem.at[0])
    nbr_copy.start()
    for side, ref in enumerate((far_ref, near_ref)):
        low = even if side == 0 else jnp.logical_not(even)
        wide = pl.multiple_of(jnp.where(low, 0, ROWS - EDGE_ROWS), 8)
        near = pl.multiple_of(jnp.where(low, 0, ROWS - 8), 8)
        lane = pl.multiple_of(jnp.where(low, 0, PART_DEV - EDGE * CELL_PARTICLES), LANES)
        base = 1 + 5 * side
        pairs = [
            (pos_ref.at[:, pl.ds(lane, EDGE * CELL_PARTICLES)], pos_v.at[side]),
            (mass_ref.at[pl.ds(wide, EDGE_ROWS)], ref.at[pl.ds(48, EDGE_ROWS)]),
            (ent_ref.at[pl.ds(near, 8)], ref.at[pl.ds(64, 8)]),
            (rho_ref.at[pl.ds(near, 8)], ref.at[pl.ds(72, 8)]),
            (act_ref.at[pl.ds(near, 8)], act_v.at[side]),
        ]
        for k, (a, b) in enumerate(pairs):
            copy = pltpu.make_async_copy(a, b, sem.at[base + k])
            copy.start()
            copies.append(copy)
    nbr_copy.wait()
    for copy in copies:
        copy.wait()
    lists = nbr_v[...].astype(jnp.float32)
    for side, ref in enumerate((far_ref, near_ref)):
        for c in range(3):
            for i in range(EDGE_ROWS):
                ref[16 * c + i : 16 * c + i + 1, :] = (
                    pos_v[side, c : c + 1, i * LANES : (i + 1) * LANES] * 0.5
                )
        ref[80:88, :] = (act_v[side] == 1).astype(jnp.float32)
        ref[88:96, :] = jnp.zeros((8, LANES), jnp.float32)
        ref[88 : 88 + NEIGHBOURS, 0:CELLS_DEV] = lists


def state_kernel(
    own_ref, pos_ref, vel_ref, mass_ref, ent_ref, rho_ref, act_ref, dest_ref, slot_ref,
    nbr_ref, far_ref, near_ref,
    kept_ref, to_far, to_far2, to_next, to_next2, to_other,
    pos_v, vel_v, act_v, dest_v, slot_v, nbr_v,
    xs, ys, zs, ms, ps, es, rho_old, rank, dens, ax, ay, az,
    fields, key, shifts, parts, hi_row, lo_row, a0, b0, packed, blocks,
    table_v, table, chunk_list, sem,
):
    own = own_ref[0]
    even = own % 2 == 0
    scale = 8.0 / (NEIGHBOURS * CELL_PARTICLES)
    loads = [
        (pos_ref, pos_v),
        (vel_ref, vel_v),
        (mass_ref, ms.at[pl.ds(EDGE_ROWS, ROWS)]),
        (ent_ref, es.at[pl.ds(EDGE_ROWS, ROWS)]),
        (rho_ref, rho_old.at[pl.ds(EDGE_ROWS, ROWS)]),
        (act_ref, act_v),
        (dest_ref, dest_v),
        (slot_ref, slot_v),
        (nbr_ref, nbr_v),
    ]
    loads = [pltpu.make_async_copy(a, b, sem.at[k]) for k, (a, b) in enumerate(loads)]
    for copy in loads:
        copy.start()

    def side_rows(first, last):
        f, n = far_ref[first:last, :], near_ref[first:last, :]
        return jnp.where(even, f, n), jnp.where(even, n, f)

    high = slice(EDGE_ROWS + ROWS, EXT_ROWS)
    for k, ref in enumerate((xs, ys, zs, ms)):
        ref[0:EDGE_ROWS, :], ref[high, :] = side_rows(16 * k, 16 * k + 16)
    zeros8 = jnp.zeros((8, LANES), jnp.float32)
    ghost_act = side_rows(80, 88)
    for ref, rows, fill in ((es, (64, 72), 0.0), (rho_old, (72, 80), 1.0)):
        ref[0:8, :] = zeros8 + fill
        ref[EXT_ROWS - 8 :, :] = zeros8 + fill
        ref[8:16, :], ref[EXT_ROWS - 16 : EXT_ROWS - 8, :] = side_rows(*rows)
    for ref in (dens, ax, ay, az, packed):
        ref[...] = jnp.zeros_like(ref)
    for copy in loads:
        copy.wait()

    act = jnp.concatenate(
        [zeros8, ghost_act[0], (act_v[...] == 1).astype(jnp.float32), ghost_act[1], zeros8],
        axis=0,
    )
    before = (
        lax.broadcasted_iota(jnp.int32, (LANES, LANES), 0)
        < lax.broadcasted_iota(jnp.int32, (LANES, LANES), 1)
    ).astype(jnp.bfloat16)
    ones = jnp.ones((LANES, LANES), jnp.bfloat16)
    act16 = act.astype(jnp.bfloat16)
    in_lanes = lax.dot_general(
        ones[0:16], act16, (((1,), (1,)), ((), ())), preferred_element_type=jnp.float32
    )
    table_v[0:8, 0:EXT_ROWS] = in_lanes[0:8].astype(jnp.int32)
    shift = own * CELLS_DEV - EDGE
    near_lists = side_rows(88, 96)
    pad = jnp.zeros((8 - NEIGHBOURS, CELLS_DEV), jnp.int32)
    table_v[8:16, 0:CELLS_DEV] = (jnp.concatenate([nbr_v[...], pad]) - shift) & 8191
    for k in range(2):
        table_v[16 + 8 * k : 24 + 8 * k, 0:LANES] = (
            near_lists[k].astype(jnp.int32) - shift
        ) & 8191
    table_copy = pltpu.make_async_copy(table_v, table, sem.at[9])
    table_copy.start()
    inside = jnp.dot(act16, before, preferred_element_type=jnp.float32)
    total = jnp.dot(act16, ones, preferred_element_type=jnp.float32)
    row_id = lax.broadcasted_iota(jnp.int32, (EXT_ROWS, LANES), 0)
    rank[...] = jnp.where(
        act > 0.5, inside + jnp.where(row_id % 2 == 1, pltpu.roll(total, 1, 0), 0.0), -1.0
    )

    dest = dest_v[...]
    away = (dest - own) & 127
    signed = jnp.where(away > 64, away - 128, away)
    group = jnp.where(signed < 0, signed + REACH, signed + REACH - 1)
    place = (slot_v[...] - PART_DEV) & (MOST - 1)
    moving = dest != own
    hi = (group >> 1) * 8 + (place >> 7)
    lo = (group & 1) * LANES + (place & (LANES - 1))
    key[...] = jnp.where(moving, hi * 256 + lo, -1)
    mover16 = moving.astype(jnp.float32).astype(jnp.bfloat16)
    above = lax.dot_general(
        before, mover16, (((0,), (0,)), ((), ())), preferred_element_type=jnp.float32
    ).astype(jnp.int32)
    in_column = jnp.dot(ones, mover16, preferred_element_type=jnp.float32).astype(jnp.int32)
    own_row = lax.broadcasted_iota(jnp.int32, (ROWS, LANES), 0)
    remaining = jnp.where(moving, own_row - above, 0)
    for bit in range(7):
        coming = pltpu.roll(remaining, ROWS - (1 << bit), 0)
        lands = (coming >> bit) & 1
        leaves = (remaining >> bit) & 1
        shifts[bit] = lands
        remaining = jnp.where(lands == 1, coming, jnp.where(leaves == 1, 0, remaining))
    mover_rows = jnp.max(in_column)

    def moved_up(x):
        for bit in range(7):
            x = jnp.where(shifts[bit] == 1, pltpu.roll(x, ROWS - (1 << bit), 0), x)
        return x

    new_key = jnp.where(own_row < in_column, moved_up(key[...]), -1)
    hi_row[...] = (new_key >> 8).astype(jnp.float32)
    lo_row[...] = (new_key & 255).astype(jnp.float32)

    def split_rows(i, carry):
        col = pl.multiple_of(i * LANES, LANES)
        p = pos_v[:, pl.ds(col, LANES)]
        v = vel_v[:, pl.ds(col, LANES)]
        for c, ref in enumerate((xs, ys, zs)):
            fields[c, pl.ds(i, 1), :] = p[c : c + 1, :]
            fields[3 + c, pl.ds(i, 1), :] = v[c : c + 1, :]
        return carry

    lax.fori_loop(0, ROWS, split_rows, 0, unroll=8)
    for c, ref in enumerate((xs, ys, zs)):
        ref[OWN, :] = fields[c] * 0.5
    fields[6] = rho_old[OWN, :]
    fields[7] = es[OWN, :]
    fields[8] = ms[OWN, :]
    table_copy.wait()

    cells = [(EDGE + k, k, 8) for k in range(CELLS_DEV)]
    cells += [(EDGE - GHOST + k, CELLS_DEV - GHOST + k, 16) for k in range(GHOST)]
    cells += [(EDGE + CELLS_DEV + k, k, 24) for k in range(GHOST)]
    at, most, own_total = 0, 0, 0
    for number, (cell, lane, row) in enumerate(cells):
        n = table[0, 2 * cell] + table[0, 2 * cell + 1]
        code = (row << 20) + (lane << 13) + (cell << 6)
        for k in range(4):
            chunk_list[at + k] = code + k
        at = at + ((n + 7) >> 3)
        most = jnp.maximum(most, n)
        if number == CELLS_DEV - 1:
            own_total = at
    all_total = at

    @pl.when(most > 32)
    def _():
        def refill(first, count, lane0, row):
            def one(k, start):
                cell = first + k
                n = table[0, 2 * cell] + table[0, 2 * cell + 1]
                code = (row << 20) + ((lane0 + k) << 13) + (cell << 6)

                def put(j, carry):
                    chunk_list[start + j] = code + j
                    return carry

                lax.fori_loop(0, (n + 7) >> 3, put, 0)
                return start + ((n + 7) >> 3)

            return lambda start: lax.fori_loop(0, count, one, start)

        start = refill(EDGE, CELLS_DEV, 0, 8)(0)
        start = refill(EDGE - GHOST, GHOST, CELLS_DEV - GHOST, 16)(start)
        refill(EDGE + CELLS_DEV, GHOST, 0, 24)(start)

    sub = lax.broadcasted_iota(jnp.int32, (8, LANES), 0).astype(jnp.float32)

    def chunk_of(position, limit):
        code = chunk_list[jnp.maximum(jnp.minimum(position, limit - 1), 0)]
        code = jnp.where(position < limit, code, DUMMY)
        cell = (code >> 6) & 127
        want = sub + ((code & 63) * 8).astype(jnp.float32)
        picks = [bcast(rank, 2 * cell + h) == want for h in range(2)]
        lane = (code >> 13) & 127
        sources = [table[(code >> 20) + q, lane] for q in range(NEIGHBOURS)]
        return cell, picks, sources

    def column(ref, cell, picks):
        both = jnp.where(picks[0], bcast(ref, 2 * cell), 0.0) + jnp.where(
            picks[1], bcast(ref, 2 * cell + 1), 0.0
        )
        return jnp.sum(both, axis=1, keepdims=True)

    def spread(ref, cell, picks, value):
        for h in range(2):
            row = jnp.sum(jnp.where(picks[h], value, 0.0), axis=0, keepdims=True)
            ref[pl.ds(2 * cell + h, 1), :] += row

    def density_step(step):
        done = []
        for u in range(UNROLL):
            cell, picks, sources = chunk_of(step * UNROLL + u, all_total)
            cx, cy, cz = (column(ref, cell, picks) for ref in (xs, ys, zs))
            total_rows = jnp.zeros((8, LANES), jnp.float32)
            for source in sources:
                for h in range(2):
                    row = 2 * source + h
                    dx = cx - bcast(xs, row)
                    dy = cy - bcast(ys, row)
                    dz = cz - bcast(zs, row)
                    u1 = jnp.maximum(1.0 - (dx * dx + dy * dy + dz * dz), 0.0)
                    total_rows += u1 * u1 * u1 * bcast(ms, row)
            value = jnp.sum(total_rows, axis=1, keepdims=True) * scale
            done.append((cell, picks, value))
        for cell, picks, value in done:
            spread(dens, cell, picks, value)

    def density_loop(step, carry):
        density_step(step)
        return carry

    lax.fori_loop(0, (all_total + UNROLL - 1) // UNROLL, density_loop, 0)

    rho = jnp.where(rank[...] >= 0.0, dens[...], rho_old[...])
    dens[...] = rho
    ps[...] = es[...] * jnp.exp(jnp.log(rho) * (-1.0 / 3.0))

    def force_step(step, carry):
        done = []
        for u in range(UNROLL):
            cell, picks, sources = chunk_of(step * UNROLL + u, own_total)
            cx, cy, cz, cp = (column(ref, cell, picks) for ref in (xs, ys, zs, ps))
            sx = jnp.zeros((8, LANES), jnp.float32)
            sy = jnp.zeros((8, LANES), jnp.float32)
            sz = jnp.zeros((8, LANES), jnp.float32)
            for source in sources:
                for h in range(2):
                    row = 2 * source + h
                    dx = cx - bcast(xs, row)
                    dy = cy - bcast(ys, row)
                    dz = cz - bcast(zs, row)
                    u1 = jnp.maximum(1.0 - (dx * dx + dy * dy + dz * dz), 0.0)
                    w = u1 * u1 * (bcast(ms, row) * (cp + bcast(ps, row)))
                    sx += w * dx
                    sy += w * dy
                    sz += w * dz
            values = [
                jnp.sum(s, axis=1, keepdims=True) * (3.0 * scale * time_step)
                for s in (sx, sy, sz)
            ]
            done.append((cell, picks, values))
        for cell, picks, values in done:
            for ref, value in zip((ax, ay, az), values):
                spread(ref, cell, picks, value)
        return carry

    lax.fori_loop(0, (own_total + UNROLL - 1) // UNROLL, force_step, 0)

    for c, acc in enumerate((ax, ay, az)):
        kicked = fields[3 + c] + acc[OWN, :]
        fields[3 + c] = kicked
        fields[c] = fields[c] + time_step * kicked
    fields[6] = dens[OWN, :]
    stays = dest_v[...] == own
    for v in range(FIELDS):
        whole = fields[v]
        kept_ref[v] = jnp.where(stays, whole, 0.0)
        whole = moved_up(whole)
        first = whole.astype(jnp.bfloat16).astype(jnp.float32)
        parts[v] = first
        parts[FIELDS + v] = whole - first

    bf = jnp.bfloat16
    iota16 = lax.broadcasted_iota(jnp.int32, (16, LANES), 0).astype(jnp.float32).astype(bf)
    one16, zero16 = jnp.ones((16, LANES), bf), jnp.zeros((16, LANES), bf)

    def twice(x):
        return jnp.concatenate([x, x], axis=0).astype(bf)

    def pack_step(step, carry):
        for j in range(PACK_ROWS):
            row = step * PACK_ROWS + j
            cols = slice(j * LANES, (j + 1) * LANES)
            hi_b, lo_b = twice(bcast(hi_row, row)), twice(bcast(lo_row, row))
            for k in range(16):
                b0[16 * k : 16 * k + 16, cols] = jnp.where(
                    lo_b == iota16 + bf(16 * k), one16, zero16
                )
            upper = hi_b == iota16
            lower = hi_b == iota16 + bf(16)
            for v in range(2 * FIELDS):
                value = twice(parts[v, pl.ds(row, 8, stride=0), :])
                a0[32 * v : 32 * v + 16, cols] = jnp.where(upper, value, zero16)
                a0[32 * v + 16 : 32 * v + 32, cols] = jnp.where(lower, value, zero16)
        packed[...] += lax.dot_general(
            a0[...], b0[...], (((1,), (1,)), ((), ())), preferred_element_type=jnp.float32
        )
        return carry

    lax.fori_loop(0, (mover_rows + PACK_ROWS - 1) // PACK_ROWS, pack_step, 0)

    for g in range(GROUPS):
        cols = slice((g & 1) * LANES, (g & 1) * LANES + LANES)
        for v in range(FIELDS):
            r = 32 * v + (g >> 1) * 8
            s = r + 32 * FIELDS
            blocks[g, v] = packed[r : r + 8, cols] + packed[s : s + 8, cols]
    turn = 1 - 2 * (own & 1)
    for ref, step in zip((to_next, to_next2, to_far, to_far2), chip_steps(own)):
        ref[0] = blocks[group_of(2 * step)]
        ref[1] = blocks[group_of(2 * step + turn)]
    to_other[...] = blocks[group_of(turn)]


def chip_steps(own):
    even = jnp.where((own >> 1) & 1 == 0, 1, -1)
    low = jnp.where((own >> 2) & 1 == 0, 2, -2)
    return even, -even, low, -low


def group_of(offset):
    g = jnp.where(offset < 0, offset + REACH, offset + REACH - 1)
    return jnp.minimum(jnp.maximum(g, 0), GROUPS - 1)


def stay_kernel(kept_ref, out_ref, rows, sem):
    def step(i, carry):
        col = pl.multiple_of(i * LANES, LANES)
        for v in range(FIELDS):
            rows[v : v + 1, pl.ds(col, LANES)] = kept_ref[v, pl.ds(i, 1), :]
        return carry

    lax.fori_loop(0, ROWS, step, 0, unroll=8)
    copy = pltpu.make_async_copy(rows, out_ref.at[:, pl.ds(0, PART_DEV)], sem.at[0])
    copy.start()
    copy.wait()


def assemble_kernel(
    own_ref, next_ref, next2_ref, far_ref, far2_ref, other_ref,
    x_next, x_next2, x_far, x_far2, held_ref, out_ref, rows, sem
):
    del held_ref
    own = own_ref[0]
    turn = 1 - 2 * (own & 1)
    steps = chip_steps(own)
    low = (own >> 2) & 1 == 0
    pick_low = low == (turn < 0)
    parts = [(ref, (0,), -2 * step) for ref, step in zip((next_ref, next2_ref, far_ref, far2_ref), steps)]
    parts += [(ref, (1,), -2 * step - turn) for ref, step in zip((x_next, x_next2), steps)]
    parts += [(other_ref, (), -turn)]
    parts += [(None, (), 3 * turn)]

    for ref, index, offset in parts:
        start = group_of(offset) * MOST
        for v in range(FIELDS):
            if ref is None:
                tile = jnp.where(pick_low, x_far[1, v], x_far2[1, v])
            else:
                tile = ref[index + (v,)]
            for r in range(8):
                col = pl.multiple_of(start + r * LANES, LANES)
                rows[v : v + 1, pl.ds(col, LANES)] = tile[r : r + 1, :]
    copy = pltpu.make_async_copy(
        rows, out_ref.at[:, pl.ds(PART_DEV, GROUPS * MOST)], sem.at[0]
    )
    copy.start()
    copy.wait()


def swapped(block, pairs):
    route = [(a, b) for a, b in pairs] + [(b, a) for a, b in pairs]
    return lax.ppermute(block, "cells", route)


def per_device(
    position,
    velocity,
    particle_mass,
    entropy,
    density_old,
    active,
    neighbours,
    destination,
    recv_slot,
):
    count = lax.axis_size("cells")
    own = lax.axis_index("cells").reshape(1)
    square = (ROWS, LANES)
    mass, ent, rho, act = (
        a.reshape(square) for a in (particle_mass, entropy, density_old, active)
    )
    lists = neighbours.T
    vm = pl.BlockSpec(memory_space=pltpu.VMEM)
    sm = pl.BlockSpec(memory_space=pltpu.SMEM)
    hbm = pl.BlockSpec(memory_space=pl.ANY)
    f32, i32 = jnp.float32, jnp.int32
    far, near = pl.pallas_call(
        edge_kernel,
        out_shape=(jax.ShapeDtypeStruct((HALO_ROWS, LANES), f32),) * 2,
        in_specs=[sm] + [hbm] * 6,
        out_specs=(vm, vm),
        scratch_shapes=[
            pltpu.VMEM((2, 3, EDGE * CELL_PARTICLES), f32),
            pltpu.VMEM((2, 8, LANES), i32),
            pltpu.VMEM((NEIGHBOURS, CELLS_DEV), i32),
            pltpu.SemaphoreType.DMA((11,)),
        ],
        compiler_params=pltpu.CompilerParams(vmem_limit_bytes=56 * 2**20),
    )(own, position, mass, ent, rho, act, lists)
    near_pairs = [(2 * k, 2 * k + 1) for k in range(count // 2)]
    far_pairs = [(2 * k + 1, (2 * k + 2) % count) for k in range(count // 2)]
    far = swapped(far, far_pairs)
    near = swapped(near, near_pairs)

    ext = pltpu.VMEM((EXT_ROWS, LANES), f32)
    flat = pltpu.VMEM((3, PART_DEV), f32)
    whole = pltpu.VMEM(square, i32)
    pair = jax.ShapeDtypeStruct((2, FIELDS, 8, LANES), f32)
    kept, *sends = pl.pallas_call(
        state_kernel,
        out_shape=(
            jax.ShapeDtypeStruct((FIELDS, ROWS, LANES), f32),
            pair,
            pair,
            pair,
            pair,
            jax.ShapeDtypeStruct((FIELDS, 8, LANES), f32),
        ),
        in_specs=[sm] + [hbm] * 9 + [vm] * 2,
        out_specs=(vm,) * 6,
        scratch_shapes=[flat, flat, whole, whole, whole]
        + [pltpu.VMEM((NEIGHBOURS, CELLS_DEV), i32)]
        + [ext] * 12
        + [
            pltpu.VMEM((FIELDS, ROWS, LANES), f32),
            whole,
            pltpu.VMEM((7, ROWS, LANES), i32),
            pltpu.VMEM((2 * FIELDS, ROWS, LANES), f32),
            pltpu.VMEM(square, f32),
            pltpu.VMEM(square, f32),
            pltpu.VMEM((64 * FIELDS, PACK_ROWS * LANES), jnp.bfloat16),
            pltpu.VMEM((256, PACK_ROWS * LANES), jnp.bfloat16),
            pltpu.VMEM((64 * FIELDS, 256), f32),
            pltpu.VMEM((GROUPS, FIELDS, 8, LANES), f32),
            pltpu.VMEM((32, 256), i32),
            pltpu.SMEM((32, 256), i32),
            pltpu.SMEM((LIST_SIZE,), i32),
            pltpu.SemaphoreType.DMA((10,)),
        ],
        compiler_params=pltpu.CompilerParams(vmem_limit_bytes=56 * 2**20),
    )(
        own,
        position,
        velocity,
        mass,
        ent,
        rho,
        act,
        destination.reshape(square),
        recv_slot.reshape(square),
        lists,
        far,
        near,
    )
    to_far, to_far2, to_next, to_next2, to_other = sends
    chips = count // 2

    def chip_pairs(distance, first):
        firsts = [c for c in range(chips) if (c // distance) % 2 == first]
        return [
            (2 * c + core, 2 * ((c + distance) % chips) + core)
            for c in firsts
            for core in range(2)
        ]

    other = swapped(to_other, near_pairs)
    next2 = swapped(to_next2, chip_pairs(1, 1))
    far2 = swapped(to_far2, chip_pairs(2, 1))
    next1 = swapped(to_next, chip_pairs(1, 0))
    far1 = swapped(to_far, chip_pairs(2, 0))
    crossed = [swapped(x, near_pairs) for x in (next1, next2, far1, far2)]
    held = pl.pallas_call(
        stay_kernel,
        out_shape=jax.ShapeDtypeStruct((FIELDS, RECV_DEV), f32),
        in_specs=[vm],
        out_specs=hbm,
        scratch_shapes=[
            pltpu.VMEM((FIELDS, PART_DEV), f32),
            pltpu.SemaphoreType.DMA((1,)),
        ],
        compiler_params=pltpu.CompilerParams(vmem_limit_bytes=16 * 2**20),
    )(kept)
    return pl.pallas_call(
        assemble_kernel,
        out_shape=jax.ShapeDtypeStruct((FIELDS, RECV_DEV), f32),
        in_specs=[sm] + [vm] * 9 + [hbm],
        out_specs=hbm,
        scratch_shapes=[
            pltpu.VMEM((FIELDS, GROUPS * MOST), f32),
            pltpu.SemaphoreType.DMA((1,)),
        ],
        input_output_aliases={10: 0},
        compiler_params=pltpu.CompilerParams(vmem_limit_bytes=16 * 2**20),
    )(own, next1, next2, far1, far2, other, *crossed, held)


def solution(mesh):
    placed = (
        P(None, "cells"),
        P(None, "cells"),
        P("cells"),
        P("cells"),
        P("cells"),
        P("cells"),
        P("cells", None),
        P("cells"),
        P("cells"),
    )
    return jax.shard_map(
        per_device, mesh=mesh, in_specs=placed, out_specs=P(None, "cells"), check_vma=False
    )
```

time: 345 us -> 53.2 us (0.15); the launches traced: 339 us -> 52.4 us
  other arithmetic: 154 us -> 0 us
  local copies, waits for them, and re-layouts: 86.1 us -> 1.68 us
  waiting for transfers between devices: 37.3 us -> 7.01 us
  loops' own time: 28.1 us -> 0 us
  Pallas kernels: 0 us -> 22.5 us
  starting transfers between devices: 33.4 us -> 21.2 us
    reduce_sum x16 -> x0, other arithmetic: 150 us -> none  [the longest x8 92.9 us: summed_force(): jnp.sum(kernel_weight * (target_particles[component][:, None, :, None] -...]
    scatter x1 -> x0, local copies, waits for them, and re-layouts: 42.8 us -> none  [pack_movers(): jnp.zeros((9, lane_total), jnp.float32).at[:, target_lane]]
    ppermute x12 -> x11, waiting for transfers between devices: 37.3 us -> 7.01 us  [swapped(): return lax.ppermute(block, 'cells', route)]
    another operation x2 -> x0, loops' own time: 28.1 us -> none  [the longest x1 14.1 us: cell_force_rows(): blocks = lax.map(one_block, starts)]
    pallas_call x0 -> x4, Pallas kernels: none -> 22.5 us  [the longest x1 18.4 us: per_device(): pl.pallas_call(state_kernel, out_shape=(jax.ShapeDtypeStruct((FIELDS, ROW...]
    ppermute x12 -> x11, starting transfers between devices: 33.4 us -> 21.2 us  [swapped(): return lax.ppermute(block, 'cells', route)]
    gather x24 -> x0, local copies, waits for them, and re-layouts: 10.9 us -> none  [one_block(): cell_particle_view[:, block_index_list]]
    dynamic_slice x24 -> x0, local copies, waits for them, and re-layouts: 9.48 us -> none  [the longest x16 9.38 us: cell_density_rows(): return lax.map(one_block, starts).reshape(-1)]
  transfers between devices with their start and end apart: 12 -> 11, of which waited for: 9 -> 4; matrix products, arithmetic and copies ran while one was open for 3% -> 0% of each run, Pallas kernels for 0% -> 3%
where the time goes in v2:
time: 53.2 us; the launch traced here: 52.4 us
  Pallas kernels  22.5 us (42%)
  starting transfers between devices  21.2 us (40%)
  waiting for transfers between devices  7.01 us (13%)
  local copies, waits for them, and re-layouts  1.68 us (3%)
    ppermute x11, starting transfers between devices, swapped(): return lax.ppermute(block, 'cells', route)  21.2 us
    pallas_call x1, Pallas kernels, per_device(): pl.pallas_call(state_kernel, out_shape=(jax.ShapeDtypeStruct((FIELDS, ROW...  18.4 us
    ppermute x11, waiting for transfers between devices, swapped(): return lax.ppermute(block, 'cells', route)  7.01 us
    unnamed x6, local copies, waits for them, and re-layouts  1.68 us
    pallas_call x1, Pallas kernels, per_device(): pl.pallas_call(edge_kernel, out_shape=(jax.ShapeDtypeStruct((HALO_ROWS, L...  1.63 us
    pallas_call x1, Pallas kernels, per_device(): pl.pallas_call(stay_kernel, out_shape=jax.ShapeDtypeStruct((FIELDS, RECV_...  1.44 us
  transfers between devices with their start and end apart: 11, of which 4 were waited for; matrix products, arithmetic and copies ran while one was open for 0% of the time, Pallas kernels for 3%

profile of v2, /device:TPU:1, one launch (start us, length us, event | category | flops | bytes accessed | tf_op | source)
XLA Modules:
  0.0 52.4 jit_solution(9498584990683011929)
XLA Ops:
  0.0 1.6 %shard_map.91 = (f32[96,128]{1,0:T(8,128)}, f32[96,128]{1,0:T(8,128)}) custom-call(s32[1]{0:T(128)} %bitcast.own_ref, f32[3,16384]{1,0:T(4,128)} %pos_ref.3, f32[128,128]{1,0:T(8,128)} %bitcast.8, f32[128,128]{1,0:T(8,128)} %bitcast.10, f32[128,128]{1,0:T(8,128)} %bitcast.12, s32[128,128]{1,0:T(8,128)} %bitcast.14, s32[6,64]{1,0:T(8,128)} %bitcast.18), custom_call_target="tpu_custom_call" | custom-call | tf_op jit(solution)/shard_map/pallas_call | solution.py:465
  1.6 3.1 %collective-permute-start = (f32[96,128]{1,0:T(8,128)}, f32[96,128]{1,0:T(8,128)S(1)}, u32[]{:S(2)}, u32[]{:S(2)}) collective-permute-start(f32[96,128]{1,0:T(8,128)} %get-tuple-element.13), channel_id=1, source_target_pairs={{1,2},{3,4},{5,6},{7,8},{9,10},{11,12},{13,14},{15,16},{17,18},{19... | collective-permute-start | bytes 147464 | tf_op jit(solution)/shard_map/ppermute | solution.py:440
  4.7 6.6 %collective-permute-start.1 = (f32[96,128]{1,0:T(8,128)}, f32[96,128]{1,0:T(8,128)S(1)}, u32[]{:S(2)}, u32[]{:S(2)}) collective-permute-start(f32[96,128]{1,0:T(8,128)} %get-tuple-element.14), channel_id=1, source_target_pairs={{0,1},{2,3},{4,5},{6,7},{8,9},{10,11},{12,13},{14,15},{16,17},{18,... | collective-permute-start | bytes 147464 | tf_op jit(solution)/shard_map/ppermute | solution.py:440
  11.3 0.0 collective-permute-done.far_ref
  11.4 0.0 copy-start.1
  11.4 1.1 %collective-permute-done.1.near_ref = f32[96,128]{1,0:T(8,128)S(1)} collective-permute-done((f32[96,128]{1,0:T(8,128)}, f32[96,128]{1,0:T(8,128)S(1)}, u32[]{:S(2)}, u32[]{:S(2)}) %collective-permute-start.1) | collective-permute-done | bytes 49184 | tf_op jit(solution)/shard_map/ppermute | solution.py:440
  12.4 0.0 copy-start.2
  12.4 0.0 copy-done.1
  12.4 0.6 %copy-done.2 = f32[96,128]{1,0:T(8,128)} copy-done((f32[96,128]{1,0:T(8,128)}, f32[96,128]{1,0:T(8,128)S(1)}, u32[]{:S(2)}) %copy-start.2) | copy-done | bytes 49176
  13.1 18.4 %shard_map.92 = (f32[9,128,128]{2,1,0:T(8,128)}, f32[2,9,8,128]{3,2,1,0:T(8,128)}, f32[2,9,8,128]{3,2,1,0:T(8,128)}, f32[2,9,8,128]{3,2,1,0:T(8,128)}, f32[2,9,8,128]{3,2,1,0:T(8,128)}, /*index=5*/f32[9,8,128]{2,1,0:T(8,128)}) custom-call(s32[1]{0:T(128)} %bitcast.own_ref, f32[3,16384]{1,0:T(4,128)} %pos_ref.3, f32[3,16384]{1,0:T(4,128)} %vel_ref.1, ...), custom_call_target="tpu_custom_call" | custom-call | tf_op jit(solution)/shard_map/pallas_call | solution.py:487
  31.5 0.1 collective-permute-start.2
  31.6 7.6 %collective-permute-start.3 = (f32[2,9,8,128]{3,2,1,0:T(8,128)}, f32[2,9,8,128]{3,2,1,0:T(8,128)S(1)}, u32[]{:S(2)}, u32[]{:S(2)}) collective-permute-start(f32[2,9,8,128]{3,2,1,0:T(8,128)} %get-tuple-element.16), channel_id=1, source_target_pairs={{2,4},{3,5},{6,8},{7,9},{10,12},{11,13},{14,16},{15,17},{18,20},{1... | collective-permute-start | bytes 221192 | tf_op jit(solution)/shard_map/ppermute | solution.py:440
  39.2 0.0 collective-permute-start.4
  39.2 1.1 %collective-permute-start.5 = (f32[2,9,8,128]{3,2,1,0:T(8,128)}, f32[2,9,8,128]{3,2,1,0:T(8,128)S(1)}, u32[]{:S(2)}, u32[]{:S(2)}) collective-permute-start(f32[2,9,8,128]{3,2,1,0:T(8,128)} %get-tuple-element.18), channel_id=1, source_target_pairs={{4,8},{5,9},{6,10},{7,11},{12,16},{13,17},{14,18},{15,19},{20,24},... | collective-permute-start | bytes 221192 | tf_op jit(solution)/shard_map/ppermute | solution.py:440
  40.3 0.0 collective-permute-done.2.next_ref
  40.3 0.0 collective-permute-start.7
  40.3 1.0 %collective-permute-done.3.next2_ref = f32[2,9,8,128]{3,2,1,0:T(8,128)S(1)} collective-permute-done((f32[2,9,8,128]{3,2,1,0:T(8,128)}, f32[2,9,8,128]{3,2,1,0:T(8,128)S(1)}, u32[]{:S(2)}, u32[]{:S(2)}) %collective-permute-start.3) | collective-permute-done | bytes 73760 | tf_op jit(solution)/shard_map/ppermute | solution.py:440
  41.3 2.1 %collective-permute-start.8 = (f32[2,9,8,128]{3,2,1,0:T(8,128)S(1)}, f32[2,9,8,128]{3,2,1,0:T(8,128)S(1)}, u32[]{:S(2)}, u32[]{:S(2)}) collective-permute-start(f32[2,9,8,128]{3,2,1,0:T(8,128)S(1)} %collective-permute-done.3.next2_ref), channel_id=1, source_target_pairs={{0,1},{2,3},{4,5},{6,7},{8,9},{10,11},{12,13},{14,15},{16,17},{18,... | collective-permute-start | bytes 221192 | tf_op jit(solution)/shard_map/ppermute | solution.py:440
  43.5 0.7 %collective-permute-done.4.far_ref = f32[2,9,8,128]{3,2,1,0:T(8,128)S(1)} collective-permute-done((f32[2,9,8,128]{3,2,1,0:T(8,128)}, f32[2,9,8,128]{3,2,1,0:T(8,128)S(1)}, u32[]{:S(2)}, u32[]{:S(2)}) %collective-permute-start.4) | collective-permute-done | bytes 73760 | tf_op jit(solution)/shard_map/ppermute | solution.py:440
  44.1 0.0 collective-permute-start.9
  44.1 4.2 %collective-permute-done.5.far2_ref = f32[2,9,8,128]{3,2,1,0:T(8,128)S(1)} collective-permute-done((f32[2,9,8,128]{3,2,1,0:T(8,128)}, f32[2,9,8,128]{3,2,1,0:T(8,128)S(1)}, u32[]{:S(2)}, u32[]{:S(2)}) %collective-permute-start.5) | collective-permute-done | bytes 73760 | tf_op jit(solution)/shard_map/ppermute | solution.py:440
  48.4 0.0 collective-permute-start.10
  48.4 0.5 collective-permute-start.6
  48.9 0.0 copy-start
  48.9 1.1 %copy-done = f32[9,128,128]{2,1,0:T(8,128)S(1)} copy-done((f32[9,128,128]{2,1,0:T(8,128)S(1)}, f32[9,128,128]{2,1,0:T(8,128)}, u32[]{:S(2)}) %copy-start) | copy-done | bytes 589848
  49.9 1.4 %shard_map.93.held_ref = f32[9,24576]{1,0:T(8,128)} custom-call(f32[9,128,128]{2,1,0:T(8,128)S(1)} %copy-done), custom_call_target="tpu_custom_call" | custom-call | tf_op jit(solution)/shard_map/pallas_call | solution.py:550
  51.4 0.0 collective-permute-done.6.other_ref
  51.4 0.0 collective-permute-done.7.x_next
  51.4 0.0 collective-permute-done.8.x_next2
  51.4 0.0 collective-permute-done.9.x_far
  51.4 0.0 collective-permute-done.10.x_far2
  51.4 1.0 %shard_map.94 = f32[9,24576]{1,0:T(8,128)} custom-call(s32[1]{0:T(128)} %bitcast.own_ref, f32[2,9,8,128]{3,2,1,0:T(8,128)S(1)} %collective-permute-done.2.next_ref, f32[2,9,8,128]{3,2,1,0:T(8,128)S(1)} %collective-permute-done.3.next2_ref, f32[2,9,8,128]{3,2,1,0:T(8,128)S(1)} %collective-permute-done.4.far_ref, ...), custom_call_target="tpu_custom_call", output_to_operand_aliasing={{}: (10, {})} | custom-call | tf_op jit(solution)/shard_map/pallas_call | solution.py:561
Async XLA Ops:
  1.6 9.7 %collective-permute-start = (f32[96,128]{1,0:T(8,128)}, f32[96,128]{1,0:T(8,128)S(1)}, u32[]{:S(2)}, u32[]{:S(2)}) collective-permute-start(f32[96,128]{1,0:T(8,128)} %get-tuple-element.13), channel_id=1, source_target_pairs={{1,2},{3,4},{5,6},{7,8},{9,10},{11,12},{13,14},{15,16},{17,18},{19... | collective-permute-start | bytes 147464 | tf_op jit(solution)/shard_map/ppermute | solution.py:440
  4.7 7.7 %collective-permute-start.1 = (f32[96,128]{1,0:T(8,128)}, f32[96,128]{1,0:T(8,128)S(1)}, u32[]{:S(2)}, u32[]{:S(2)}) collective-permute-start(f32[96,128]{1,0:T(8,128)} %get-tuple-element.14), channel_id=1, source_target_pairs={{0,1},{2,3},{4,5},{6,7},{8,9},{10,11},{12,13},{14,15},{16,17},{18,... | collective-permute-start | bytes 147464 | tf_op jit(solution)/shard_map/ppermute | solution.py:440
  11.4 1.1 %copy-start.1 = (f32[96,128]{1,0:T(8,128)}, f32[96,128]{1,0:T(8,128)S(1)}, u32[]{:S(2)}) copy-start(f32[96,128]{1,0:T(8,128)S(1)} %collective-permute-done.far_ref) | copy-start | bytes 147460
  12.4 0.6 %copy-start.2 = (f32[96,128]{1,0:T(8,128)}, f32[96,128]{1,0:T(8,128)S(1)}, u32[]{:S(2)}) copy-start(f32[96,128]{1,0:T(8,128)S(1)} %collective-permute-done.1.near_ref) | copy-start | bytes 147460
  31.5 8.8 %collective-permute-start.2 = (f32[2,9,8,128]{3,2,1,0:T(8,128)}, f32[2,9,8,128]{3,2,1,0:T(8,128)S(1)}, u32[]{:S(2)}, u32[]{:S(2)}) collective-permute-start(f32[2,9,8,128]{3,2,1,0:T(8,128)} %get-tuple-element.15), channel_id=1, source_target_pairs={{0,2},{1,3},{4,6},{5,7},{8,10},{9,11},{12,14},{13,15},{16,18},{17,... | collective-permute-start | bytes 221192 | tf_op jit(solution)/shard_map/ppermute | solution.py:440
  31.6 9.7 %collective-permute-start.3 = (f32[2,9,8,128]{3,2,1,0:T(8,128)}, f32[2,9,8,128]{3,2,1,0:T(8,128)S(1)}, u32[]{:S(2)}, u32[]{:S(2)}) collective-permute-start(f32[2,9,8,128]{3,2,1,0:T(8,128)} %get-tuple-element.16), channel_id=1, source_target_pairs={{2,4},{3,5},{6,8},{7,9},{10,12},{11,13},{14,16},{15,17},{18,20},{1... | collective-permute-start | bytes 221192 | tf_op jit(solution)/shard_map/ppermute | solution.py:440
  39.2 4.9 %collective-permute-start.4 = (f32[2,9,8,128]{3,2,1,0:T(8,128)}, f32[2,9,8,128]{3,2,1,0:T(8,128)S(1)}, u32[]{:S(2)}, u32[]{:S(2)}) collective-permute-start(f32[2,9,8,128]{3,2,1,0:T(8,128)} %get-tuple-element.17), channel_id=1, source_target_pairs={{0,4},{1,5},{2,6},{3,7},{8,12},{9,13},{10,14},{11,15},{16,20},{17,... | collective-permute-start | bytes 221192 | tf_op jit(solution)/shard_map/ppermute | solution.py:440
  39.2 9.1 %collective-permute-start.5 = (f32[2,9,8,128]{3,2,1,0:T(8,128)}, f32[2,9,8,128]{3,2,1,0:T(8,128)S(1)}, u32[]{:S(2)}, u32[]{:S(2)}) collective-permute-start(f32[2,9,8,128]{3,2,1,0:T(8,128)} %get-tuple-element.18), channel_id=1, source_target_pairs={{4,8},{5,9},{6,10},{7,11},{12,16},{13,17},{14,18},{15,19},{20,24},... | collective-permute-start | bytes 221192 | tf_op jit(solution)/shard_map/ppermute | solution.py:440
  40.3 11.1 %collective-permute-start.7 = (f32[2,9,8,128]{3,2,1,0:T(8,128)S(1)}, f32[2,9,8,128]{3,2,1,0:T(8,128)S(1)}, u32[]{:S(2)}, u32[]{:S(2)}) collective-permute-start(f32[2,9,8,128]{3,2,1,0:T(8,128)S(1)} %collective-permute-done.2.next_ref), channel_id=1, source_target_pairs={{0,1},{2,3},{4,5},{6,7},{8,9},{10,11},{12,13},{14,15},{16,17},{18,... | collective-permute-start | bytes 221192 | tf_op jit(solution)/shard_map/ppermute | solution.py:440
  41.3 10.1 %collective-permute-start.8 = (f32[2,9,8,128]{3,2,1,0:T(8,128)S(1)}, f32[2,9,8,128]{3,2,1,0:T(8,128)S(1)}, u32[]{:S(2)}, u32[]{:S(2)}) collective-permute-start(f32[2,9,8,128]{3,2,1,0:T(8,128)S(1)} %collective-permute-done.3.next2_ref), channel_id=1, source_target_pairs={{0,1},{2,3},{4,5},{6,7},{8,9},{10,11},{12,13},{14,15},{16,17},{18,... | collective-permute-start | bytes 221192 | tf_op jit(solution)/shard_map/ppermute | solution.py:440
  44.1 7.3 %collective-permute-start.9 = (f32[2,9,8,128]{3,2,1,0:T(8,128)S(1)}, f32[2,9,8,128]{3,2,1,0:T(8,128)S(1)}, u32[]{:S(2)}, u32[]{:S(2)}) collective-permute-start(f32[2,9,8,128]{3,2,1,0:T(8,128)S(1)} %collective-permute-done.4.far_ref), channel_id=1, source_target_pairs={{0,1},{2,3},{4,5},{6,7},{8,9},{10,11},{12,13},{14,15},{16,17},{18,... | collective-permute-start | bytes 221192 | tf_op jit(solution)/shard_map/ppermute | solution.py:440
  48.4 3.1 %collective-permute-start.10 = (f32[2,9,8,128]{3,2,1,0:T(8,128)S(1)}, f32[2,9,8,128]{3,2,1,0:T(8,128)S(1)}, u32[]{:S(2)}, u32[]{:S(2)}) collective-permute-start(f32[2,9,8,128]{3,2,1,0:T(8,128)S(1)} %collective-permute-done.5.far2_ref), channel_id=1, source_target_pairs={{0,1},{2,3},{4,5},{6,7},{8,9},{10,11},{12,13},{14,15},{16,17},{18,... | collective-permute-start | bytes 221192 | tf_op jit(solution)/shard_map/ppermute | solution.py:440
  48.4 3.0 %collective-permute-start.6 = (f32[9,8,128]{2,1,0:T(8,128)}, f32[9,8,128]{2,1,0:T(8,128)S(1)}, u32[]{:S(2)}, u32[]{:S(2)}) collective-permute-start(f32[9,8,128]{2,1,0:T(8,128)} %get-tuple-element.19), channel_id=1, source_target_pairs={{0,1},{2,3},{4,5},{6,7},{8,9},{10,11},{12,13},{14,15},{16,17},{18,... | collective-permute-start | bytes 110600 | tf_op jit(solution)/shard_map/ppermute | solution.py:440
  48.9 1.1 %copy-start = (f32[9,128,128]{2,1,0:T(8,128)S(1)}, f32[9,128,128]{2,1,0:T(8,128)}, u32[]{:S(2)}) copy-start(f32[9,128,128]{2,1,0:T(8,128)} %get-tuple-element.20.kept_ref) | copy-start | bytes 1769476

commit v3 on v2

--- a/solution.py
+++ b/solution.py
@@ -27,7 +27,7 @@
 OWN = slice(EDGE_ROWS, EDGE_ROWS + ROWS)
 PACK_ROWS = 8
 DUMMY = EDGE * 64 + 32 + (8 << 20)
-UNROLL = 8
+UNROLL = 16
 LIST_SIZE = LISTED * 32 + 64
 GROUPS = 2 * REACH
 time_step = 0.25
@@ -80,48 +80,43 @@
 
 def state_kernel(
     own_ref, pos_ref, vel_ref, mass_ref, ent_ref, rho_ref, act_ref, dest_ref, slot_ref,
-    nbr_ref, far_ref, near_ref,
+    nbr_ref, far_in, near_in,
     kept_ref, to_far, to_far2, to_next, to_next2, to_other,
     pos_v, vel_v, act_v, dest_v, slot_v, nbr_v,
     xs, ys, zs, ms, ps, es, rho_old, rank, dens, ax, ay, az,
     fields, key, shifts, parts, hi_row, lo_row, a0, b0, packed, blocks,
-    table_v, table, chunk_list, sem,
+    far_ref, near_ref, table_v, table, chunk_list, sem,
 ):
     own = own_ref[0]
     even = own % 2 == 0
     scale = 8.0 / (NEIGHBOURS * CELL_PARTICLES)
     loads = [
+        (act_ref, act_v),
+        (nbr_ref, nbr_v),
+        (far_in, far_ref),
+        (near_in, near_ref),
+        (dest_ref, dest_v),
+        (slot_ref, slot_v),
+        (rho_ref, rho_old.at[pl.ds(EDGE_ROWS, ROWS)]),
+        (mass_ref, ms.at[pl.ds(EDGE_ROWS, ROWS)]),
+        (ent_ref, es.at[pl.ds(EDGE_ROWS, ROWS)]),
         (pos_ref, pos_v),
         (vel_ref, vel_v),
-        (mass_ref, ms.at[pl.ds(EDGE_ROWS, ROWS)]),
-        (ent_ref, es.at[pl.ds(EDGE_ROWS, ROWS)]),
-        (rho_ref, rho_old.at[pl.ds(EDGE_ROWS, ROWS)]),
-        (act_ref, act_v),
-        (dest_ref, dest_v),
-        (slot_ref, slot_v),
-        (nbr_ref, nbr_v),
     ]
     loads = [pltpu.make_async_copy(a, b, sem.at[k]) for k, (a, b) in enumerate(loads)]
     for copy in loads:
         copy.start()
+    for ref in (dens, ax, ay, az, packed):
+        ref[...] = jnp.zeros_like(ref)
+    for copy in loads[:4]:
+        copy.wait()
 
     def side_rows(first, last):
         f, n = far_ref[first:last, :], near_ref[first:last, :]
         return jnp.where(even, f, n), jnp.where(even, n, f)
 
-    high = slice(EDGE_ROWS + ROWS, EXT_ROWS)
-    for k, ref in enumerate((xs, ys, zs, ms)):
-        ref[0:EDGE_ROWS, :], ref[high, :] = side_rows(16 * k, 16 * k + 16)
     zeros8 = jnp.zeros((8, LANES), jnp.float32)
     ghost_act = side_rows(80, 88)
-    for ref, rows, fill in ((es, (64, 72), 0.0), (rho_old, (72, 80), 1.0)):
-        ref[0:8, :] = zeros8 + fill
-        ref[EXT_ROWS - 8 :, :] = zeros8 + fill
-        ref[8:16, :], ref[EXT_ROWS - 16 : EXT_ROWS - 8, :] = side_rows(*rows)
-    for ref in (dens, ax, ay, az, packed):
-        ref[...] = jnp.zeros_like(ref)
-    for copy in loads:
-        copy.wait()
 
     act = jnp.concatenate(
         [zeros8, ghost_act[0], (act_v[...] == 1).astype(jnp.float32), ghost_act[1], zeros8],
@@ -136,7 +131,10 @@
     in_lanes = lax.dot_general(
         ones[0:16], act16, (((1,), (1,)), ((), ())), preferred_element_type=jnp.float32
     )
-    table_v[0:8, 0:EXT_ROWS] = in_lanes[0:8].astype(jnp.int32)
+    halves = lax.broadcasted_iota(jnp.int32, (EXT_ROWS, LANES), 0) >> 1
+    joined = (halves == lax.broadcasted_iota(jnp.int32, (EXT_ROWS, LANES), 1)).astype(jnp.bfloat16)
+    in_cells = jnp.dot(in_lanes.astype(jnp.bfloat16), joined, preferred_element_type=jnp.float32)
+    table_v[0:8, :] = in_cells[0:8].astype(jnp.int32)
     shift = own * CELLS_DEV - EDGE
     near_lists = side_rows(88, 96)
     pad = jnp.zeros((8 - NEIGHBOURS, CELLS_DEV), jnp.int32)
@@ -145,14 +143,24 @@
         table_v[16 + 8 * k : 24 + 8 * k, 0:LANES] = (
             near_lists[k].astype(jnp.int32) - shift
         ) & 8191
-    table_copy = pltpu.make_async_copy(table_v, table, sem.at[9])
+    table_copy = pltpu.make_async_copy(table_v, table, sem.at[11])
     table_copy.start()
+    high = slice(EDGE_ROWS + ROWS, EXT_ROWS)
+    for k, ref in enumerate((xs, ys, zs, ms)):
+        ref[0:EDGE_ROWS, :], ref[high, :] = side_rows(16 * k, 16 * k + 16)
+    for ref, rows, fill in ((es, (64, 72), 0.0), (rho_old, (72, 80), 1.0)):
+        ref[0:8, :] = zeros8 + fill
+        ref[EXT_ROWS - 8 :, :] = zeros8 + fill
+        ref[8:16, :], ref[EXT_ROWS - 16 : EXT_ROWS - 8, :] = side_rows(*rows)
     inside = jnp.dot(act16, before, preferred_element_type=jnp.float32)
     total = jnp.dot(act16, ones, preferred_element_type=jnp.float32)
     row_id = lax.broadcasted_iota(jnp.int32, (EXT_ROWS, LANES), 0)
     rank[...] = jnp.where(
         act > 0.5, inside + jnp.where(row_id % 2 == 1, pltpu.roll(total, 1, 0), 0.0), -1.0
     )
+
+    for copy in loads[4:]:
+        copy.wait()
 
     dest = dest_v[...]
     away = (dest - own) & 127
@@ -209,7 +217,7 @@
     cells += [(EDGE + CELLS_DEV + k, k, 24) for k in range(GHOST)]
     at, most, own_total = 0, 0, 0
     for number, (cell, lane, row) in enumerate(cells):
-        n = table[0, 2 * cell] + table[0, 2 * cell + 1]
+        n = table[0, cell]
         code = (row << 20) + (lane << 13) + (cell << 6)
         for k in range(4):
             chunk_list[at + k] = code + k
@@ -224,7 +232,7 @@
         def refill(first, count, lane0, row):
             def one(k, start):
                 cell = first + k
-                n = table[0, 2 * cell] + table[0, 2 * cell + 1]
+                n = table[0, cell]
                 code = (row << 20) + ((lane0 + k) << 13) + (cell << 6)
 
                 def put(j, carry):
@@ -390,11 +398,15 @@
     return jnp.minimum(jnp.maximum(g, 0), GROUPS - 1)
 
 
-def stay_kernel(kept_ref, out_ref, rows, sem):
+def stay_kernel(kept_ref, out_ref, kept_v, rows, sem):
+    load = pltpu.make_async_copy(kept_ref, kept_v, sem.at[1])
+    load.start()
+    load.wait()
+
     def step(i, carry):
         col = pl.multiple_of(i * LANES, LANES)
         for v in range(FIELDS):
-            rows[v : v + 1, pl.ds(col, LANES)] = kept_ref[v, pl.ds(i, 1), :]
+            rows[v : v + 1, pl.ds(col, LANES)] = kept_v[v, pl.ds(i, 1), :]
         return carry
 
     lax.fori_loop(0, ROWS, step, 0, unroll=8)
@@ -473,7 +485,7 @@
             pltpu.VMEM((NEIGHBOURS, CELLS_DEV), i32),
             pltpu.SemaphoreType.DMA((11,)),
         ],
-        compiler_params=pltpu.CompilerParams(vmem_limit_bytes=56 * 2**20),
+        compiler_params=pltpu.CompilerParams(vmem_limit_bytes=64 * 2**20),
     )(own, position, mass, ent, rho, act, lists)
     near_pairs = [(2 * k, 2 * k + 1) for k in range(count // 2)]
     far_pairs = [(2 * k + 1, (2 * k + 2) % count) for k in range(count // 2)]
@@ -494,7 +506,7 @@
             pair,
             jax.ShapeDtypeStruct((FIELDS, 8, LANES), f32),
         ),
-        in_specs=[sm] + [hbm] * 9 + [vm] * 2,
+        in_specs=[sm] + [hbm] * 11,
         out_specs=(vm,) * 6,
         scratch_shapes=[flat, flat, whole, whole, whole]
         + [pltpu.VMEM((NEIGHBOURS, CELLS_DEV), i32)]
@@ -510,12 +522,14 @@
             pltpu.VMEM((256, PACK_ROWS * LANES), jnp.bfloat16),
             pltpu.VMEM((64 * FIELDS, 256), f32),
             pltpu.VMEM((GROUPS, FIELDS, 8, LANES), f32),
-            pltpu.VMEM((32, 256), i32),
-            pltpu.SMEM((32, 256), i32),
+            pltpu.VMEM((HALO_ROWS, LANES), f32),
+            pltpu.VMEM((HALO_ROWS, LANES), f32),
+            pltpu.VMEM((32, LANES), i32),
+            pltpu.SMEM((32, LANES), i32),
             pltpu.SMEM((LIST_SIZE,), i32),
-            pltpu.SemaphoreType.DMA((10,)),
+            pltpu.SemaphoreType.DMA((12,)),
         ],
-        compiler_params=pltpu.CompilerParams(vmem_limit_bytes=56 * 2**20),
+        compiler_params=pltpu.CompilerParams(vmem_limit_bytes=64 * 2**20),
     )(
         own,
         position,
@@ -546,18 +560,23 @@
     far2 = swapped(to_far2, chip_pairs(2, 1))
     next1 = swapped(to_next, chip_pairs(1, 0))
     far1 = swapped(to_far, chip_pairs(2, 0))
-    crossed = [swapped(x, near_pairs) for x in (next1, next2, far1, far2)]
     held = pl.pallas_call(
         stay_kernel,
         out_shape=jax.ShapeDtypeStruct((FIELDS, RECV_DEV), f32),
-        in_specs=[vm],
+        in_specs=[hbm],
         out_specs=hbm,
         scratch_shapes=[
+            pltpu.VMEM((FIELDS, ROWS, LANES), f32),
             pltpu.VMEM((FIELDS, PART_DEV), f32),
-            pltpu.SemaphoreType.DMA((1,)),
+            pltpu.SemaphoreType.DMA((2,)),
         ],
-        compiler_params=pltpu.CompilerParams(vmem_limit_bytes=16 * 2**20),
+        compiler_params=pltpu.CompilerParams(vmem_limit_bytes=64 * 2**20),
+        cost_estimate=pl.CostEstimate(
+            flops=4 * 2**20, bytes_accessed=4 * 2**20, transcendentals=0
+        ),
     )(kept)
+    next1, held = lax.optimization_barrier((next1, held))
+    crossed = [swapped(x, near_pairs) for x in (next1, next2, far1, far2)]
     return pl.pallas_call(
         assemble_kernel,
         out_shape=jax.ShapeDtypeStruct((FIELDS, RECV_DEV), f32),

time: 53.2 us -> 50.2 us (0.944)
  starting transfers between devices: 21.2 us -> 19.4 us
  local copies, waits for them, and re-layouts: 1.68 us -> 0 us
  waiting for transfers between devices: 7.01 us -> 8 us
    pallas_call x1, Pallas kernels: 18.4 us -> 16.3 us  [per_device(): pl.pallas_call(state_kernel, out_shape=(jax.ShapeDtypeStruct((FIELDS, ROW...]
    ppermute x11, starting transfers between devices: 21.2 us -> 19.4 us  [swapped(): return lax.ppermute(block, 'cells', route)]
    unnamed x6 -> x0, local copies, waits for them, and re-layouts: 1.68 us -> none
    pallas_call x1, Pallas kernels: 1.44 us -> 2.51 us  [per_device(): pl.pallas_call(stay_kernel, out_shape=jax.ShapeDtypeStruct((FIELDS, RECV_...]
    pallas_call x1, Pallas kernels: 0.99 us -> 1.98 us  [per_device(): pl.pallas_call(assemble_kernel, out_shape=jax.ShapeDtypeStruct((FIELDS, R...]
    ppermute x11, waiting for transfers between devices: 7.01 us -> 8 us  [swapped(): return lax.ppermute(block, 'cells', route)]
  transfers between devices with their start and end apart: 11 -> 11, of which waited for: 4 -> 4; matrix products, arithmetic and copies ran while one was open for 0% -> 0% of each run, Pallas kernels for 3% -> 5%
where the time goes in v3:
time: 50.2 us; the launch traced here: 49.9 us
  Pallas kernels  22.4 us (45%)
  starting transfers between devices  19.4 us (39%)
  waiting for transfers between devices  8 us (16%)
    ppermute x11, starting transfers between devices, swapped(): return lax.ppermute(block, 'cells', route)  19.4 us
    pallas_call x1, Pallas kernels, per_device(): pl.pallas_call(state_kernel, out_shape=(jax.ShapeDtypeStruct((FIELDS, ROW...  16.3 us
    ppermute x11, waiting for transfers between devices, swapped(): return lax.ppermute(block, 'cells', route)  8 us
    pallas_call x1, Pallas kernels, per_device(): pl.pallas_call(stay_kernel, out_shape=jax.ShapeDtypeStruct((FIELDS, RECV_...  2.51 us
    pallas_call x1, Pallas kernels, per_device(): pl.pallas_call(assemble_kernel, out_shape=jax.ShapeDtypeStruct((FIELDS, R...  1.98 us
    pallas_call x1, Pallas kernels, per_device(): pl.pallas_call(edge_kernel, out_shape=(jax.ShapeDtypeStruct((HALO_ROWS, L...  1.63 us
  transfers between devices with their start and end apart: 11, of which 4 were waited for; matrix products, arithmetic and copies ran while one was open for 0% of the time, Pallas kernels for 5%

profile of v3, /device:TPU:1, one launch (start us, length us, event | category | flops | bytes accessed | tf_op | source)
XLA Modules:
  0.0 49.9 jit_solution(7274087106877907777)
XLA Ops:
  0.0 1.6 %shard_map.91 = (f32[96,128]{1,0:T(8,128)}, f32[96,128]{1,0:T(8,128)}) custom-call(s32[1]{0:T(128)} %bitcast.own_ref, f32[3,16384]{1,0:T(4,128)} %pos_ref.3, f32[128,128]{1,0:T(8,128)} %bitcast.8, f32[128,128]{1,0:T(8,128)} %bitcast.10, f32[128,128]{1,0:T(8,128)} %bitcast.12, s32[128,128]{1,0:T(8,128)} %bitcast.14, s32[6,64]{1,0:T(8,128)} %bitcast.18), custom_call_target="tpu_custom_call" | custom-call | tf_op jit(solution)/shard_map/pallas_call | solution.py:477
  1.6 3.1 %collective-permute-start = (f32[96,128]{1,0:T(8,128)}, f32[96,128]{1,0:T(8,128)}, u32[]{:S(2)}, u32[]{:S(2)}) collective-permute-start(f32[96,128]{1,0:T(8,128)} %get-tuple-element.15), channel_id=1, source_target_pairs={{1,2},{3,4},{5,6},{7,8},{9,10},{11,12},{13,14},{15,16},{17,18},{19... | collective-permute-start | bytes 147464 | tf_op jit(solution)/shard_map/ppermute | solution.py:452
  4.7 6.6 %collective-permute-start.1 = (f32[96,128]{1,0:T(8,128)}, f32[96,128]{1,0:T(8,128)}, u32[]{:S(2)}, u32[]{:S(2)}) collective-permute-start(f32[96,128]{1,0:T(8,128)} %get-tuple-element.16), channel_id=1, source_target_pairs={{0,1},{2,3},{4,5},{6,7},{8,9},{10,11},{12,13},{14,15},{16,17},{18,... | collective-permute-start | bytes 147464 | tf_op jit(solution)/shard_map/ppermute | solution.py:452
  11.3 0.0 collective-permute-done.far_in
  11.3 1.2 %collective-permute-done.1.near_in = f32[96,128]{1,0:T(8,128)} collective-permute-done((f32[96,128]{1,0:T(8,128)}, f32[96,128]{1,0:T(8,128)}, u32[]{:S(2)}, u32[]{:S(2)}) %collective-permute-start.1) | collective-permute-done | bytes 49184 | tf_op jit(solution)/shard_map/ppermute | solution.py:452
  12.6 16.3 %shard_map.92 = (f32[9,128,128]{2,1,0:T(8,128)}, f32[2,9,8,128]{3,2,1,0:T(8,128)}, f32[2,9,8,128]{3,2,1,0:T(8,128)}, f32[2,9,8,128]{3,2,1,0:T(8,128)}, f32[2,9,8,128]{3,2,1,0:T(8,128)}, /*index=5*/f32[9,8,128]{2,1,0:T(8,128)}) custom-call(s32[1]{0:T(128)} %bitcast.own_ref, f32[3,16384]{1,0:T(4,128)} %pos_ref.3, f32[3,16384]{1,0:T(4,128)} %vel_ref.1, ...), custom_call_target="tpu_custom_call" | custom-call | tf_op jit(solution)/shard_map/pallas_call | solution.py:499
  28.9 0.1 collective-permute-start.2
  29.0 7.7 %collective-permute-start.3 = (f32[2,9,8,128]{3,2,1,0:T(8,128)}, f32[2,9,8,128]{3,2,1,0:T(8,128)}, u32[]{:S(2)}, u32[]{:S(2)}) collective-permute-start(f32[2,9,8,128]{3,2,1,0:T(8,128)} %get-tuple-element.20), channel_id=1, source_target_pairs={{2,4},{3,5},{6,8},{7,9},{10,12},{11,13},{14,16},{15,17},{18,20},{1... | collective-permute-start | bytes 221192 | tf_op jit(solution)/shard_map/ppermute | solution.py:452
  36.7 0.0 collective-permute-start.4
  36.7 1.1 %collective-permute-start.5 = (f32[2,9,8,128]{3,2,1,0:T(8,128)}, f32[2,9,8,128]{3,2,1,0:T(8,128)}, u32[]{:S(2)}, u32[]{:S(2)}) collective-permute-start(f32[2,9,8,128]{3,2,1,0:T(8,128)} %get-tuple-element.22), channel_id=1, source_target_pairs={{4,8},{5,9},{6,10},{7,11},{12,16},{13,17},{14,18},{15,19},{20,24},... | collective-permute-start | bytes 221192 | tf_op jit(solution)/shard_map/ppermute | solution.py:452
  37.8 2.5 %shard_map.93.held_ref = f32[9,24576]{1,0:T(8,128)} custom-call(f32[9,128,128]{2,1,0:T(8,128)} %get-tuple-element.18.kept_ref), custom_call_target="tpu_custom_call" | custom-call | flops 4194304 | bytes 4194304 | tf_op jit(solution)/shard_map/pallas_call | solution.py:563
  40.3 0.0 collective-permute-done.2.next_ref
  40.3 0.0 collective-permute-done.3.next2_ref
  40.3 0.3 collective-permute-start.8
  40.6 1.1 %collective-permute-done.4.far_ref = f32[2,9,8,128]{3,2,1,0:T(8,128)} collective-permute-done((f32[2,9,8,128]{3,2,1,0:T(8,128)}, f32[2,9,8,128]{3,2,1,0:T(8,128)}, u32[]{:S(2)}, u32[]{:S(2)}) %collective-permute-start.4) | collective-permute-done | bytes 73760 | tf_op jit(solution)/shard_map/ppermute | solution.py:452
  41.7 0.0 collective-permute-start.9
  41.7 4.2 %collective-permute-done.5.far2_ref = f32[2,9,8,128]{3,2,1,0:T(8,128)} collective-permute-done((f32[2,9,8,128]{3,2,1,0:T(8,128)}, f32[2,9,8,128]{3,2,1,0:T(8,128)}, u32[]{:S(2)}, u32[]{:S(2)}) %collective-permute-start.5) | collective-permute-done | bytes 73760 | tf_op jit(solution)/shard_map/ppermute | solution.py:452
  45.9 0.0 collective-permute-start.10
  45.9 0.5 %collective-permute-start.7 = (f32[2,9,8,128]{3,2,1,0:T(8,128)}, f32[2,9,8,128]{3,2,1,0:T(8,128)S(1)}, u32[]{:S(2)}, u32[]{:S(2)}) collective-permute-start(f32[2,9,8,128]{3,2,1,0:T(8,128)} %collective-permute-done.2.next_ref), channel_id=1, source_target_pairs={{0,1},{2,3},{4,5},{6,7},{8,9},{10,11},{12,13},{14,15},{16,17},{18,... | collective-permute-start | bytes 221192 | tf_op jit(solution)/shard_map/ppermute | solution.py:452
  46.4 0.0 collective-permute-start.6
  46.4 1.4 %collective-permute-done.6.other_ref = f32[9,8,128]{2,1,0:T(8,128)S(1)} collective-permute-done((f32[9,8,128]{2,1,0:T(8,128)}, f32[9,8,128]{2,1,0:T(8,128)S(1)}, u32[]{:S(2)}, u32[]{:S(2)}) %collective-permute-start.6) | collective-permute-done | bytes 36896 | tf_op jit(solution)/shard_map/ppermute | solution.py:452
  47.9 0.0 collective-permute-done.8.x_next2
  47.9 0.0 collective-permute-done.9.x_far
  47.9 0.0 collective-permute-done.10.x_far2
  47.9 0.0 collective-permute-done.7.x_next
  47.9 2.0 %shard_map.94 = f32[9,24576]{1,0:T(8,128)} custom-call(s32[1]{0:T(128)} %bitcast.own_ref, f32[2,9,8,128]{3,2,1,0:T(8,128)} %collective-permute-done.2.next_ref, f32[2,9,8,128]{3,2,1,0:T(8,128)} %collective-permute-done.3.next2_ref, f32[2,9,8,128]{3,2,1,0:T(8,128)} %collective-permute-done.4.far_ref, ...), custom_call_target="tpu_custom_call", output_to_operand_aliasing={{}: (10, {})} | custom-call | tf_op jit(solution)/shard_map/pallas_call | solution.py:580
Async XLA Ops:
  1.6 9.7 %collective-permute-start = (f32[96,128]{1,0:T(8,128)}, f32[96,128]{1,0:T(8,128)}, u32[]{:S(2)}, u32[]{:S(2)}) collective-permute-start(f32[96,128]{1,0:T(8,128)} %get-tuple-element.15), channel_id=1, source_target_pairs={{1,2},{3,4},{5,6},{7,8},{9,10},{11,12},{13,14},{15,16},{17,18},{19... | collective-permute-start | bytes 147464 | tf_op jit(solution)/shard_map/ppermute | solution.py:452
  4.7 7.8 %collective-permute-start.1 = (f32[96,128]{1,0:T(8,128)}, f32[96,128]{1,0:T(8,128)}, u32[]{:S(2)}, u32[]{:S(2)}) collective-permute-start(f32[96,128]{1,0:T(8,128)} %get-tuple-element.16), channel_id=1, source_target_pairs={{0,1},{2,3},{4,5},{6,7},{8,9},{10,11},{12,13},{14,15},{16,17},{18,... | collective-permute-start | bytes 147464 | tf_op jit(solution)/shard_map/ppermute | solution.py:452
  28.9 11.4 %collective-permute-start.2 = (f32[2,9,8,128]{3,2,1,0:T(8,128)}, f32[2,9,8,128]{3,2,1,0:T(8,128)}, u32[]{:S(2)}, u32[]{:S(2)}) collective-permute-start(f32[2,9,8,128]{3,2,1,0:T(8,128)} %get-tuple-element.17), channel_id=1, source_target_pairs={{0,2},{1,3},{4,6},{5,7},{8,10},{9,11},{12,14},{13,15},{16,18},{17,... | collective-permute-start | bytes 221192 | tf_op jit(solution)/shard_map/ppermute | solution.py:452
  29.0 11.3 %collective-permute-start.3 = (f32[2,9,8,128]{3,2,1,0:T(8,128)}, f32[2,9,8,128]{3,2,1,0:T(8,128)}, u32[]{:S(2)}, u32[]{:S(2)}) collective-permute-start(f32[2,9,8,128]{3,2,1,0:T(8,128)} %get-tuple-element.20), channel_id=1, source_target_pairs={{2,4},{3,5},{6,8},{7,9},{10,12},{11,13},{14,16},{15,17},{18,20},{1... | collective-permute-start | bytes 221192 | tf_op jit(solution)/shard_map/ppermute | solution.py:452
  36.7 5.0 %collective-permute-start.4 = (f32[2,9,8,128]{3,2,1,0:T(8,128)}, f32[2,9,8,128]{3,2,1,0:T(8,128)}, u32[]{:S(2)}, u32[]{:S(2)}) collective-permute-start(f32[2,9,8,128]{3,2,1,0:T(8,128)} %get-tuple-element.21), channel_id=1, source_target_pairs={{0,4},{1,5},{2,6},{3,7},{8,12},{9,13},{10,14},{11,15},{16,20},{17,... | collective-permute-start | bytes 221192 | tf_op jit(solution)/shard_map/ppermute | solution.py:452
  36.7 9.2 %collective-permute-start.5 = (f32[2,9,8,128]{3,2,1,0:T(8,128)}, f32[2,9,8,128]{3,2,1,0:T(8,128)}, u32[]{:S(2)}, u32[]{:S(2)}) collective-permute-start(f32[2,9,8,128]{3,2,1,0:T(8,128)} %get-tuple-element.22), channel_id=1, source_target_pairs={{4,8},{5,9},{6,10},{7,11},{12,16},{13,17},{14,18},{15,19},{20,24},... | collective-permute-start | bytes 221192 | tf_op jit(solution)/shard_map/ppermute | solution.py:452
  40.3 7.6 %collective-permute-start.8 = (f32[2,9,8,128]{3,2,1,0:T(8,128)}, f32[2,9,8,128]{3,2,1,0:T(8,128)S(1)}, u32[]{:S(2)}, u32[]{:S(2)}) collective-permute-start(f32[2,9,8,128]{3,2,1,0:T(8,128)} %collective-permute-done.3.next2_ref), channel_id=1, source_target_pairs={{0,1},{2,3},{4,5},{6,7},{8,9},{10,11},{12,13},{14,15},{16,17},{18,... | collective-permute-start | bytes 221192 | tf_op jit(solution)/shard_map/ppermute | solution.py:452
  41.7 6.2 %collective-permute-start.9 = (f32[2,9,8,128]{3,2,1,0:T(8,128)}, f32[2,9,8,128]{3,2,1,0:T(8,128)S(1)}, u32[]{:S(2)}, u32[]{:S(2)}) collective-permute-start(f32[2,9,8,128]{3,2,1,0:T(8,128)} %collective-permute-done.4.far_ref), channel_id=1, source_target_pairs={{0,1},{2,3},{4,5},{6,7},{8,9},{10,11},{12,13},{14,15},{16,17},{18,... | collective-permute-start | bytes 221192 | tf_op jit(solution)/shard_map/ppermute | solution.py:452
  45.9 1.9 %collective-permute-start.10 = (f32[2,9,8,128]{3,2,1,0:T(8,128)}, f32[2,9,8,128]{3,2,1,0:T(8,128)S(1)}, u32[]{:S(2)}, u32[]{:S(2)}) collective-permute-start(f32[2,9,8,128]{3,2,1,0:T(8,128)} %collective-permute-done.5.far2_ref), channel_id=1, source_target_pairs={{0,1},{2,3},{4,5},{6,7},{8,9},{10,11},{12,13},{14,15},{16,17},{18,... | collective-permute-start | bytes 221192 | tf_op jit(solution)/shard_map/ppermute | solution.py:452
  45.9 1.9 %collective-permute-start.7 = (f32[2,9,8,128]{3,2,1,0:T(8,128)}, f32[2,9,8,128]{3,2,1,0:T(8,128)S(1)}, u32[]{:S(2)}, u32[]{:S(2)}) collective-permute-start(f32[2,9,8,128]{3,2,1,0:T(8,128)} %collective-permute-done.2.next_ref), channel_id=1, source_target_pairs={{0,1},{2,3},{4,5},{6,7},{8,9},{10,11},{12,13},{14,15},{16,17},{18,... | collective-permute-start | bytes 221192 | tf_op jit(solution)/shard_map/ppermute | solution.py:452
  46.4 1.4 %collective-permute-start.6 = (f32[9,8,128]{2,1,0:T(8,128)}, f32[9,8,128]{2,1,0:T(8,128)S(1)}, u32[]{:S(2)}, u32[]{:S(2)}) collective-permute-start(f32[9,8,128]{2,1,0:T(8,128)} %get-tuple-element.23), channel_id=1, source_target_pairs={{0,1},{2,3},{4,5},{6,7},{8,9},{10,11},{12,13},{14,15},{16,17},{18,... | collective-permute-start | bytes 110600 | tf_op jit(solution)/shard_map/ppermute | solution.py:452

commit v4 on v3

--- a/solution.py
+++ b/solution.py
@@ -25,7 +25,9 @@
 GHOST = HALO
 LISTED = CELLS_DEV + 2 * GHOST
 OWN = slice(EDGE_ROWS, EDGE_ROWS + ROWS)
-PACK_ROWS = 8
+PACK_ROWS = 16
+KEPT_STEPS = 8
+TERMS = 2 * NEIGHBOURS
 DUMMY = EDGE * 64 + 32 + (8 << 20)
 UNROLL = 16
 LIST_SIZE = LISTED * 32 + 64
@@ -78,14 +80,59 @@
         ref[88 : 88 + NEIGHBOURS, 0:CELLS_DEV] = lists
 
 
+def order_kernel(own_ref, dest_in, slot_in, hi_out, lo_out, bits_out, dest_ref, slot_ref, sem):
+    own = own_ref[0]
+    loads = [
+        pltpu.make_async_copy(dest_in, dest_ref, sem.at[0]),
+        pltpu.make_async_copy(slot_in, slot_ref, sem.at[1]),
+    ]
+    for copy in loads:
+        copy.start()
+    for copy in loads:
+        copy.wait()
+    before = (
+        lax.broadcasted_iota(jnp.int32, (LANES, LANES), 0)
+        < lax.broadcasted_iota(jnp.int32, (LANES, LANES), 1)
+    ).astype(jnp.bfloat16)
+    ones = jnp.ones((LANES, LANES), jnp.bfloat16)
+    dest = dest_ref[...]
+    away = (dest - own) & 127
+    signed = jnp.where(away > 64, away - 128, away)
+    group = jnp.where(signed < 0, signed + REACH, signed + REACH - 1)
+    place = (slot_ref[...] - PART_DEV) & (MOST - 1)
+    moving = dest != own
+    hi = (group >> 1) * 8 + (place >> 7)
+    lo = (group & 1) * LANES + (place & (LANES - 1))
+    key = jnp.where(moving, hi * 256 + lo, -1)
+    bits = jnp.zeros((ROWS, LANES), jnp.int32)
+    mover16 = moving.astype(jnp.float32).astype(jnp.bfloat16)
+    above = lax.dot_general(
+        before, mover16, (((0,), (0,)), ((), ())), preferred_element_type=jnp.float32
+    ).astype(jnp.int32)
+    in_column = jnp.dot(ones, mover16, preferred_element_type=jnp.float32).astype(jnp.int32)
+    own_row = lax.broadcasted_iota(jnp.int32, (ROWS, LANES), 0)
+    remaining = jnp.where(moving, own_row - above, 0)
+    for bit in range(7):
+        coming = pltpu.roll(remaining, ROWS - (1 << bit), 0)
+        lands = (coming >> bit) & 1
+        leaves = (remaining >> bit) & 1
+        bits = bits | (lands << bit)
+        key = jnp.where(lands == 1, pltpu.roll(key, ROWS - (1 << bit), 0), key)
+        remaining = jnp.where(lands == 1, coming, jnp.where(leaves == 1, 0, remaining))
+    key = jnp.where(own_row < in_column, key, -1)
+    hi_out[...] = (key >> 8).astype(jnp.float32)
+    lo_out[...] = (key & 255).astype(jnp.float32)
+    bits_out[...] = bits
+
+
 def state_kernel(
-    own_ref, pos_ref, vel_ref, mass_ref, ent_ref, rho_ref, act_ref, dest_ref, slot_ref,
-    nbr_ref, far_in, near_in,
+    own_ref, pos_ref, vel_ref, mass_ref, ent_ref, rho_ref, act_ref, dest_ref,
+    nbr_ref, far_in, near_in, hi_in, lo_in, bits_in,
     kept_ref, to_far, to_far2, to_next, to_next2, to_other,
-    pos_v, vel_v, act_v, dest_v, slot_v, nbr_v,
+    pos_v, vel_v, act_v, dest_v, nbr_v,
     xs, ys, zs, ms, ps, es, rho_old, rank, dens, ax, ay, az,
-    fields, key, shifts, parts, hi_row, lo_row, a0, b0, packed, blocks,
-    far_ref, near_ref, table_v, table, chunk_list, sem,
+    fields, bits, parts, hi_row, lo_row, a0, b0, packed, blocks,
+    far_ref, near_ref, sq, mp, factors, table_v, table, chunk_list, sem,
 ):
     own = own_ref[0]
     even = own % 2 == 0
@@ -96,7 +143,9 @@
         (far_in, far_ref),
         (near_in, near_ref),
         (dest_ref, dest_v),
-        (slot_ref, slot_v),
+        (hi_in, hi_row),
+        (lo_in, lo_row),
+        (bits_in, bits),
         (rho_ref, rho_old.at[pl.ds(EDGE_ROWS, ROWS)]),
         (mass_ref, ms.at[pl.ds(EDGE_ROWS, ROWS)]),
         (ent_ref, es.at[pl.ds(EDGE_ROWS, ROWS)]),
@@ -143,7 +192,7 @@
         table_v[16 + 8 * k : 24 + 8 * k, 0:LANES] = (
             near_lists[k].astype(jnp.int32) - shift
         ) & 8191
-    table_copy = pltpu.make_async_copy(table_v, table, sem.at[11])
+    table_copy = pltpu.make_async_copy(table_v, table, sem.at[15])
     table_copy.start()
     high = slice(EDGE_ROWS + ROWS, EXT_ROWS)
     for k, ref in enumerate((xs, ys, zs, ms)):
@@ -161,39 +210,6 @@
 
     for copy in loads[4:]:
         copy.wait()
-
-    dest = dest_v[...]
-    away = (dest - own) & 127
-    signed = jnp.where(away > 64, away - 128, away)
-    group = jnp.where(signed < 0, signed + REACH, signed + REACH - 1)
-    place = (slot_v[...] - PART_DEV) & (MOST - 1)
-    moving = dest != own
-    hi = (group >> 1) * 8 + (place >> 7)
-    lo = (group & 1) * LANES + (place & (LANES - 1))
-    key[...] = jnp.where(moving, hi * 256 + lo, -1)
-    mover16 = moving.astype(jnp.float32).astype(jnp.bfloat16)
-    above = lax.dot_general(
-        before, mover16, (((0,), (0,)), ((), ())), preferred_element_type=jnp.float32
-    ).astype(jnp.int32)
-    in_column = jnp.dot(ones, mover16, preferred_element_type=jnp.float32).astype(jnp.int32)
-    own_row = lax.broadcasted_iota(jnp.int32, (ROWS, LANES), 0)
-    remaining = jnp.where(moving, own_row - above, 0)
-    for bit in range(7):
-        coming = pltpu.roll(remaining, ROWS - (1 << bit), 0)
-        lands = (coming >> bit) & 1
-        leaves = (remaining >> bit) & 1
-        shifts[bit] = lands
-        remaining = jnp.where(lands == 1, coming, jnp.where(leaves == 1, 0, remaining))
-    mover_rows = jnp.max(in_column)
-
-    def moved_up(x):
-        for bit in range(7):
-            x = jnp.where(shifts[bit] == 1, pltpu.roll(x, ROWS - (1 << bit), 0), x)
-        return x
-
-    new_key = jnp.where(own_row < in_column, moved_up(key[...]), -1)
-    hi_row[...] = (new_key >> 8).astype(jnp.float32)
-    lo_row[...] = (new_key & 255).astype(jnp.float32)
 
     def split_rows(i, carry):
         col = pl.multiple_of(i * LANES, LANES)
@@ -271,65 +287,97 @@
             row = jnp.sum(jnp.where(picks[h], value, 0.0), axis=0, keepdims=True)
             ref[pl.ds(2 * cell + h, 1), :] += row
 
-    def density_step(step):
+    sq[...] = -(xs[...] * xs[...] + ys[...] * ys[...] + zs[...] * zs[...])
+
+    def target(cell, picks):
+        cx, cy, cz = (column(ref, cell, picks) for ref in (xs, ys, zs))
+        inner = 1.0 - (cx * cx + cy * cy + cz * cz)
+        return cx, cy, cz, [jnp.broadcast_to(x, (8, LANES)) for x in (inner, 2.0 * cx, 2.0 * cy, 2.0 * cz)]
+
+    def factor(wide, row):
+        inner, tx, ty, tz = wide
+        near = (inner + bcast(sq, row)) + tx * bcast(xs, row)
+        near = (near + ty * bcast(ys, row)) + tz * bcast(zs, row)
+        return jnp.maximum(near, 0.0)
+
+    def density_step(step, keep):
         done = []
         for u in range(UNROLL):
-            cell, picks, sources = chunk_of(step * UNROLL + u, all_total)
-            cx, cy, cz = (column(ref, cell, picks) for ref in (xs, ys, zs))
+            position = step * UNROLL + u
+            cell, picks, sources = chunk_of(position, all_total)
+            wide = target(cell, picks)[3]
             total_rows = jnp.zeros((8, LANES), jnp.float32)
-            for source in sources:
+            for q, source in enumerate(sources):
                 for h in range(2):
                     row = 2 * source + h
-                    dx = cx - bcast(xs, row)
-                    dy = cy - bcast(ys, row)
-                    dz = cz - bcast(zs, row)
-                    u1 = jnp.maximum(1.0 - (dx * dx + dy * dy + dz * dz), 0.0)
+                    u1 = factor(wide, row)
+                    if keep:
+                        factors[position * TERMS + 2 * q + h] = u1
                     total_rows += u1 * u1 * u1 * bcast(ms, row)
             value = jnp.sum(total_rows, axis=1, keepdims=True) * scale
             done.append((cell, picks, value))
         for cell, picks, value in done:
             spread(dens, cell, picks, value)
 
-    def density_loop(step, carry):
-        density_step(step)
-        return carry
-
-    lax.fori_loop(0, (all_total + UNROLL - 1) // UNROLL, density_loop, 0)
+    def loop(limit, body):
+        steps = (limit + UNROLL - 1) // UNROLL
+
+        def run(keep):
+            def one(step, carry):
+                body(step, keep)
+                return carry
+
+            return one
+
+        lax.fori_loop(0, jnp.minimum(steps, KEPT_STEPS), run(True), 0)
+        lax.fori_loop(KEPT_STEPS, steps, run(False), 0)
+
+    loop(all_total, density_step)
 
     rho = jnp.where(rank[...] >= 0.0, dens[...], rho_old[...])
     dens[...] = rho
     ps[...] = es[...] * jnp.exp(jnp.log(rho) * (-1.0 / 3.0))
 
-    def force_step(step, carry):
+    mp[...] = ms[...] * ps[...]
+
+    def force_step(step, keep):
         done = []
         for u in range(UNROLL):
-            cell, picks, sources = chunk_of(step * UNROLL + u, own_total)
-            cx, cy, cz, cp = (column(ref, cell, picks) for ref in (xs, ys, zs, ps))
-            sx = jnp.zeros((8, LANES), jnp.float32)
-            sy = jnp.zeros((8, LANES), jnp.float32)
-            sz = jnp.zeros((8, LANES), jnp.float32)
-            for source in sources:
+            position = step * UNROLL + u
+            cell, picks, sources = chunk_of(position, own_total)
+            cx, cy, cz, wide = target(cell, picks)
+            cp = jnp.broadcast_to(column(ps, cell, picks), (8, LANES))
+            s0 = jnp.zeros((8, LANES), jnp.float32)
+            sums = [s0, s0, s0]
+            for q, source in enumerate(sources):
                 for h in range(2):
                     row = 2 * source + h
-                    dx = cx - bcast(xs, row)
-                    dy = cy - bcast(ys, row)
-                    dz = cz - bcast(zs, row)
-                    u1 = jnp.maximum(1.0 - (dx * dx + dy * dy + dz * dz), 0.0)
-                    w = u1 * u1 * (bcast(ms, row) * (cp + bcast(ps, row)))
-                    sx += w * dx
-                    sy += w * dy
-                    sz += w * dz
+                    if keep:
+                        u1 = factors[position * TERMS + 2 * q + h]
+                    else:
+                        u1 = factor(wide, row)
+                    w = (u1 * u1) * (cp * bcast(ms, row) + bcast(mp, row))
+                    s0 += w
+                    sums = [t + w * bcast(ref, row) for t, ref in zip(sums, (xs, ys, zs))]
             values = [
-                jnp.sum(s, axis=1, keepdims=True) * (3.0 * scale * time_step)
-                for s in (sx, sy, sz)
+                jnp.sum(c * s0 - t, axis=1, keepdims=True) * (3.0 * scale * time_step)
+                for c, t in zip((cx, cy, cz), sums)
             ]
             done.append((cell, picks, values))
         for cell, picks, values in done:
             for ref, value in zip((ax, ay, az), values):
                 spread(ref, cell, picks, value)
-        return carry
-
-    lax.fori_loop(0, (own_total + UNROLL - 1) // UNROLL, force_step, 0)
+
+    loop(own_total, force_step)
+
+    own_row = lax.broadcasted_iota(jnp.int32, (ROWS, LANES), 0)
+    mover_rows = jnp.max(jnp.where(hi_row[...] >= 0.0, own_row + 1, 0))
+
+    def moved_up(x):
+        for bit in range(7):
+            lands = (bits[...] >> bit) & 1
+            x = jnp.where(lands == 1, pltpu.roll(x, ROWS - (1 << bit), 0), x)
+        return x
 
     for c, acc in enumerate((ax, ay, az)):
         kicked = fields[3 + c] + acc[OWN, :]
@@ -416,8 +464,8 @@
 
 
 def assemble_kernel(
-    own_ref, next_ref, next2_ref, far_ref, far2_ref, other_ref,
-    x_next, x_next2, x_far, x_far2, held_ref, out_ref, rows, sem
+    own_ref, next2_ref, far2_ref, next_ref, far_ref, other_ref,
+    x_next2, x_far2, x_next, x_far, held_ref, out_ref, rows, sem
 ):
     del held_ref
     own = own_ref[0]
@@ -492,6 +540,26 @@
     far = swapped(far, far_pairs)
     near = swapped(near, near_pairs)
 
+    dest, slot = destination.reshape(square), recv_slot.reshape(square)
+    order = pl.pallas_call(
+        order_kernel,
+        out_shape=(
+            jax.ShapeDtypeStruct(square, f32),
+            jax.ShapeDtypeStruct(square, f32),
+            jax.ShapeDtypeStruct(square, i32),
+        ),
+        in_specs=[sm] + [hbm] * 2,
+        out_specs=(vm,) * 3,
+        scratch_shapes=[
+            pltpu.VMEM(square, i32),
+            pltpu.VMEM(square, i32),
+            pltpu.SemaphoreType.DMA((2,)),
+        ],
+        compiler_params=pltpu.CompilerParams(vmem_limit_bytes=64 * 2**20),
+        cost_estimate=pl.CostEstimate(
+            flops=2**24, bytes_accessed=2**23, transcendentals=0
+        ),
+    )(own, dest, slot)
     ext = pltpu.VMEM((EXT_ROWS, LANES), f32)
     flat = pltpu.VMEM((3, PART_DEV), f32)
     whole = pltpu.VMEM(square, i32)
@@ -506,15 +574,14 @@
             pair,
             jax.ShapeDtypeStruct((FIELDS, 8, LANES), f32),
         ),
-        in_specs=[sm] + [hbm] * 11,
+        in_specs=[sm] + [hbm] * 13,
         out_specs=(vm,) * 6,
-        scratch_shapes=[flat, flat, whole, whole, whole]
+        scratch_shapes=[flat, flat, whole, whole]
         + [pltpu.VMEM((NEIGHBOURS, CELLS_DEV), i32)]
         + [ext] * 12
         + [
             pltpu.VMEM((FIELDS, ROWS, LANES), f32),
             whole,
-            pltpu.VMEM((7, ROWS, LANES), i32),
             pltpu.VMEM((2 * FIELDS, ROWS, LANES), f32),
             pltpu.VMEM(square, f32),
             pltpu.VMEM(square, f32),
@@ -524,10 +591,13 @@
             pltpu.VMEM((GROUPS, FIELDS, 8, LANES), f32),
             pltpu.VMEM((HALO_ROWS, LANES), f32),
             pltpu.VMEM((HALO_ROWS, LANES), f32),
+            ext,
+            ext,
+            pltpu.VMEM((KEPT_STEPS * UNROLL * TERMS, 8, LANES), f32),
             pltpu.VMEM((32, LANES), i32),
             pltpu.SMEM((32, LANES), i32),
             pltpu.SMEM((LIST_SIZE,), i32),
-            pltpu.SemaphoreType.DMA((12,)),
+            pltpu.SemaphoreType.DMA((16,)),
         ],
         compiler_params=pltpu.CompilerParams(vmem_limit_bytes=64 * 2**20),
     )(
@@ -538,11 +608,11 @@
         ent,
         rho,
         act,
-        destination.reshape(square),
-        recv_slot.reshape(square),
+        dest,
         lists,
         far,
         near,
+        *order,
     )
     to_far, to_far2, to_next, to_next2, to_other = sends
     chips = count // 2
@@ -570,13 +640,13 @@
             pltpu.VMEM((FIELDS, PART_DEV), f32),
             pltpu.SemaphoreType.DMA((2,)),
         ],
-        compiler_params=pltpu.CompilerParams(vmem_limit_bytes=64 * 2**20),
+        compiler_params=pltpu.CompilerParams(vmem_limit_bytes=64 * 2**20 - 450 * 2**10),
         cost_estimate=pl.CostEstimate(
             flops=4 * 2**20, bytes_accessed=4 * 2**20, transcendentals=0
         ),
     )(kept)
-    next1, held = lax.optimization_barrier((next1, held))
-    crossed = [swapped(x, near_pairs) for x in (next1, next2, far1, far2)]
+    far1, held = lax.optimization_barrier((far1, held))
+    crossed = [swapped(x, near_pairs) for x in (next2, far2, next1, far1)]
     return pl.pallas_call(
         assemble_kernel,
         out_shape=jax.ShapeDtypeStruct((FIELDS, RECV_DEV), f32),
@@ -588,7 +658,7 @@
         ],
         input_output_aliases={10: 0},
         compiler_params=pltpu.CompilerParams(vmem_limit_bytes=16 * 2**20),
-    )(own, next1, next2, far1, far2, other, *crossed, held)
+    )(own, next2, far2, next1, far1, other, *crossed, held)
 
 
 def solution(mesh):

time: 50.2 us -> 47.5 us (0.946)
  waiting for transfers between devices: 8 us -> 5.12 us
  starting transfers between devices: 19.4 us -> 20.1 us
    ppermute x11, waiting for transfers between devices: 8 us -> 5.12 us  [swapped(): return lax.ppermute(block, 'cells', route)]
    pallas_call x0 -> x1, Pallas kernels: none -> 1.94 us  [per_device(): pl.pallas_call(order_kernel, out_shape=(jax.ShapeDtypeStruct(square, f32)...]
    pallas_call x1, Pallas kernels: 16.3 us -> 14.8 us  [per_device(): pl.pallas_call(state_kernel, out_shape=(jax.ShapeDtypeStruct((FIELDS, ROW...]
    pallas_call x1, Pallas kernels: 1.98 us -> 0.99 us  [per_device(): pl.pallas_call(assemble_kernel, out_shape=jax.ShapeDtypeStruct((FIELDS, R...]
    ppermute x11, starting transfers between devices: 19.4 us -> 20.1 us  [swapped(): return lax.ppermute(block, 'cells', route)]
  transfers between devices with their start and end apart: 11 -> 11, of which waited for: 4 -> 2; matrix products, arithmetic and copies ran while one was open for 0% -> 0% of each run, Pallas kernels for 5% -> 9%
where the time goes in v4:
time: 47.5 us; the launch traced here: 47.2 us
  Pallas kernels  21.9 us (46%)
  starting transfers between devices  20.1 us (42%)
  waiting for transfers between devices  5.12 us (11%)
    ppermute x11, starting transfers between devices, swapped(): return lax.ppermute(block, 'cells', route)  20.1 us
    pallas_call x1, Pallas kernels, per_device(): pl.pallas_call(state_kernel, out_shape=(jax.ShapeDtypeStruct((FIELDS, ROW...  14.8 us
    ppermute x11, waiting for transfers between devices, swapped(): return lax.ppermute(block, 'cells', route)  5.12 us
    pallas_call x1, Pallas kernels, per_device(): pl.pallas_call(stay_kernel, out_shape=jax.ShapeDtypeStruct((FIELDS, RECV_...  2.51 us
    pallas_call x1, Pallas kernels, per_device(): pl.pallas_call(order_kernel, out_shape=(jax.ShapeDtypeStruct(square, f32)...  1.94 us
    pallas_call x1, Pallas kernels, per_device(): pl.pallas_call(edge_kernel, out_shape=(jax.ShapeDtypeStruct((HALO_ROWS, L...  1.63 us
    pallas_call x1, Pallas kernels, per_device(): pl.pallas_call(assemble_kernel, out_shape=jax.ShapeDtypeStruct((FIELDS, R...  0.99 us
  transfers between devices with their start and end apart: 11, of which 2 were waited for; matrix products, arithmetic and copies ran while one was open for 0% of the time, Pallas kernels for 9%

profile of v4, /device:TPU:1, one launch (start us, length us, event | category | flops | bytes accessed | tf_op | source)
XLA Modules:
  0.0 47.2 jit_solution(2846366507086852691)
XLA Ops:
  0.0 1.6 %shard_map.91 = (f32[96,128]{1,0:T(8,128)}, f32[96,128]{1,0:T(8,128)}) custom-call(s32[1]{0:T(128)} %bitcast.own_ref, f32[3,16384]{1,0:T(4,128)} %pos_ref.3, f32[128,128]{1,0:T(8,128)} %bitcast.8, f32[128,128]{1,0:T(8,128)} %bitcast.10, f32[128,128]{1,0:T(8,128)} %bitcast.12, s32[128,128]{1,0:T(8,128)} %bitcast.14, s32[6,64]{1,0:T(8,128)} %bitcast.19), custom_call_target="tpu_custom_call" | custom-call | tf_op jit(solution)/shard_map/pallas_call | solution.py:525
  1.6 3.1 %collective-permute-start = (f32[96,128]{1,0:T(8,128)}, f32[96,128]{1,0:T(8,128)}, u32[]{:S(2)}, u32[]{:S(2)}) collective-permute-start(f32[96,128]{1,0:T(8,128)} %get-tuple-element.18), channel_id=1, source_target_pairs={{1,2},{3,4},{5,6},{7,8},{9,10},{11,12},{13,14},{15,16},{17,18},{19... | collective-permute-start | bytes 147464 | tf_op jit(solution)/shard_map/ppermute | solution.py:500
  4.7 6.6 %collective-permute-start.1 = (f32[96,128]{1,0:T(8,128)}, f32[96,128]{1,0:T(8,128)}, u32[]{:S(2)}, u32[]{:S(2)}) collective-permute-start(f32[96,128]{1,0:T(8,128)} %get-tuple-element.19), channel_id=1, source_target_pairs={{0,1},{2,3},{4,5},{6,7},{8,9},{10,11},{12,13},{14,15},{16,17},{18,... | collective-permute-start | bytes 147464 | tf_op jit(solution)/shard_map/ppermute | solution.py:500
  11.3 1.9 %shard_map.92 = (f32[128,128]{1,0:T(8,128)}, f32[128,128]{1,0:T(8,128)}, s32[128,128]{1,0:T(8,128)}) custom-call(s32[1]{0:T(128)} %bitcast.own_ref, s32[128,128]{1,0:T(8,128)} %bitcast.16, s32[128,128]{1,0:T(8,128)} %bitcast.18), custom_call_target="tpu_custom_call" | custom-call | flops 16777216 | bytes 8388608 | tf_op jit(solution)/shard_map/pallas_call | solution.py:544
  13.3 0.0 collective-permute-done.far_in
  13.3 0.0 collective-permute-done.1.near_in
  13.3 14.8 %shard_map.93 = (f32[9,128,128]{2,1,0:T(8,128)}, f32[2,9,8,128]{3,2,1,0:T(8,128)}, f32[2,9,8,128]{3,2,1,0:T(8,128)}, f32[2,9,8,128]{3,2,1,0:T(8,128)}, f32[2,9,8,128]{3,2,1,0:T(8,128)}, /*index=5*/f32[9,8,128]{2,1,0:T(8,128)}) custom-call(s32[1]{0:T(128)} %bitcast.own_ref, f32[3,16384]{1,0:T(4,128)} %pos_ref.3, f32[3,16384]{1,0:T(4,128)} %vel_ref.1, ...), custom_call_target="tpu_custom_call" | custom-call | tf_op jit(solution)/shard_map/pallas_call | solution.py:567
  28.1 0.0 copy-start
  28.1 0.1 collective-permute-start.5
  28.2 7.0 %collective-permute-start.2 = (f32[2,9,8,128]{3,2,1,0:T(8,128)}, f32[2,9,8,128]{3,2,1,0:T(8,128)S(1)}, u32[]{:S(2)}, u32[]{:S(2)}) collective-permute-start(f32[2,9,8,128]{3,2,1,0:T(8,128)} %get-tuple-element.23), channel_id=1, source_target_pairs={{2,4},{3,5},{6,8},{7,9},{10,12},{11,13},{14,16},{15,17},{18,20},{1... | collective-permute-start | bytes 221192 | tf_op jit(solution)/shard_map/ppermute | solution.py:500
  35.2 2.3 %collective-permute-start.3 = (f32[2,9,8,128]{3,2,1,0:T(8,128)}, f32[2,9,8,128]{3,2,1,0:T(8,128)S(1)}, u32[]{:S(2)}, u32[]{:S(2)}) collective-permute-start(f32[2,9,8,128]{3,2,1,0:T(8,128)} %get-tuple-element.24), channel_id=1, source_target_pairs={{4,8},{5,9},{6,10},{7,11},{12,16},{13,17},{14,18},{15,19},{20,24},... | collective-permute-start | bytes 221192 | tf_op jit(solution)/shard_map/ppermute | solution.py:500
  37.4 0.0 collective-permute-start.4
  37.5 2.5 %shard_map.94.held_ref = f32[9,24576]{1,0:T(8,128)} custom-call(f32[9,128,128]{2,1,0:T(8,128)} %get-tuple-element.27.kept_ref), custom_call_target="tpu_custom_call" | custom-call | flops 4194304 | bytes 4194304 | tf_op jit(solution)/shard_map/pallas_call | solution.py:633
  40.0 0.0 collective-permute-done.5.far_ref
  40.0 0.0 collective-permute-done.2.next2_ref
  40.0 0.1 collective-permute-start.7
  40.1 4.2 %collective-permute-done.3.far2_ref = f32[2,9,8,128]{3,2,1,0:T(8,128)S(1)} collective-permute-done((f32[2,9,8,128]{3,2,1,0:T(8,128)}, f32[2,9,8,128]{3,2,1,0:T(8,128)S(1)}, u32[]{:S(2)}, u32[]{:S(2)}) %collective-permute-start.3) | collective-permute-done | bytes 73760 | tf_op jit(solution)/shard_map/ppermute | solution.py:500
  44.3 0.0 collective-permute-start.8
  44.3 0.0 collective-permute-done.4.next_ref
  44.3 0.5 %collective-permute-start.9 = (f32[2,9,8,128]{3,2,1,0:T(8,128)S(1)}, f32[2,9,8,128]{3,2,1,0:T(8,128)S(1)}, u32[]{:S(2)}, u32[]{:S(2)}) collective-permute-start(f32[2,9,8,128]{3,2,1,0:T(8,128)S(1)} %collective-permute-done.4.next_ref), channel_id=1, source_target_pairs={{0,1},{2,3},{4,5},{6,7},{8,9},{10,11},{12,13},{14,15},{16,17},{18,... | collective-permute-start | bytes 221192 | tf_op jit(solution)/shard_map/ppermute | solution.py:500
  44.8 0.0 collective-permute-start.10
  44.8 0.0 copy-done
  44.8 0.5 %collective-permute-start.6 = (f32[9,8,128]{2,1,0:T(8,128)S(1)}, f32[9,8,128]{2,1,0:T(8,128)S(1)}, u32[]{:S(2)}, u32[]{:S(2)}) collective-permute-start(f32[9,8,128]{2,1,0:T(8,128)S(1)} %copy-done), channel_id=1, source_target_pairs={{0,1},{2,3},{4,5},{6,7},{8,9},{10,11},{12,13},{14,15},{16,17},{18,... | collective-permute-start | bytes 110600 | tf_op jit(solution)/shard_map/ppermute | solution.py:500
  45.3 0.9 %collective-permute-done.6.other_ref = f32[9,8,128]{2,1,0:T(8,128)S(1)} collective-permute-done((f32[9,8,128]{2,1,0:T(8,128)S(1)}, f32[9,8,128]{2,1,0:T(8,128)S(1)}, u32[]{:S(2)}, u32[]{:S(2)}) %collective-permute-start.6) | collective-permute-done | bytes 36896 | tf_op jit(solution)/shard_map/ppermute | solution.py:500
  46.2 0.0 collective-permute-done.7.x_next2
  46.2 0.0 collective-permute-done.8.x_far2
  46.2 0.0 collective-permute-done.9.x_next
  46.2 0.0 collective-permute-done.10.x_far
  46.2 1.0 %shard_map.95 = f32[9,24576]{1,0:T(8,128)} custom-call(s32[1]{0:T(128)} %bitcast.own_ref, f32[2,9,8,128]{3,2,1,0:T(8,128)S(1)} %collective-permute-done.2.next2_ref, f32[2,9,8,128]{3,2,1,0:T(8,128)S(1)} %collective-permute-done.3.far2_ref, f32[2,9,8,128]{3,2,1,0:T(8,128)S(1)} %collective-permute-done.4.next_ref, ...), custom_call_target="tpu_custom_call", output_to_operand_aliasing={{}: (10, {})} | custom-call | tf_op jit(solution)/shard_map/pallas_call | solution.py:650
Async XLA Ops:
  1.6 11.7 %collective-permute-start = (f32[96,128]{1,0:T(8,128)}, f32[96,128]{1,0:T(8,128)}, u32[]{:S(2)}, u32[]{:S(2)}) collective-permute-start(f32[96,128]{1,0:T(8,128)} %get-tuple-element.18), channel_id=1, source_target_pairs={{1,2},{3,4},{5,6},{7,8},{9,10},{11,12},{13,14},{15,16},{17,18},{19... | collective-permute-start | bytes 147464 | tf_op jit(solution)/shard_map/ppermute | solution.py:500
  4.7 8.6 %collective-permute-start.1 = (f32[96,128]{1,0:T(8,128)}, f32[96,128]{1,0:T(8,128)}, u32[]{:S(2)}, u32[]{:S(2)}) collective-permute-start(f32[96,128]{1,0:T(8,128)} %get-tuple-element.19), channel_id=1, source_target_pairs={{0,1},{2,3},{4,5},{6,7},{8,9},{10,11},{12,13},{14,15},{16,17},{18,... | collective-permute-start | bytes 147464 | tf_op jit(solution)/shard_map/ppermute | solution.py:500
  28.1 16.7 %copy-start = (f32[9,8,128]{2,1,0:T(8,128)S(1)}, f32[9,8,128]{2,1,0:T(8,128)}, u32[]{:S(2)}) copy-start(f32[9,8,128]{2,1,0:T(8,128)} %get-tuple-element.29) | copy-start | bytes 110596
  28.1 11.8 %collective-permute-start.5 = (f32[2,9,8,128]{3,2,1,0:T(8,128)}, f32[2,9,8,128]{3,2,1,0:T(8,128)S(1)}, u32[]{:S(2)}, u32[]{:S(2)}) collective-permute-start(f32[2,9,8,128]{3,2,1,0:T(8,128)} %get-tuple-element.26), channel_id=1, source_target_pairs={{0,4},{1,5},{2,6},{3,7},{8,12},{9,13},{10,14},{11,15},{16,20},{17,... | collective-permute-start | bytes 221192 | tf_op jit(solution)/shard_map/ppermute | solution.py:500
  28.2 11.8 %collective-permute-start.2 = (f32[2,9,8,128]{3,2,1,0:T(8,128)}, f32[2,9,8,128]{3,2,1,0:T(8,128)S(1)}, u32[]{:S(2)}, u32[]{:S(2)}) collective-permute-start(f32[2,9,8,128]{3,2,1,0:T(8,128)} %get-tuple-element.23), channel_id=1, source_target_pairs={{2,4},{3,5},{6,8},{7,9},{10,12},{11,13},{14,16},{15,17},{18,20},{1... | collective-permute-start | bytes 221192 | tf_op jit(solution)/shard_map/ppermute | solution.py:500
  35.2 9.1 %collective-permute-start.3 = (f32[2,9,8,128]{3,2,1,0:T(8,128)}, f32[2,9,8,128]{3,2,1,0:T(8,128)S(1)}, u32[]{:S(2)}, u32[]{:S(2)}) collective-permute-start(f32[2,9,8,128]{3,2,1,0:T(8,128)} %get-tuple-element.24), channel_id=1, source_target_pairs={{4,8},{5,9},{6,10},{7,11},{12,16},{13,17},{14,18},{15,19},{20,24},... | collective-permute-start | bytes 221192 | tf_op jit(solution)/shard_map/ppermute | solution.py:500
  37.4 6.9 %collective-permute-start.4 = (f32[2,9,8,128]{3,2,1,0:T(8,128)}, f32[2,9,8,128]{3,2,1,0:T(8,128)S(1)}, u32[]{:S(2)}, u32[]{:S(2)}) collective-permute-start(f32[2,9,8,128]{3,2,1,0:T(8,128)} %get-tuple-element.25), channel_id=1, source_target_pairs={{0,2},{1,3},{4,6},{5,7},{8,10},{9,11},{12,14},{13,15},{16,18},{17,... | collective-permute-start | bytes 221192 | tf_op jit(solution)/shard_map/ppermute | solution.py:500
  40.0 6.2 %collective-permute-start.7 = (f32[2,9,8,128]{3,2,1,0:T(8,128)S(1)}, f32[2,9,8,128]{3,2,1,0:T(8,128)S(1)}, u32[]{:S(2)}, u32[]{:S(2)}) collective-permute-start(f32[2,9,8,128]{3,2,1,0:T(8,128)S(1)} %collective-permute-done.2.next2_ref), channel_id=1, source_target_pairs={{0,1},{2,3},{4,5},{6,7},{8,9},{10,11},{12,13},{14,15},{16,17},{18,... | collective-permute-start | bytes 221192 | tf_op jit(solution)/shard_map/ppermute | solution.py:500
  44.3 1.9 %collective-permute-start.8 = (f32[2,9,8,128]{3,2,1,0:T(8,128)S(1)}, f32[2,9,8,128]{3,2,1,0:T(8,128)S(1)}, u32[]{:S(2)}, u32[]{:S(2)}) collective-permute-start(f32[2,9,8,128]{3,2,1,0:T(8,128)S(1)} %collective-permute-done.3.far2_ref), channel_id=1, source_target_pairs={{0,1},{2,3},{4,5},{6,7},{8,9},{10,11},{12,13},{14,15},{16,17},{18,... | collective-permute-start | bytes 221192 | tf_op jit(solution)/shard_map/ppermute | solution.py:500
  44.3 1.9 %collective-permute-start.9 = (f32[2,9,8,128]{3,2,1,0:T(8,128)S(1)}, f32[2,9,8,128]{3,2,1,0:T(8,128)S(1)}, u32[]{:S(2)}, u32[]{:S(2)}) collective-permute-start(f32[2,9,8,128]{3,2,1,0:T(8,128)S(1)} %collective-permute-done.4.next_ref), channel_id=1, source_target_pairs={{0,1},{2,3},{4,5},{6,7},{8,9},{10,11},{12,13},{14,15},{16,17},{18,... | collective-permute-start | bytes 221192 | tf_op jit(solution)/shard_map/ppermute | solution.py:500
  44.8 1.4 %collective-permute-start.10 = (f32[2,9,8,128]{3,2,1,0:T(8,128)S(1)}, f32[2,9,8,128]{3,2,1,0:T(8,128)S(1)}, u32[]{:S(2)}, u32[]{:S(2)}) collective-permute-start(f32[2,9,8,128]{3,2,1,0:T(8,128)S(1)} %collective-permute-done.5.far_ref), channel_id=1, source_target_pairs={{0,1},{2,3},{4,5},{6,7},{8,9},{10,11},{12,13},{14,15},{16,17},{18,... | collective-permute-start | bytes 221192 | tf_op jit(solution)/shard_map/ppermute | solution.py:500
  44.8 1.4 %collective-permute-start.6 = (f32[9,8,128]{2,1,0:T(8,128)S(1)}, f32[9,8,128]{2,1,0:T(8,128)S(1)}, u32[]{:S(2)}, u32[]{:S(2)}) collective-permute-start(f32[9,8,128]{2,1,0:T(8,128)S(1)} %copy-done), channel_id=1, source_target_pairs={{0,1},{2,3},{4,5},{6,7},{8,9},{10,11},{12,13},{14,15},{16,17},{18,... | collective-permute-start | bytes 110600 | tf_op jit(solution)/shard_map/ppermute | solution.py:500

commit v5 on v4

--- a/solution.py
+++ b/solution.py
@@ -464,8 +464,8 @@
 
 
 def assemble_kernel(
-    own_ref, next2_ref, far2_ref, next_ref, far_ref, other_ref,
-    x_next2, x_far2, x_next, x_far, held_ref, out_ref, rows, sem
+    own_ref, far2_ref, next2_ref, far_ref, next_ref, other_ref,
+    x_far2, x_next2, x_far, x_next, held_ref, out_ref, rows, sem
 ):
     del held_ref
     own = own_ref[0]
@@ -645,8 +645,8 @@
             flops=4 * 2**20, bytes_accessed=4 * 2**20, transcendentals=0
         ),
     )(kept)
-    far1, held = lax.optimization_barrier((far1, held))
-    crossed = [swapped(x, near_pairs) for x in (next2, far2, next1, far1)]
+    far2, held = lax.optimization_barrier((far2, held))
+    crossed = [swapped(x, near_pairs) for x in (far2, next2, far1, next1)]
     return pl.pallas_call(
         assemble_kernel,
         out_shape=jax.ShapeDtypeStruct((FIELDS, RECV_DEV), f32),
@@ -658,7 +658,7 @@
         ],
         input_output_aliases={10: 0},
         compiler_params=pltpu.CompilerParams(vmem_limit_bytes=16 * 2**20),
-    )(own, next2, far2, next1, far1, other, *crossed, held)
+    )(own, far2, next2, far1, next1, other, *crossed, held)
 
 
 def solution(mesh):

time: 47.5 us -> 44.1 us (0.928)
  waiting for transfers between devices: 5.12 us -> 0.89 us
  starting transfers between devices: 20.1 us -> 21 us
    ppermute x11, waiting for transfers between devices: 5.12 us -> 0.89 us  [swapped(): return lax.ppermute(block, 'cells', route)]
    ppermute x11, starting transfers between devices: 20.1 us -> 21 us  [swapped(): return lax.ppermute(block, 'cells', route)]
  transfers between devices with their start and end apart: 11 -> 11, of which waited for: 2 -> 1; matrix products, arithmetic and copies ran while one was open for 0% -> 0% of each run, Pallas kernels for 9% -> 10%
where the time goes in v5:
time: 44.1 us; the launch traced here: 43.9 us
  Pallas kernels  21.9 us (50%)
  starting transfers between devices  21 us (48%)
  waiting for transfers between devices  0.89 us (2%)
    ppermute x11, starting transfers between devices, swapped(): return lax.ppermute(block, 'cells', route)  21 us
    pallas_call x1, Pallas kernels, per_device(): pl.pallas_call(state_kernel, out_shape=(jax.ShapeDtypeStruct((FIELDS, ROW...  14.8 us
    pallas_call x1, Pallas kernels, per_device(): pl.pallas_call(stay_kernel, out_shape=jax.ShapeDtypeStruct((FIELDS, RECV_...  2.51 us
    pallas_call x1, Pallas kernels, per_device(): pl.pallas_call(order_kernel, out_shape=(jax.ShapeDtypeStruct(square, f32)...  1.94 us
    pallas_call x1, Pallas kernels, per_device(): pl.pallas_call(edge_kernel, out_shape=(jax.ShapeDtypeStruct((HALO_ROWS, L...  1.63 us
    pallas_call x1, Pallas kernels, per_device(): pl.pallas_call(assemble_kernel, out_shape=jax.ShapeDtypeStruct((FIELDS, R...  0.99 us
    ppermute x11, waiting for transfers between devices, swapped(): return lax.ppermute(block, 'cells', route)  0.89 us
  transfers between devices with their start and end apart: 11, of which 1 were waited for; matrix products, arithmetic and copies ran while one was open for 0% of the time, Pallas kernels for 10%

profile of v5, /device:TPU:1, one launch (start us, length us, event | category | flops | bytes accessed | tf_op | source)
XLA Modules:
  0.0 43.9 jit_solution(5575559087109292840)
XLA Ops:
  0.0 1.6 %shard_map.91 = (f32[96,128]{1,0:T(8,128)}, f32[96,128]{1,0:T(8,128)}) custom-call(s32[1]{0:T(128)} %bitcast.own_ref, f32[3,16384]{1,0:T(4,128)} %pos_ref.3, f32[128,128]{1,0:T(8,128)} %bitcast.8, f32[128,128]{1,0:T(8,128)} %bitcast.10, f32[128,128]{1,0:T(8,128)} %bitcast.12, s32[128,128]{1,0:T(8,128)} %bitcast.14, s32[6,64]{1,0:T(8,128)} %bitcast.19), custom_call_target="tpu_custom_call" | custom-call | tf_op jit(solution)/shard_map/pallas_call | solution.py:525
  1.6 3.1 %collective-permute-start = (f32[96,128]{1,0:T(8,128)}, f32[96,128]{1,0:T(8,128)}, u32[]{:S(2)}, u32[]{:S(2)}) collective-permute-start(f32[96,128]{1,0:T(8,128)} %get-tuple-element.18), channel_id=1, source_target_pairs={{1,2},{3,4},{5,6},{7,8},{9,10},{11,12},{13,14},{15,16},{17,18},{19... | collective-permute-start | bytes 147464 | tf_op jit(solution)/shard_map/ppermute | solution.py:500
  4.7 6.6 %collective-permute-start.1 = (f32[96,128]{1,0:T(8,128)}, f32[96,128]{1,0:T(8,128)}, u32[]{:S(2)}, u32[]{:S(2)}) collective-permute-start(f32[96,128]{1,0:T(8,128)} %get-tuple-element.19), channel_id=1, source_target_pairs={{0,1},{2,3},{4,5},{6,7},{8,9},{10,11},{12,13},{14,15},{16,17},{18,... | collective-permute-start | bytes 147464 | tf_op jit(solution)/shard_map/ppermute | solution.py:500
  11.3 1.9 %shard_map.92 = (f32[128,128]{1,0:T(8,128)}, f32[128,128]{1,0:T(8,128)}, s32[128,128]{1,0:T(8,128)}) custom-call(s32[1]{0:T(128)} %bitcast.own_ref, s32[128,128]{1,0:T(8,128)} %bitcast.16, s32[128,128]{1,0:T(8,128)} %bitcast.18), custom_call_target="tpu_custom_call" | custom-call | flops 16777216 | bytes 8388608 | tf_op jit(solution)/shard_map/pallas_call | solution.py:544
  13.3 0.0 collective-permute-done.far_in
  13.3 0.0 collective-permute-done.1.near_in
  13.3 14.8 %shard_map.93 = (f32[9,128,128]{2,1,0:T(8,128)}, f32[2,9,8,128]{3,2,1,0:T(8,128)}, f32[2,9,8,128]{3,2,1,0:T(8,128)}, f32[2,9,8,128]{3,2,1,0:T(8,128)}, f32[2,9,8,128]{3,2,1,0:T(8,128)}, /*index=5*/f32[9,8,128]{2,1,0:T(8,128)}) custom-call(s32[1]{0:T(128)} %bitcast.own_ref, f32[3,16384]{1,0:T(4,128)} %pos_ref.3, f32[3,16384]{1,0:T(4,128)} %vel_ref.1, ...), custom_call_target="tpu_custom_call" | custom-call | tf_op jit(solution)/shard_map/pallas_call | solution.py:567
  28.1 0.0 copy-start
  28.1 1.7 %collective-permute-start.2 = (f32[2,9,8,128]{3,2,1,0:T(8,128)}, f32[2,9,8,128]{3,2,1,0:T(8,128)S(1)}, u32[]{:S(2)}, u32[]{:S(2)}) collective-permute-start(f32[2,9,8,128]{3,2,1,0:T(8,128)} %get-tuple-element.23), channel_id=1, source_target_pairs={{4,8},{5,9},{6,10},{7,11},{12,16},{13,17},{14,18},{15,19},{20,24},... | collective-permute-start | bytes 221192 | tf_op jit(solution)/shard_map/ppermute | solution.py:500
  29.8 5.4 %collective-permute-start.3 = (f32[2,9,8,128]{3,2,1,0:T(8,128)}, f32[2,9,8,128]{3,2,1,0:T(8,128)S(1)}, u32[]{:S(2)}, u32[]{:S(2)}) collective-permute-start(f32[2,9,8,128]{3,2,1,0:T(8,128)} %get-tuple-element.26), channel_id=1, source_target_pairs={{2,4},{3,5},{6,8},{7,9},{10,12},{11,13},{14,16},{15,17},{18,20},{1... | collective-permute-start | bytes 221192 | tf_op jit(solution)/shard_map/ppermute | solution.py:500
  35.2 2.3 %collective-permute-start.4 = (f32[2,9,8,128]{3,2,1,0:T(8,128)}, f32[2,9,8,128]{3,2,1,0:T(8,128)S(1)}, u32[]{:S(2)}, u32[]{:S(2)}) collective-permute-start(f32[2,9,8,128]{3,2,1,0:T(8,128)} %get-tuple-element.27), channel_id=1, source_target_pairs={{0,4},{1,5},{2,6},{3,7},{8,12},{9,13},{10,14},{11,15},{16,20},{17,... | collective-permute-start | bytes 221192 | tf_op jit(solution)/shard_map/ppermute | solution.py:500
  37.4 0.0 collective-permute-start.5
  37.4 2.5 %shard_map.94.held_ref = f32[9,24576]{1,0:T(8,128)} custom-call(f32[9,128,128]{2,1,0:T(8,128)} %get-tuple-element.24.kept_ref), custom_call_target="tpu_custom_call" | custom-call | flops 4194304 | bytes 4194304 | tf_op jit(solution)/shard_map/pallas_call | solution.py:633
  40.0 0.0 collective-permute-done.2.far2_ref
  40.0 0.0 collective-permute-done.3.next2_ref
  40.0 1.0 %collective-permute-start.8 = (f32[2,9,8,128]{3,2,1,0:T(8,128)S(1)}, f32[2,9,8,128]{3,2,1,0:T(8,128)S(1)}, u32[]{:S(2)}, u32[]{:S(2)}) collective-permute-start(f32[2,9,8,128]{3,2,1,0:T(8,128)S(1)} %collective-permute-done.3.next2_ref), channel_id=1, source_target_pairs={{0,1},{2,3},{4,5},{6,7},{8,9},{10,11},{12,13},{14,15},{16,17},{18,... | collective-permute-start | bytes 221192 | tf_op jit(solution)/shard_map/ppermute | solution.py:500
  41.0 0.0 collective-permute-done.4.far_ref
  41.0 0.0 collective-permute-start.9
  41.0 0.0 collective-permute-done.5.next_ref
  41.0 0.5 %collective-permute-start.10 = (f32[2,9,8,128]{3,2,1,0:T(8,128)S(1)}, f32[2,9,8,128]{3,2,1,0:T(8,128)S(1)}, u32[]{:S(2)}, u32[]{:S(2)}) collective-permute-start(f32[2,9,8,128]{3,2,1,0:T(8,128)S(1)} %collective-permute-done.5.next_ref), channel_id=1, source_target_pairs={{0,1},{2,3},{4,5},{6,7},{8,9},{10,11},{12,13},{14,15},{16,17},{18,... | collective-permute-start | bytes 221192 | tf_op jit(solution)/shard_map/ppermute | solution.py:500
  41.5 0.1 collective-permute-start.7
  41.6 0.0 copy-done
  41.6 0.4 collective-permute-start.6
  42.0 0.9 %collective-permute-done.6.other_ref = f32[9,8,128]{2,1,0:T(8,128)S(1)} collective-permute-done((f32[9,8,128]{2,1,0:T(8,128)S(1)}, f32[9,8,128]{2,1,0:T(8,128)S(1)}, u32[]{:S(2)}, u32[]{:S(2)}) %collective-permute-start.6) | collective-permute-done | bytes 36896 | tf_op jit(solution)/shard_map/ppermute | solution.py:500
  42.9 0.0 collective-permute-done.8.x_next2
  42.9 0.0 collective-permute-done.9.x_far
  42.9 0.0 collective-permute-done.10.x_next
  42.9 0.0 collective-permute-done.7.x_far2
  42.9 1.0 %shard_map.95 = f32[9,24576]{1,0:T(8,128)} custom-call(s32[1]{0:T(128)} %bitcast.own_ref, f32[2,9,8,128]{3,2,1,0:T(8,128)S(1)} %collective-permute-done.2.far2_ref, f32[2,9,8,128]{3,2,1,0:T(8,128)S(1)} %collective-permute-done.3.next2_ref, f32[2,9,8,128]{3,2,1,0:T(8,128)S(1)} %collective-permute-done.4.far_ref, ...), custom_call_target="tpu_custom_call", output_to_operand_aliasing={{}: (10, {})} | custom-call | tf_op jit(solution)/shard_map/pallas_call | solution.py:650
Async XLA Ops:
  1.6 11.7 %collective-permute-start = (f32[96,128]{1,0:T(8,128)}, f32[96,128]{1,0:T(8,128)}, u32[]{:S(2)}, u32[]{:S(2)}) collective-permute-start(f32[96,128]{1,0:T(8,128)} %get-tuple-element.18), channel_id=1, source_target_pairs={{1,2},{3,4},{5,6},{7,8},{9,10},{11,12},{13,14},{15,16},{17,18},{19... | collective-permute-start | bytes 147464 | tf_op jit(solution)/shard_map/ppermute | solution.py:500
  4.7 8.6 %collective-permute-start.1 = (f32[96,128]{1,0:T(8,128)}, f32[96,128]{1,0:T(8,128)}, u32[]{:S(2)}, u32[]{:S(2)}) collective-permute-start(f32[96,128]{1,0:T(8,128)} %get-tuple-element.19), channel_id=1, source_target_pairs={{0,1},{2,3},{4,5},{6,7},{8,9},{10,11},{12,13},{14,15},{16,17},{18,... | collective-permute-start | bytes 147464 | tf_op jit(solution)/shard_map/ppermute | solution.py:500
  28.1 13.5 %copy-start = (f32[9,8,128]{2,1,0:T(8,128)S(1)}, f32[9,8,128]{2,1,0:T(8,128)}, u32[]{:S(2)}) copy-start(f32[9,8,128]{2,1,0:T(8,128)} %get-tuple-element.29) | copy-start | bytes 110596
  28.1 11.8 %collective-permute-start.2 = (f32[2,9,8,128]{3,2,1,0:T(8,128)}, f32[2,9,8,128]{3,2,1,0:T(8,128)S(1)}, u32[]{:S(2)}, u32[]{:S(2)}) collective-permute-start(f32[2,9,8,128]{3,2,1,0:T(8,128)} %get-tuple-element.23), channel_id=1, source_target_pairs={{4,8},{5,9},{6,10},{7,11},{12,16},{13,17},{14,18},{15,19},{20,24},... | collective-permute-start | bytes 221192 | tf_op jit(solution)/shard_map/ppermute | solution.py:500
  29.8 10.2 %collective-permute-start.3 = (f32[2,9,8,128]{3,2,1,0:T(8,128)}, f32[2,9,8,128]{3,2,1,0:T(8,128)S(1)}, u32[]{:S(2)}, u32[]{:S(2)}) collective-permute-start(f32[2,9,8,128]{3,2,1,0:T(8,128)} %get-tuple-element.26), channel_id=1, source_target_pairs={{2,4},{3,5},{6,8},{7,9},{10,12},{11,13},{14,16},{15,17},{18,20},{1... | collective-permute-start | bytes 221192 | tf_op jit(solution)/shard_map/ppermute | solution.py:500
  35.2 5.8 %collective-permute-start.4 = (f32[2,9,8,128]{3,2,1,0:T(8,128)}, f32[2,9,8,128]{3,2,1,0:T(8,128)S(1)}, u32[]{:S(2)}, u32[]{:S(2)}) collective-permute-start(f32[2,9,8,128]{3,2,1,0:T(8,128)} %get-tuple-element.27), channel_id=1, source_target_pairs={{0,4},{1,5},{2,6},{3,7},{8,12},{9,13},{10,14},{11,15},{16,20},{17,... | collective-permute-start | bytes 221192 | tf_op jit(solution)/shard_map/ppermute | solution.py:500
  37.4 3.5 %collective-permute-start.5 = (f32[2,9,8,128]{3,2,1,0:T(8,128)}, f32[2,9,8,128]{3,2,1,0:T(8,128)S(1)}, u32[]{:S(2)}, u32[]{:S(2)}) collective-permute-start(f32[2,9,8,128]{3,2,1,0:T(8,128)} %get-tuple-element.28), channel_id=1, source_target_pairs={{0,2},{1,3},{4,6},{5,7},{8,10},{9,11},{12,14},{13,15},{16,18},{17,... | collective-permute-start | bytes 221192 | tf_op jit(solution)/shard_map/ppermute | solution.py:500
  40.0 2.9 %collective-permute-start.8 = (f32[2,9,8,128]{3,2,1,0:T(8,128)S(1)}, f32[2,9,8,128]{3,2,1,0:T(8,128)S(1)}, u32[]{:S(2)}, u32[]{:S(2)}) collective-permute-start(f32[2,9,8,128]{3,2,1,0:T(8,128)S(1)} %collective-permute-done.3.next2_ref), channel_id=1, source_target_pairs={{0,1},{2,3},{4,5},{6,7},{8,9},{10,11},{12,13},{14,15},{16,17},{18,... | collective-permute-start | bytes 221192 | tf_op jit(solution)/shard_map/ppermute | solution.py:500
  41.0 1.9 %collective-permute-start.9 = (f32[2,9,8,128]{3,2,1,0:T(8,128)S(1)}, f32[2,9,8,128]{3,2,1,0:T(8,128)S(1)}, u32[]{:S(2)}, u32[]{:S(2)}) collective-permute-start(f32[2,9,8,128]{3,2,1,0:T(8,128)S(1)} %collective-permute-done.4.far_ref), channel_id=1, source_target_pairs={{0,1},{2,3},{4,5},{6,7},{8,9},{10,11},{12,13},{14,15},{16,17},{18,... | collective-permute-start | bytes 221192 | tf_op jit(solution)/shard_map/ppermute | solution.py:500
  41.0 1.9 %collective-permute-start.10 = (f32[2,9,8,128]{3,2,1,0:T(8,128)S(1)}, f32[2,9,8,128]{3,2,1,0:T(8,128)S(1)}, u32[]{:S(2)}, u32[]{:S(2)}) collective-permute-start(f32[2,9,8,128]{3,2,1,0:T(8,128)S(1)} %collective-permute-done.5.next_ref), channel_id=1, source_target_pairs={{0,1},{2,3},{4,5},{6,7},{8,9},{10,11},{12,13},{14,15},{16,17},{18,... | collective-permute-start | bytes 221192 | tf_op jit(solution)/shard_map/ppermute | solution.py:500
  41.5 1.4 %collective-permute-start.7 = (f32[2,9,8,128]{3,2,1,0:T(8,128)S(1)}, f32[2,9,8,128]{3,2,1,0:T(8,128)S(1)}, u32[]{:S(2)}, u32[]{:S(2)}) collective-permute-start(f32[2,9,8,128]{3,2,1,0:T(8,128)S(1)} %collective-permute-done.2.far2_ref), channel_id=1, source_target_pairs={{0,1},{2,3},{4,5},{6,7},{8,9},{10,11},{12,13},{14,15},{16,17},{18,... | collective-permute-start | bytes 221192 | tf_op jit(solution)/shard_map/ppermute | solution.py:500
  41.6 1.3 %collective-permute-start.6 = (f32[9,8,128]{2,1,0:T(8,128)S(1)}, f32[9,8,128]{2,1,0:T(8,128)S(1)}, u32[]{:S(2)}, u32[]{:S(2)}) collective-permute-start(f32[9,8,128]{2,1,0:T(8,128)S(1)} %copy-done), channel_id=1, source_target_pairs={{0,1},{2,3},{4,5},{6,7},{8,9},{10,11},{12,13},{14,15},{16,17},{18,... | collective-permute-start | bytes 110600 | tf_op jit(solution)/shard_map/ppermute | solution.py:500

commit v6 on v5

--- a/solution.py
+++ b/solution.py
@@ -41,8 +41,8 @@
 
 
 def edge_kernel(
-    own_ref, pos_ref, mass_ref, ent_ref, rho_ref, act_ref, nbr_ref, far_ref, near_ref,
-    pos_v, act_v, nbr_v, sem
+    own_ref, pos_ref, mass_ref, ent_ref, rho_ref, act_ref, nbr_ref, far_out, near_out,
+    far_ref, near_ref, pos_v, act_v, nbr_v, sem
 ):
     even = own_ref[0] % 2 == 0
     copies = []
@@ -66,18 +66,24 @@
             copy.start()
             copies.append(copy)
     nbr_copy.wait()
-    for copy in copies:
-        copy.wait()
     lists = nbr_v[...].astype(jnp.float32)
-    for side, ref in enumerate((far_ref, near_ref)):
+    outs = []
+    for side, (ref, out) in enumerate(((far_ref, far_out), (near_ref, near_out))):
+        ref[88:96, :] = jnp.zeros((8, LANES), jnp.float32)
+        ref[88 : 88 + NEIGHBOURS, 0:CELLS_DEV] = lists
+        for copy in copies[5 * side : 5 * side + 5]:
+            copy.wait()
         for c in range(3):
             for i in range(EDGE_ROWS):
                 ref[16 * c + i : 16 * c + i + 1, :] = (
                     pos_v[side, c : c + 1, i * LANES : (i + 1) * LANES] * 0.5
                 )
         ref[80:88, :] = (act_v[side] == 1).astype(jnp.float32)
-        ref[88:96, :] = jnp.zeros((8, LANES), jnp.float32)
-        ref[88 : 88 + NEIGHBOURS, 0:CELLS_DEV] = lists
+        copy = pltpu.make_async_copy(ref, out, sem.at[11 + side])
+        copy.start()
+        outs.append(copy)
+    for copy in outs:
+        copy.wait()
 
 
 def order_kernel(own_ref, dest_in, slot_in, hi_out, lo_out, bits_out, dest_ref, slot_ref, sem):
@@ -128,11 +134,11 @@
 def state_kernel(
     own_ref, pos_ref, vel_ref, mass_ref, ent_ref, rho_ref, act_ref, dest_ref,
     nbr_ref, far_in, near_in, hi_in, lo_in, bits_in,
-    kept_ref, to_far, to_far2, to_next, to_next2, to_other,
+    kept_out, to_far, to_far2, to_next, to_next2, to_other,
     pos_v, vel_v, act_v, dest_v, nbr_v,
     xs, ys, zs, ms, ps, es, rho_old, rank, dens, ax, ay, az,
     fields, bits, parts, hi_row, lo_row, a0, b0, packed, blocks,
-    far_ref, near_ref, sq, mp, factors, table_v, table, chunk_list, sem,
+    kept_ref, far_ref, near_ref, sq, mp, factors, table_v, table, chunk_list, sem,
 ):
     own = own_ref[0]
     even = own % 2 == 0
@@ -393,6 +399,9 @@
         parts[v] = first
         parts[FIELDS + v] = whole - first
 
+    kept_copy = pltpu.make_async_copy(kept_ref, kept_out, sem.at[14])
+    kept_copy.start()
+
     bf = jnp.bfloat16
     iota16 = lax.broadcasted_iota(jnp.int32, (16, LANES), 0).astype(jnp.float32).astype(bf)
     one16, zero16 = jnp.ones((16, LANES), bf), jnp.zeros((16, LANES), bf)
@@ -433,6 +442,7 @@
         ref[0] = blocks[group_of(2 * step)]
         ref[1] = blocks[group_of(2 * step + turn)]
     to_other[...] = blocks[group_of(turn)]
+    kept_copy.wait()
 
 
 def chip_steps(own):
@@ -526,12 +536,14 @@
         edge_kernel,
         out_shape=(jax.ShapeDtypeStruct((HALO_ROWS, LANES), f32),) * 2,
         in_specs=[sm] + [hbm] * 6,
-        out_specs=(vm, vm),
+        out_specs=(hbm, hbm),
         scratch_shapes=[
+            pltpu.VMEM((HALO_ROWS, LANES), f32),
+            pltpu.VMEM((HALO_ROWS, LANES), f32),
             pltpu.VMEM((2, 3, EDGE * CELL_PARTICLES), f32),
             pltpu.VMEM((2, 8, LANES), i32),
             pltpu.VMEM((NEIGHBOURS, CELLS_DEV), i32),
-            pltpu.SemaphoreType.DMA((11,)),
+            pltpu.SemaphoreType.DMA((13,)),
         ],
         compiler_params=pltpu.CompilerParams(vmem_limit_bytes=64 * 2**20),
     )(own, position, mass, ent, rho, act, lists)
@@ -575,7 +587,7 @@
             jax.ShapeDtypeStruct((FIELDS, 8, LANES), f32),
         ),
         in_specs=[sm] + [hbm] * 13,
-        out_specs=(vm,) * 6,
+        out_specs=(hbm,) + (vm,) * 5,
         scratch_shapes=[flat, flat, whole, whole]
         + [pltpu.VMEM((NEIGHBOURS, CELLS_DEV), i32)]
         + [ext] * 12
@@ -589,6 +601,7 @@
             pltpu.VMEM((256, PACK_ROWS * LANES), jnp.bfloat16),
             pltpu.VMEM((64 * FIELDS, 256), f32),
             pltpu.VMEM((GROUPS, FIELDS, 8, LANES), f32),
+            pltpu.VMEM((FIELDS, ROWS, LANES), f32),
             pltpu.VMEM((HALO_ROWS, LANES), f32),
             pltpu.VMEM((HALO_ROWS, LANES), f32),
             ext,

time: 44.1 us -> 43.9 us (level)
  no operation moved by 1% of the time
where the time goes in v6:
time: 43.9 us; the launch traced here: 43.6 us
  Pallas kernels  21.6 us (49%)
  starting transfers between devices  21 us (48%)
  waiting for transfers between devices  0.89 us (2%)
    ppermute x11, starting transfers between devices, swapped(): return lax.ppermute(block, 'cells', route)  21 us
    pallas_call x1, Pallas kernels, per_device(): pl.pallas_call(state_kernel, out_shape=(jax.ShapeDtypeStruct((FIELDS, ROW...  14.6 us
    pallas_call x1, Pallas kernels, per_device(): pl.pallas_call(stay_kernel, out_shape=jax.ShapeDtypeStruct((FIELDS, RECV_...  2.51 us
    pallas_call x1, Pallas kernels, per_device(): pl.pallas_call(order_kernel, out_shape=(jax.ShapeDtypeStruct(square, f32)...  1.94 us
    pallas_call x1, Pallas kernels, per_device(): pl.pallas_call(edge_kernel, out_shape=(jax.ShapeDtypeStruct((HALO_ROWS, L...  1.61 us
    pallas_call x1, Pallas kernels, per_device(): pl.pallas_call(assemble_kernel, out_shape=jax.ShapeDtypeStruct((FIELDS, R...  0.99 us
    ppermute x11, waiting for transfers between devices, swapped(): return lax.ppermute(block, 'cells', route)  0.89 us
  transfers between devices with their start and end apart: 11, of which 1 were waited for; matrix products, arithmetic and copies ran while one was open for 0% of the time, Pallas kernels for 10%

profile of v6, /device:TPU:1, one launch (start us, length us, event | category | flops | bytes accessed | tf_op | source)
XLA Modules:
  0.0 43.6 jit_solution(11056279733623487812)
XLA Ops:
  0.0 1.6 %shard_map.91 = (f32[96,128]{1,0:T(8,128)}, f32[96,128]{1,0:T(8,128)}) custom-call(s32[1]{0:T(128)} %bitcast.own_ref, f32[3,16384]{1,0:T(4,128)} %pos_ref.3, f32[128,128]{1,0:T(8,128)} %bitcast.8, f32[128,128]{1,0:T(8,128)} %bitcast.10, f32[128,128]{1,0:T(8,128)} %bitcast.12, s32[128,128]{1,0:T(8,128)} %bitcast.14, s32[6,64]{1,0:T(8,128)} %bitcast.19), custom_call_target="tpu_custom_call" | custom-call | tf_op jit(solution)/shard_map/pallas_call | solution.py:535
  1.6 3.1 %collective-permute-start = (f32[96,128]{1,0:T(8,128)}, f32[96,128]{1,0:T(8,128)}, u32[]{:S(2)}, u32[]{:S(2)}) collective-permute-start(f32[96,128]{1,0:T(8,128)} %get-tuple-element.18), channel_id=1, source_target_pairs={{1,2},{3,4},{5,6},{7,8},{9,10},{11,12},{13,14},{15,16},{17,18},{19... | collective-permute-start | bytes 147464 | tf_op jit(solution)/shard_map/ppermute | solution.py:510
  4.7 6.6 %collective-permute-start.1 = (f32[96,128]{1,0:T(8,128)}, f32[96,128]{1,0:T(8,128)}, u32[]{:S(2)}, u32[]{:S(2)}) collective-permute-start(f32[96,128]{1,0:T(8,128)} %get-tuple-element.19), channel_id=1, source_target_pairs={{0,1},{2,3},{4,5},{6,7},{8,9},{10,11},{12,13},{14,15},{16,17},{18,... | collective-permute-start | bytes 147464 | tf_op jit(solution)/shard_map/ppermute | solution.py:510
  11.3 1.9 %shard_map.92 = (f32[128,128]{1,0:T(8,128)}, f32[128,128]{1,0:T(8,128)}, s32[128,128]{1,0:T(8,128)}) custom-call(s32[1]{0:T(128)} %bitcast.own_ref, s32[128,128]{1,0:T(8,128)} %bitcast.16, s32[128,128]{1,0:T(8,128)} %bitcast.18), custom_call_target="tpu_custom_call" | custom-call | flops 16777216 | bytes 8388608 | tf_op jit(solution)/shard_map/pallas_call | solution.py:556
  13.3 0.0 collective-permute-done.far_in
  13.3 0.0 collective-permute-done.1.near_in
  13.3 14.6 %shard_map.93 = (f32[9,128,128]{2,1,0:T(8,128)}, f32[2,9,8,128]{3,2,1,0:T(8,128)}, f32[2,9,8,128]{3,2,1,0:T(8,128)}, f32[2,9,8,128]{3,2,1,0:T(8,128)}, f32[2,9,8,128]{3,2,1,0:T(8,128)}, /*index=5*/f32[9,8,128]{2,1,0:T(8,128)}) custom-call(s32[1]{0:T(128)} %bitcast.own_ref, f32[3,16384]{1,0:T(4,128)} %pos_ref.3, f32[3,16384]{1,0:T(4,128)} %vel_ref.1, ...), custom_call_target="tpu_custom_call" | custom-call | tf_op jit(solution)/shard_map/pallas_call | solution.py:579
  27.9 0.0 copy-start
  27.9 1.7 %collective-permute-start.2 = (f32[2,9,8,128]{3,2,1,0:T(8,128)}, f32[2,9,8,128]{3,2,1,0:T(8,128)S(1)}, u32[]{:S(2)}, u32[]{:S(2)}) collective-permute-start(f32[2,9,8,128]{3,2,1,0:T(8,128)} %get-tuple-element.23), channel_id=1, source_target_pairs={{4,8},{5,9},{6,10},{7,11},{12,16},{13,17},{14,18},{15,19},{20,24},... | collective-permute-start | bytes 221192 | tf_op jit(solution)/shard_map/ppermute | solution.py:510
  29.6 5.4 %collective-permute-start.3 = (f32[2,9,8,128]{3,2,1,0:T(8,128)}, f32[2,9,8,128]{3,2,1,0:T(8,128)S(1)}, u32[]{:S(2)}, u32[]{:S(2)}) collective-permute-start(f32[2,9,8,128]{3,2,1,0:T(8,128)} %get-tuple-element.26), channel_id=1, source_target_pairs={{2,4},{3,5},{6,8},{7,9},{10,12},{11,13},{14,16},{15,17},{18,20},{1... | collective-permute-start | bytes 221192 | tf_op jit(solution)/shard_map/ppermute | solution.py:510
  35.0 2.3 %collective-permute-start.4 = (f32[2,9,8,128]{3,2,1,0:T(8,128)}, f32[2,9,8,128]{3,2,1,0:T(8,128)S(1)}, u32[]{:S(2)}, u32[]{:S(2)}) collective-permute-start(f32[2,9,8,128]{3,2,1,0:T(8,128)} %get-tuple-element.27), channel_id=1, source_target_pairs={{0,4},{1,5},{2,6},{3,7},{8,12},{9,13},{10,14},{11,15},{16,20},{17,... | collective-permute-start | bytes 221192 | tf_op jit(solution)/shard_map/ppermute | solution.py:510
  37.2 0.0 collective-permute-start.5
  37.2 2.5 %shard_map.94.held_ref = f32[9,24576]{1,0:T(8,128)} custom-call(f32[9,128,128]{2,1,0:T(8,128)} %get-tuple-element.24.kept_ref), custom_call_target="tpu_custom_call" | custom-call | flops 4194304 | bytes 4194304 | tf_op jit(solution)/shard_map/pallas_call | solution.py:646
  39.8 0.0 collective-permute-done.2.far2_ref
  39.8 0.0 collective-permute-done.3.next2_ref
  39.8 0.9 %collective-permute-start.8 = (f32[2,9,8,128]{3,2,1,0:T(8,128)S(1)}, f32[2,9,8,128]{3,2,1,0:T(8,128)S(1)}, u32[]{:S(2)}, u32[]{:S(2)}) collective-permute-start(f32[2,9,8,128]{3,2,1,0:T(8,128)S(1)} %collective-permute-done.3.next2_ref), channel_id=1, source_target_pairs={{0,1},{2,3},{4,5},{6,7},{8,9},{10,11},{12,13},{14,15},{16,17},{18,... | collective-permute-start | bytes 221192 | tf_op jit(solution)/shard_map/ppermute | solution.py:510
  40.7 0.0 collective-permute-done.4.far_ref
  40.7 0.0 collective-permute-start.9
  40.7 0.0 collective-permute-done.5.next_ref
  40.7 0.5 %collective-permute-start.10 = (f32[2,9,8,128]{3,2,1,0:T(8,128)S(1)}, f32[2,9,8,128]{3,2,1,0:T(8,128)S(1)}, u32[]{:S(2)}, u32[]{:S(2)}) collective-permute-start(f32[2,9,8,128]{3,2,1,0:T(8,128)S(1)} %collective-permute-done.5.next_ref), channel_id=1, source_target_pairs={{0,1},{2,3},{4,5},{6,7},{8,9},{10,11},{12,13},{14,15},{16,17},{18,... | collective-permute-start | bytes 221192 | tf_op jit(solution)/shard_map/ppermute | solution.py:510
  41.3 0.1 collective-permute-start.7
  41.3 0.0 copy-done
  41.3 0.4 collective-permute-start.6
  41.8 0.9 %collective-permute-done.6.other_ref = f32[9,8,128]{2,1,0:T(8,128)S(1)} collective-permute-done((f32[9,8,128]{2,1,0:T(8,128)S(1)}, f32[9,8,128]{2,1,0:T(8,128)S(1)}, u32[]{:S(2)}, u32[]{:S(2)}) %collective-permute-start.6) | collective-permute-done | bytes 36896 | tf_op jit(solution)/shard_map/ppermute | solution.py:510
  42.6 0.0 collective-permute-done.8.x_next2
  42.6 0.0 collective-permute-done.9.x_far
  42.6 0.0 collective-permute-done.10.x_next
  42.6 0.0 collective-permute-done.7.x_far2
  42.7 1.0 %shard_map.95 = f32[9,24576]{1,0:T(8,128)} custom-call(s32[1]{0:T(128)} %bitcast.own_ref, f32[2,9,8,128]{3,2,1,0:T(8,128)S(1)} %collective-permute-done.2.far2_ref, f32[2,9,8,128]{3,2,1,0:T(8,128)S(1)} %collective-permute-done.3.next2_ref, f32[2,9,8,128]{3,2,1,0:T(8,128)S(1)} %collective-permute-done.4.far_ref, ...), custom_call_target="tpu_custom_call", output_to_operand_aliasing={{}: (10, {})} | custom-call | tf_op jit(solution)/shard_map/pallas_call | solution.py:663
Async XLA Ops:
  1.6 11.7 %collective-permute-start = (f32[96,128]{1,0:T(8,128)}, f32[96,128]{1,0:T(8,128)}, u32[]{:S(2)}, u32[]{:S(2)}) collective-permute-start(f32[96,128]{1,0:T(8,128)} %get-tuple-element.18), channel_id=1, source_target_pairs={{1,2},{3,4},{5,6},{7,8},{9,10},{11,12},{13,14},{15,16},{17,18},{19... | collective-permute-start | bytes 147464 | tf_op jit(solution)/shard_map/ppermute | solution.py:510
  4.7 8.6 %collective-permute-start.1 = (f32[96,128]{1,0:T(8,128)}, f32[96,128]{1,0:T(8,128)}, u32[]{:S(2)}, u32[]{:S(2)}) collective-permute-start(f32[96,128]{1,0:T(8,128)} %get-tuple-element.19), channel_id=1, source_target_pairs={{0,1},{2,3},{4,5},{6,7},{8,9},{10,11},{12,13},{14,15},{16,17},{18,... | collective-permute-start | bytes 147464 | tf_op jit(solution)/shard_map/ppermute | solution.py:510
  27.9 13.4 %copy-start = (f32[9,8,128]{2,1,0:T(8,128)S(1)}, f32[9,8,128]{2,1,0:T(8,128)}, u32[]{:S(2)}) copy-start(f32[9,8,128]{2,1,0:T(8,128)} %get-tuple-element.29) | copy-start | bytes 110596
  27.9 11.9 %collective-permute-start.2 = (f32[2,9,8,128]{3,2,1,0:T(8,128)}, f32[2,9,8,128]{3,2,1,0:T(8,128)S(1)}, u32[]{:S(2)}, u32[]{:S(2)}) collective-permute-start(f32[2,9,8,128]{3,2,1,0:T(8,128)} %get-tuple-element.23), channel_id=1, source_target_pairs={{4,8},{5,9},{6,10},{7,11},{12,16},{13,17},{14,18},{15,19},{20,24},... | collective-permute-start | bytes 221192 | tf_op jit(solution)/shard_map/ppermute | solution.py:510
  29.6 10.2 %collective-permute-start.3 = (f32[2,9,8,128]{3,2,1,0:T(8,128)}, f32[2,9,8,128]{3,2,1,0:T(8,128)S(1)}, u32[]{:S(2)}, u32[]{:S(2)}) collective-permute-start(f32[2,9,8,128]{3,2,1,0:T(8,128)} %get-tuple-element.26), channel_id=1, source_target_pairs={{2,4},{3,5},{6,8},{7,9},{10,12},{11,13},{14,16},{15,17},{18,20},{1... | collective-permute-start | bytes 221192 | tf_op jit(solution)/shard_map/ppermute | solution.py:510
  35.0 5.8 %collective-permute-start.4 = (f32[2,9,8,128]{3,2,1,0:T(8,128)}, f32[2,9,8,128]{3,2,1,0:T(8,128)S(1)}, u32[]{:S(2)}, u32[]{:S(2)}) collective-permute-start(f32[2,9,8,128]{3,2,1,0:T(8,128)} %get-tuple-element.27), channel_id=1, source_target_pairs={{0,4},{1,5},{2,6},{3,7},{8,12},{9,13},{10,14},{11,15},{16,20},{17,... | collective-permute-start | bytes 221192 | tf_op jit(solution)/shard_map/ppermute | solution.py:510
  37.2 3.5 %collective-permute-start.5 = (f32[2,9,8,128]{3,2,1,0:T(8,128)}, f32[2,9,8,128]{3,2,1,0:T(8,128)S(1)}, u32[]{:S(2)}, u32[]{:S(2)}) collective-permute-start(f32[2,9,8,128]{3,2,1,0:T(8,128)} %get-tuple-element.28), channel_id=1, source_target_pairs={{0,2},{1,3},{4,6},{5,7},{8,10},{9,11},{12,14},{13,15},{16,18},{17,... | collective-permute-start | bytes 221192 | tf_op jit(solution)/shard_map/ppermute | solution.py:510
  39.8 2.9 %collective-permute-start.8 = (f32[2,9,8,128]{3,2,1,0:T(8,128)S(1)}, f32[2,9,8,128]{3,2,1,0:T(8,128)S(1)}, u32[]{:S(2)}, u32[]{:S(2)}) collective-permute-start(f32[2,9,8,128]{3,2,1,0:T(8,128)S(1)} %collective-permute-done.3.next2_ref), channel_id=1, source_target_pairs={{0,1},{2,3},{4,5},{6,7},{8,9},{10,11},{12,13},{14,15},{16,17},{18,... | collective-permute-start | bytes 221192 | tf_op jit(solution)/shard_map/ppermute | solution.py:510
  40.7 1.9 %collective-permute-start.9 = (f32[2,9,8,128]{3,2,1,0:T(8,128)S(1)}, f32[2,9,8,128]{3,2,1,0:T(8,128)S(1)}, u32[]{:S(2)}, u32[]{:S(2)}) collective-permute-start(f32[2,9,8,128]{3,2,1,0:T(8,128)S(1)} %collective-permute-done.4.far_ref), channel_id=1, source_target_pairs={{0,1},{2,3},{4,5},{6,7},{8,9},{10,11},{12,13},{14,15},{16,17},{18,... | collective-permute-start | bytes 221192 | tf_op jit(solution)/shard_map/ppermute | solution.py:510
  40.7 1.9 %collective-permute-start.10 = (f32[2,9,8,128]{3,2,1,0:T(8,128)S(1)}, f32[2,9,8,128]{3,2,1,0:T(8,128)S(1)}, u32[]{:S(2)}, u32[]{:S(2)}) collective-permute-start(f32[2,9,8,128]{3,2,1,0:T(8,128)S(1)} %collective-permute-done.5.next_ref), channel_id=1, source_target_pairs={{0,1},{2,3},{4,5},{6,7},{8,9},{10,11},{12,13},{14,15},{16,17},{18,... | collective-permute-start | bytes 221192 | tf_op jit(solution)/shard_map/ppermute | solution.py:510
  41.3 1.4 %collective-permute-start.7 = (f32[2,9,8,128]{3,2,1,0:T(8,128)S(1)}, f32[2,9,8,128]{3,2,1,0:T(8,128)S(1)}, u32[]{:S(2)}, u32[]{:S(2)}) collective-permute-start(f32[2,9,8,128]{3,2,1,0:T(8,128)S(1)} %collective-permute-done.2.far2_ref), channel_id=1, source_target_pairs={{0,1},{2,3},{4,5},{6,7},{8,9},{10,11},{12,13},{14,15},{16,17},{18,... | collective-permute-start | bytes 221192 | tf_op jit(solution)/shard_map/ppermute | solution.py:510
  41.3 1.3 %collective-permute-start.6 = (f32[9,8,128]{2,1,0:T(8,128)S(1)}, f32[9,8,128]{2,1,0:T(8,128)S(1)}, u32[]{:S(2)}, u32[]{:S(2)}) collective-permute-start(f32[9,8,128]{2,1,0:T(8,128)S(1)} %copy-done), channel_id=1, source_target_pairs={{0,1},{2,3},{4,5},{6,7},{8,9},{10,11},{12,13},{14,15},{16,17},{18,... | collective-permute-start | bytes 110600 | tf_op jit(solution)/shard_map/ppermute | solution.py:510

commit v7 on v6

--- a/solution.py
+++ b/solution.py
@@ -20,6 +20,7 @@
 EDGE = 2 * HALO
 EXT = CELLS_DEV + 2 * EDGE
 EXT_ROWS = 2 * EXT
+SPARE = 8
 EDGE_ROWS = 2 * EDGE
 HALO_ROWS = 96
 GHOST = HALO
@@ -149,8 +150,8 @@
         (far_in, far_ref),
         (near_in, near_ref),
         (dest_ref, dest_v),
-        (hi_in, hi_row),
-        (lo_in, lo_row),
+        (hi_in, hi_row.at[pl.ds(0, ROWS)]),
+        (lo_in, lo_row.at[pl.ds(0, ROWS)]),
         (bits_in, bits),
         (rho_ref, rho_old.at[pl.ds(EDGE_ROWS, ROWS)]),
         (mass_ref, ms.at[pl.ds(EDGE_ROWS, ROWS)]),
@@ -205,12 +206,12 @@
         ref[0:EDGE_ROWS, :], ref[high, :] = side_rows(16 * k, 16 * k + 16)
     for ref, rows, fill in ((es, (64, 72), 0.0), (rho_old, (72, 80), 1.0)):
         ref[0:8, :] = zeros8 + fill
-        ref[EXT_ROWS - 8 :, :] = zeros8 + fill
+        ref[EXT_ROWS - 8 : EXT_ROWS, :] = zeros8 + fill
         ref[8:16, :], ref[EXT_ROWS - 16 : EXT_ROWS - 8, :] = side_rows(*rows)
     inside = jnp.dot(act16, before, preferred_element_type=jnp.float32)
     total = jnp.dot(act16, ones, preferred_element_type=jnp.float32)
     row_id = lax.broadcasted_iota(jnp.int32, (EXT_ROWS, LANES), 0)
-    rank[...] = jnp.where(
+    rank[0:EXT_ROWS, :] = jnp.where(
         act > 0.5, inside + jnp.where(row_id % 2 == 1, pltpu.roll(total, 1, 0), 0.0), -1.0
     )
 
@@ -293,7 +294,7 @@
             row = jnp.sum(jnp.where(picks[h], value, 0.0), axis=0, keepdims=True)
             ref[pl.ds(2 * cell + h, 1), :] += row
 
-    sq[...] = -(xs[...] * xs[...] + ys[...] * ys[...] + zs[...] * zs[...])
+    sq[0:EXT_ROWS, :] = -sum(r[0:EXT_ROWS, :] * r[0:EXT_ROWS, :] for r in (xs, ys, zs))
 
     def target(cell, picks):
         cx, cy, cz = (column(ref, cell, picks) for ref in (xs, ys, zs))
@@ -340,11 +341,12 @@
 
     loop(all_total, density_step)
 
-    rho = jnp.where(rank[...] >= 0.0, dens[...], rho_old[...])
-    dens[...] = rho
-    ps[...] = es[...] * jnp.exp(jnp.log(rho) * (-1.0 / 3.0))
-
-    mp[...] = ms[...] * ps[...]
+    used = slice(0, EXT_ROWS)
+    rho = jnp.where(rank[used, :] >= 0.0, dens[used, :], rho_old[used, :])
+    dens[used, :] = rho
+    ps[used, :] = es[used, :] * jnp.exp(jnp.log(rho) * (-1.0 / 3.0))
+
+    mp[used, :] = ms[used, :] * ps[used, :]
 
     def force_step(step, keep):
         done = []
@@ -377,7 +379,7 @@
     loop(own_total, force_step)
 
     own_row = lax.broadcasted_iota(jnp.int32, (ROWS, LANES), 0)
-    mover_rows = jnp.max(jnp.where(hi_row[...] >= 0.0, own_row + 1, 0))
+    mover_rows = jnp.max(jnp.where(hi_row[0:ROWS, :] >= 0.0, own_row + 1, 0))
 
     def moved_up(x):
         for bit in range(7):
@@ -396,8 +398,8 @@
         kept_ref[v] = jnp.where(stays, whole, 0.0)
         whole = moved_up(whole)
         first = whole.astype(jnp.bfloat16).astype(jnp.float32)
-        parts[v] = first
-        parts[FIELDS + v] = whole - first
+        parts[v, 0:ROWS, :] = first
+        parts[FIELDS + v, 0:ROWS, :] = whole - first
 
     kept_copy = pltpu.make_async_copy(kept_ref, kept_out, sem.at[14])
     kept_copy.start()
@@ -572,7 +574,7 @@
             flops=2**24, bytes_accessed=2**23, transcendentals=0
         ),
     )(own, dest, slot)
-    ext = pltpu.VMEM((EXT_ROWS, LANES), f32)
+    ext = pltpu.VMEM((EXT_ROWS + SPARE, LANES), f32)
     flat = pltpu.VMEM((3, PART_DEV), f32)
     whole = pltpu.VMEM(square, i32)
     pair = jax.ShapeDtypeStruct((2, FIELDS, 8, LANES), f32)
@@ -594,9 +596,9 @@
         + [
             pltpu.VMEM((FIELDS, ROWS, LANES), f32),
             whole,
-            pltpu.VMEM((2 * FIELDS, ROWS, LANES), f32),
-            pltpu.VMEM(square, f32),
-            pltpu.VMEM(square, f32),
+            pltpu.VMEM((2 * FIELDS, ROWS + SPARE, LANES), f32),
+            pltpu.VMEM((ROWS + SPARE, LANES), f32),
+            pltpu.VMEM((ROWS + SPARE, LANES), f32),
             pltpu.VMEM((64 * FIELDS, PACK_ROWS * LANES), jnp.bfloat16),
             pltpu.VMEM((256, PACK_ROWS * LANES), jnp.bfloat16),
             pltpu.VMEM((64 * FIELDS, 256), f32),

time: 43.9 us -> 44.2 us (level)
  no operation moved by 1% of the time
where the time goes in v7:
time: 44.2 us; the launch traced here: 43.7 us
  Pallas kernels  21.6 us (49%)
  starting transfers between devices  21 us (48%)
  waiting for transfers between devices  0.89 us (2%)
    ppermute x11, starting transfers between devices, swapped(): return lax.ppermute(block, 'cells', route)  21 us
    pallas_call x1, Pallas kernels, per_device(): pl.pallas_call(state_kernel, out_shape=(jax.ShapeDtypeStruct((FIELDS, ROW...  14.6 us
    pallas_call x1, Pallas kernels, per_device(): pl.pallas_call(stay_kernel, out_shape=jax.ShapeDtypeStruct((FIELDS, RECV_...  2.51 us
    pallas_call x1, Pallas kernels, per_device(): pl.pallas_call(order_kernel, out_shape=(jax.ShapeDtypeStruct(square, f32)...  1.94 us
    pallas_call x1, Pallas kernels, per_device(): pl.pallas_call(edge_kernel, out_shape=(jax.ShapeDtypeStruct((HALO_ROWS, L...  1.61 us
    pallas_call x1, Pallas kernels, per_device(): pl.pallas_call(assemble_kernel, out_shape=jax.ShapeDtypeStruct((FIELDS, R...  0.99 us
    ppermute x11, waiting for transfers between devices, swapped(): return lax.ppermute(block, 'cells', route)  0.89 us
  transfers between devices with their start and end apart: 11, of which 1 were waited for; matrix products, arithmetic and copies ran while one was open for 0% of the time, Pallas kernels for 10%

profile of v7, /device:TPU:1, one launch (start us, length us, event | category | flops | bytes accessed | tf_op | source)
XLA Modules:
  0.0 43.7 jit_solution(2467296328659248379)
XLA Ops:
  0.0 1.6 %shard_map.91 = (f32[96,128]{1,0:T(8,128)}, f32[96,128]{1,0:T(8,128)}) custom-call(s32[1]{0:T(128)} %bitcast.own_ref, f32[3,16384]{1,0:T(4,128)} %pos_ref.3, f32[128,128]{1,0:T(8,128)} %bitcast.8, f32[128,128]{1,0:T(8,128)} %bitcast.10, f32[128,128]{1,0:T(8,128)} %bitcast.12, s32[128,128]{1,0:T(8,128)} %bitcast.14, s32[6,64]{1,0:T(8,128)} %bitcast.19), custom_call_target="tpu_custom_call" | custom-call | tf_op jit(solution)/shard_map/pallas_call | solution.py:537
  1.6 3.1 %collective-permute-start = (f32[96,128]{1,0:T(8,128)}, f32[96,128]{1,0:T(8,128)}, u32[]{:S(2)}, u32[]{:S(2)}) collective-permute-start(f32[96,128]{1,0:T(8,128)} %get-tuple-element.18), channel_id=1, source_target_pairs={{1,2},{3,4},{5,6},{7,8},{9,10},{11,12},{13,14},{15,16},{17,18},{19... | collective-permute-start | bytes 147464 | tf_op jit(solution)/shard_map/ppermute | solution.py:512
  4.7 6.6 %collective-permute-start.1 = (f32[96,128]{1,0:T(8,128)}, f32[96,128]{1,0:T(8,128)}, u32[]{:S(2)}, u32[]{:S(2)}) collective-permute-start(f32[96,128]{1,0:T(8,128)} %get-tuple-element.19), channel_id=1, source_target_pairs={{0,1},{2,3},{4,5},{6,7},{8,9},{10,11},{12,13},{14,15},{16,17},{18,... | collective-permute-start | bytes 147464 | tf_op jit(solution)/shard_map/ppermute | solution.py:512
  11.3 1.9 %shard_map.92 = (f32[128,128]{1,0:T(8,128)}, f32[128,128]{1,0:T(8,128)}, s32[128,128]{1,0:T(8,128)}) custom-call(s32[1]{0:T(128)} %bitcast.own_ref, s32[128,128]{1,0:T(8,128)} %bitcast.16, s32[128,128]{1,0:T(8,128)} %bitcast.18), custom_call_target="tpu_custom_call" | custom-call | flops 16777216 | bytes 8388608 | tf_op jit(solution)/shard_map/pallas_call | solution.py:558
  13.3 0.0 collective-permute-done.far_in
  13.3 0.0 collective-permute-done.1.near_in
  13.3 14.6 %shard_map.93 = (f32[9,128,128]{2,1,0:T(8,128)}, f32[2,9,8,128]{3,2,1,0:T(8,128)}, f32[2,9,8,128]{3,2,1,0:T(8,128)}, f32[2,9,8,128]{3,2,1,0:T(8,128)}, f32[2,9,8,128]{3,2,1,0:T(8,128)}, /*index=5*/f32[9,8,128]{2,1,0:T(8,128)}) custom-call(s32[1]{0:T(128)} %bitcast.own_ref, f32[3,16384]{1,0:T(4,128)} %pos_ref.3, f32[3,16384]{1,0:T(4,128)} %vel_ref.1, ...), custom_call_target="tpu_custom_call" | custom-call | tf_op jit(solution)/shard_map/pallas_call | solution.py:581
  27.9 0.0 copy-start
  27.9 1.6 %collective-permute-start.2 = (f32[2,9,8,128]{3,2,1,0:T(8,128)}, f32[2,9,8,128]{3,2,1,0:T(8,128)S(1)}, u32[]{:S(2)}, u32[]{:S(2)}) collective-permute-start(f32[2,9,8,128]{3,2,1,0:T(8,128)} %get-tuple-element.23), channel_id=1, source_target_pairs={{4,8},{5,9},{6,10},{7,11},{12,16},{13,17},{14,18},{15,19},{20,24},... | collective-permute-start | bytes 221192 | tf_op jit(solution)/shard_map/ppermute | solution.py:512
  29.5 5.4 %collective-permute-start.3 = (f32[2,9,8,128]{3,2,1,0:T(8,128)}, f32[2,9,8,128]{3,2,1,0:T(8,128)S(1)}, u32[]{:S(2)}, u32[]{:S(2)}) collective-permute-start(f32[2,9,8,128]{3,2,1,0:T(8,128)} %get-tuple-element.26), channel_id=1, source_target_pairs={{2,4},{3,5},{6,8},{7,9},{10,12},{11,13},{14,16},{15,17},{18,20},{1... | collective-permute-start | bytes 221192 | tf_op jit(solution)/shard_map/ppermute | solution.py:512
  34.9 2.3 %collective-permute-start.4 = (f32[2,9,8,128]{3,2,1,0:T(8,128)}, f32[2,9,8,128]{3,2,1,0:T(8,128)S(1)}, u32[]{:S(2)}, u32[]{:S(2)}) collective-permute-start(f32[2,9,8,128]{3,2,1,0:T(8,128)} %get-tuple-element.27), channel_id=1, source_target_pairs={{0,4},{1,5},{2,6},{3,7},{8,12},{9,13},{10,14},{11,15},{16,20},{17,... | collective-permute-start | bytes 221192 | tf_op jit(solution)/shard_map/ppermute | solution.py:512
  37.2 0.0 collective-permute-start.5
  37.2 2.5 %shard_map.94.held_ref = f32[9,24576]{1,0:T(8,128)} custom-call(f32[9,128,128]{2,1,0:T(8,128)} %get-tuple-element.24.kept_ref), custom_call_target="tpu_custom_call" | custom-call | flops 4194304 | bytes 4194304 | tf_op jit(solution)/shard_map/pallas_call | solution.py:648
  39.7 0.0 collective-permute-done.2.far2_ref
  39.8 0.0 collective-permute-done.3.next2_ref
  39.8 1.0 %collective-permute-start.8 = (f32[2,9,8,128]{3,2,1,0:T(8,128)S(1)}, f32[2,9,8,128]{3,2,1,0:T(8,128)S(1)}, u32[]{:S(2)}, u32[]{:S(2)}) collective-permute-start(f32[2,9,8,128]{3,2,1,0:T(8,128)S(1)} %collective-permute-done.3.next2_ref), channel_id=1, source_target_pairs={{0,1},{2,3},{4,5},{6,7},{8,9},{10,11},{12,13},{14,15},{16,17},{18,... | collective-permute-start | bytes 221192 | tf_op jit(solution)/shard_map/ppermute | solution.py:512
  40.7 0.0 collective-permute-done.4.far_ref
  40.8 0.0 collective-permute-start.9
  40.8 0.0 collective-permute-done.5.next_ref
  40.8 0.5 %collective-permute-start.10 = (f32[2,9,8,128]{3,2,1,0:T(8,128)S(1)}, f32[2,9,8,128]{3,2,1,0:T(8,128)S(1)}, u32[]{:S(2)}, u32[]{:S(2)}) collective-permute-start(f32[2,9,8,128]{3,2,1,0:T(8,128)S(1)} %collective-permute-done.5.next_ref), channel_id=1, source_target_pairs={{0,1},{2,3},{4,5},{6,7},{8,9},{10,11},{12,13},{14,15},{16,17},{18,... | collective-permute-start | bytes 221192 | tf_op jit(solution)/shard_map/ppermute | solution.py:512
  41.3 0.1 collective-permute-start.7
  41.4 0.0 copy-done
  41.4 0.4 collective-permute-start.6
  41.8 0.9 %collective-permute-done.6.other_ref = f32[9,8,128]{2,1,0:T(8,128)S(1)} collective-permute-done((f32[9,8,128]{2,1,0:T(8,128)S(1)}, f32[9,8,128]{2,1,0:T(8,128)S(1)}, u32[]{:S(2)}, u32[]{:S(2)}) %collective-permute-start.6) | collective-permute-done | bytes 36896 | tf_op jit(solution)/shard_map/ppermute | solution.py:512
  42.6 0.0 collective-permute-done.8.x_next2
  42.6 0.0 collective-permute-done.9.x_far
  42.7 0.0 collective-permute-done.10.x_next
  42.7 0.0 collective-permute-done.7.x_far2
  42.7 1.0 %shard_map.95 = f32[9,24576]{1,0:T(8,128)} custom-call(s32[1]{0:T(128)} %bitcast.own_ref, f32[2,9,8,128]{3,2,1,0:T(8,128)S(1)} %collective-permute-done.2.far2_ref, f32[2,9,8,128]{3,2,1,0:T(8,128)S(1)} %collective-permute-done.3.next2_ref, f32[2,9,8,128]{3,2,1,0:T(8,128)S(1)} %collective-permute-done.4.far_ref, ...), custom_call_target="tpu_custom_call", output_to_operand_aliasing={{}: (10, {})} | custom-call | tf_op jit(solution)/shard_map/pallas_call | solution.py:665
Async XLA Ops:
  1.6 11.7 %collective-permute-start = (f32[96,128]{1,0:T(8,128)}, f32[96,128]{1,0:T(8,128)}, u32[]{:S(2)}, u32[]{:S(2)}) collective-permute-start(f32[96,128]{1,0:T(8,128)} %get-tuple-element.18), channel_id=1, source_target_pairs={{1,2},{3,4},{5,6},{7,8},{9,10},{11,12},{13,14},{15,16},{17,18},{19... | collective-permute-start | bytes 147464 | tf_op jit(solution)/shard_map/ppermute | solution.py:512
  4.7 8.6 %collective-permute-start.1 = (f32[96,128]{1,0:T(8,128)}, f32[96,128]{1,0:T(8,128)}, u32[]{:S(2)}, u32[]{:S(2)}) collective-permute-start(f32[96,128]{1,0:T(8,128)} %get-tuple-element.19), channel_id=1, source_target_pairs={{0,1},{2,3},{4,5},{6,7},{8,9},{10,11},{12,13},{14,15},{16,17},{18,... | collective-permute-start | bytes 147464 | tf_op jit(solution)/shard_map/ppermute | solution.py:512
  27.9 13.5 %copy-start = (f32[9,8,128]{2,1,0:T(8,128)S(1)}, f32[9,8,128]{2,1,0:T(8,128)}, u32[]{:S(2)}) copy-start(f32[9,8,128]{2,1,0:T(8,128)} %get-tuple-element.29) | copy-start | bytes 110596
  27.9 11.8 %collective-permute-start.2 = (f32[2,9,8,128]{3,2,1,0:T(8,128)}, f32[2,9,8,128]{3,2,1,0:T(8,128)S(1)}, u32[]{:S(2)}, u32[]{:S(2)}) collective-permute-start(f32[2,9,8,128]{3,2,1,0:T(8,128)} %get-tuple-element.23), channel_id=1, source_target_pairs={{4,8},{5,9},{6,10},{7,11},{12,16},{13,17},{14,18},{15,19},{20,24},... | collective-permute-start | bytes 221192 | tf_op jit(solution)/shard_map/ppermute | solution.py:512
  29.5 10.2 %collective-permute-start.3 = (f32[2,9,8,128]{3,2,1,0:T(8,128)}, f32[2,9,8,128]{3,2,1,0:T(8,128)S(1)}, u32[]{:S(2)}, u32[]{:S(2)}) collective-permute-start(f32[2,9,8,128]{3,2,1,0:T(8,128)} %get-tuple-element.26), channel_id=1, source_target_pairs={{2,4},{3,5},{6,8},{7,9},{10,12},{11,13},{14,16},{15,17},{18,20},{1... | collective-permute-start | bytes 221192 | tf_op jit(solution)/shard_map/ppermute | solution.py:512
  34.9 5.8 %collective-permute-start.4 = (f32[2,9,8,128]{3,2,1,0:T(8,128)}, f32[2,9,8,128]{3,2,1,0:T(8,128)S(1)}, u32[]{:S(2)}, u32[]{:S(2)}) collective-permute-start(f32[2,9,8,128]{3,2,1,0:T(8,128)} %get-tuple-element.27), channel_id=1, source_target_pairs={{0,4},{1,5},{2,6},{3,7},{8,12},{9,13},{10,14},{11,15},{16,20},{17,... | collective-permute-start | bytes 221192 | tf_op jit(solution)/shard_map/ppermute | solution.py:512
  37.2 3.5 %collective-permute-start.5 = (f32[2,9,8,128]{3,2,1,0:T(8,128)}, f32[2,9,8,128]{3,2,1,0:T(8,128)S(1)}, u32[]{:S(2)}, u32[]{:S(2)}) collective-permute-start(f32[2,9,8,128]{3,2,1,0:T(8,128)} %get-tuple-element.28), channel_id=1, source_target_pairs={{0,2},{1,3},{4,6},{5,7},{8,10},{9,11},{12,14},{13,15},{16,18},{17,... | collective-permute-start | bytes 221192 | tf_op jit(solution)/shard_map/ppermute | solution.py:512
  39.8 2.9 %collective-permute-start.8 = (f32[2,9,8,128]{3,2,1,0:T(8,128)S(1)}, f32[2,9,8,128]{3,2,1,0:T(8,128)S(1)}, u32[]{:S(2)}, u32[]{:S(2)}) collective-permute-start(f32[2,9,8,128]{3,2,1,0:T(8,128)S(1)} %collective-permute-done.3.next2_ref), channel_id=1, source_target_pairs={{0,1},{2,3},{4,5},{6,7},{8,9},{10,11},{12,13},{14,15},{16,17},{18,... | collective-permute-start | bytes 221192 | tf_op jit(solution)/shard_map/ppermute | solution.py:512
  40.8 1.9 %collective-permute-start.9 = (f32[2,9,8,128]{3,2,1,0:T(8,128)S(1)}, f32[2,9,8,128]{3,2,1,0:T(8,128)S(1)}, u32[]{:S(2)}, u32[]{:S(2)}) collective-permute-start(f32[2,9,8,128]{3,2,1,0:T(8,128)S(1)} %collective-permute-done.4.far_ref), channel_id=1, source_target_pairs={{0,1},{2,3},{4,5},{6,7},{8,9},{10,11},{12,13},{14,15},{16,17},{18,... | collective-permute-start | bytes 221192 | tf_op jit(solution)/shard_map/ppermute | solution.py:512
  40.8 1.9 %collective-permute-start.10 = (f32[2,9,8,128]{3,2,1,0:T(8,128)S(1)}, f32[2,9,8,128]{3,2,1,0:T(8,128)S(1)}, u32[]{:S(2)}, u32[]{:S(2)}) collective-permute-start(f32[2,9,8,128]{3,2,1,0:T(8,128)S(1)} %collective-permute-done.5.next_ref), channel_id=1, source_target_pairs={{0,1},{2,3},{4,5},{6,7},{8,9},{10,11},{12,13},{14,15},{16,17},{18,... | collective-permute-start | bytes 221192 | tf_op jit(solution)/shard_map/ppermute | solution.py:512
  41.3 1.4 %collective-permute-start.7 = (f32[2,9,8,128]{3,2,1,0:T(8,128)S(1)}, f32[2,9,8,128]{3,2,1,0:T(8,128)S(1)}, u32[]{:S(2)}, u32[]{:S(2)}) collective-permute-start(f32[2,9,8,128]{3,2,1,0:T(8,128)S(1)} %collective-permute-done.2.far2_ref), channel_id=1, source_target_pairs={{0,1},{2,3},{4,5},{6,7},{8,9},{10,11},{12,13},{14,15},{16,17},{18,... | collective-permute-start | bytes 221192 | tf_op jit(solution)/shard_map/ppermute | solution.py:512
  41.4 1.3 %collective-permute-start.6 = (f32[9,8,128]{2,1,0:T(8,128)S(1)}, f32[9,8,128]{2,1,0:T(8,128)S(1)}, u32[]{:S(2)}, u32[]{:S(2)}) collective-permute-start(f32[9,8,128]{2,1,0:T(8,128)S(1)} %copy-done), channel_id=1, source_target_pairs={{0,1},{2,3},{4,5},{6,7},{8,9},{10,11},{12,13},{14,15},{16,17},{18,... | collective-permute-start | bytes 110600 | tf_op jit(solution)/shard_map/ppermute | solution.py:512
